TPU v7x, 128 devices: a whole 4x4x4 slice. The times are simulated.
128 devices in a mesh: cp: 8 (over z_lo, y), dp: 16 (over z_hi, x, core).
Axes of the slice: x: 4, y: 4, z: 4 (z_hi: 2, z_lo: 2; z = z_hi * 2 + z_lo), core: 2. Of those that a mesh axis runs over, the one named last changes fastest.
Arguments:
- hidden_in: bfloat16 [16, 1024, 4096], P('dp', 'cp'), may hold values from -6 to 6
- out_grad: bfloat16 [16, 1024, 4096], P('dp', 'cp'), may hold values from -6 to 6
- queries: bfloat16 [16, 1024, 4096], P('dp', 'cp'), may hold values from -5 to 5
- keys: bfloat16 [16, 1024, 256], P('dp', 'cp'), may hold values from -5 to 5
- values: bfloat16 [16, 1024, 256], P('dp', 'cp'), may hold values from -6 to 6
- out_proj: bfloat16 [4096, 4096], P('cp', 'dp'), may hold values from -0.09375 to 0.09375
- expert_ids: int32 [16, 1024, 2], P('dp', 'cp'), may hold values from 0 to 63, all different within a row; in each aligned block of 128 rows (0 to 127, 128 to 255, ..., all dimensions but the last counted through in order) at most 5 rows name the same one
- gate_probs: float32 [16, 1024, 2], P('dp', 'cp'), may hold values from 0.2 to 1
- w_gate: bfloat16 [128, 4096, 768], P(('cp', 'dp')), may hold values from -0.09375 to 0.09375
- w_up: bfloat16 [128, 4096, 768], P(('cp', 'dp')), may hold values from -0.09375 to 0.09375
- w_down: bfloat16 [128, 768, 4096], P(('cp', 'dp')), may hold values from -0.15625 to 0.15625
Outputs:
- resid_grad: bfloat16 [16, 1024, 4096], P('dp', 'cp')
- query_grad: bfloat16 [16, 1024, 4096], P('dp', 'cp')
- key_grad: bfloat16 [16, 1024, 256], P('dp', 'cp')
- value_grad: bfloat16 [16, 1024, 256], P('dp', 'cp')
Inputs may be any that keep to these rules, and one draw needn't show every extreme that they name: `expert_ids`: each token names 2 different experts; among the 128 tokens of one device (aligned blocks of the sequence) no expert is named more than 5 times, a bound that some block reaches.
All inputs are finite; a program needn't handle non-finite values.
Results may differ from a plain program's by a relative error of at most 0.028.
Values may be sent and summed in bfloat16 or wider, within the bound.
No kernel may reach another device: no remote copies, remote signals or barrier semaphores. Data moves between devices by JAX's collectives and lax.ppermute only.
A program may use at most 192 MiB of HBM per device.

v0:
```python
import jax
import jax.numpy as jnp
from jax import lax
from jax.sharding import PartitionSpec as P

QUERY_HEADS = 32
KEY_VALUE_HEADS = 2
HEAD_SIZE = 128


def expert_back(rows_in, grads_in, gate_mat, up_mat, down_mat):
    pre_gate = jnp.dot(rows_in, gate_mat, preferred_element_type=jnp.float32)
    pre_up = jnp.dot(rows_in, up_mat, preferred_element_type=jnp.float32)
    upstream = lax.dot_general(
        grads_in, down_mat, (((1,), (1,)), ((), ())), preferred_element_type=jnp.float32
    )
    sigmoid_gate = jax.nn.sigmoid(pre_gate)
    d_gate = (upstream * pre_up * sigmoid_gate * (1.0 + pre_gate * (1.0 - sigmoid_gate))).astype(
        jnp.bfloat16
    )
    d_up = (upstream * pre_gate * sigmoid_gate).astype(jnp.bfloat16)
    back_gate = lax.dot_general(
        d_gate, gate_mat, (((1,), (1,)), ((), ())), preferred_element_type=jnp.float32
    )
    back_up = lax.dot_general(
        d_up, up_mat, (((1,), (1,)), ((), ())), preferred_element_type=jnp.float32
    )
    return back_gate + back_up


def body(
    hidden_in,
    out_grad,
    queries,
    keys,
    values,
    out_proj,
    expert_ids,
    gate_probs,
    w_gate,
    w_up,
    w_down,
):
    cp_count = lax.axis_size("cp")
    dp_count = lax.axis_size("dp")
    all_devices = cp_count * dp_count
    experts = all_devices // 2
    local_tokens = hidden_in.shape[1]
    width = hidden_in.shape[2]
    top_count = expert_ids.shape[2]
    capacity = max(2, local_tokens * top_count * 5 // (4 * experts))
    flat_ids = expert_ids.reshape(local_tokens * top_count)
    expert_hot = (flat_ids[:, None] == jnp.arange(experts, dtype=jnp.int32)[None, :]).astype(
        jnp.int32
    )
    earlier = jnp.cumsum(expert_hot, axis=0) - expert_hot
    slot_index = flat_ids * capacity + jnp.sum(earlier * expert_hot, axis=1)
    placing = (
        jnp.arange(experts * capacity, dtype=jnp.int32)[:, None] == slot_index[None, :]
    ).astype(jnp.bfloat16)
    picking = jnp.sum(placing.reshape(experts * capacity, local_tokens, top_count), axis=2)
    rows_here = hidden_in[0]
    grads_here = out_grad[0]
    doubled = (experts, 2, capacity, width)
    send_rows = jnp.dot(picking, rows_here, preferred_element_type=jnp.float32).astype(jnp.bfloat16)
    send_grads = jnp.dot(picking, grads_here, preferred_element_type=jnp.float32).astype(
        jnp.bfloat16
    )
    send_rows = jnp.broadcast_to(send_rows.reshape(experts, 1, capacity, width), doubled).reshape(
        all_devices, capacity, width
    )
    send_grads = jnp.broadcast_to(send_grads.reshape(experts, 1, capacity, width), doubled).reshape(
        all_devices, capacity, width
    )
    rows_in = lax.all_to_all(send_rows, ("cp", "dp"), split_axis=0, concat_axis=0, tiled=True)
    grads_in = lax.all_to_all(send_grads, ("cp", "dp"), split_axis=0, concat_axis=0, tiled=True)
    item_count = rows_in.shape[1]
    back = expert_back(
        rows_in.reshape(-1, width), grads_in.reshape(-1, width), w_gate[0], w_up[0], w_down[0]
    )
    back = back.reshape(all_devices, item_count, width)
    result = lax.all_to_all(
        back.astype(jnp.bfloat16), ("cp", "dp"), split_axis=0, concat_axis=0, tiled=True
    ).astype(back.dtype)
    summed = jnp.sum(result.reshape(experts, 2, capacity, width), axis=1).reshape(
        experts * capacity, width
    )
    per_route = summed[slot_index].reshape(local_tokens, top_count, width)
    moe_grad = jnp.sum(per_route * gate_probs[0][:, :, None], axis=1)
    resid = (grads_here.astype(jnp.float32) + moe_grad).astype(jnp.bfloat16)
    sequence_length = local_tokens * cp_count
    head_width = out_proj.shape[0]
    local_heads = head_width // HEAD_SIZE
    full_resid = lax.all_gather(resid, "cp", axis=0, tiled=True)
    ctx_grad = lax.dot_general(
        full_resid,
        lax.all_gather(out_proj, "dp", axis=1, tiled=True),
        (((1,), (1,)), ((), ())),
        preferred_element_type=jnp.float32,
    ).astype(jnp.bfloat16)
    ctx_heads = ctx_grad.reshape(sequence_length, local_heads, HEAD_SIZE)
    query_here = queries[0].reshape(1, local_tokens, cp_count, head_width)
    query_heads = lax.all_to_all(query_here, "cp", split_axis=2, concat_axis=0, tiled=True).reshape(
        sequence_length, local_heads, HEAD_SIZE
    )
    key_all, value_all = (
        lax.all_gather(keys[0], "cp", axis=0, tiled=True),
        lax.all_gather(values[0], "cp", axis=0, tiled=True),
    )
    query_group_count = QUERY_HEADS // KEY_VALUE_HEADS
    own_head = lax.axis_index("cp") * local_heads // query_group_count
    key_head = lax.dynamic_slice_in_dim(key_all, own_head * HEAD_SIZE, HEAD_SIZE, 1)
    value_head = lax.dynamic_slice_in_dim(value_all, own_head * HEAD_SIZE, HEAD_SIZE, 1)
    scale = HEAD_SIZE ** (-0.5)
    block_rows = min(512, sequence_length)
    query_parts = []
    key_acc = jnp.zeros((sequence_length, HEAD_SIZE), jnp.float32)
    value_acc = jnp.zeros((sequence_length, HEAD_SIZE), jnp.float32)
    for block_number in range(sequence_length // block_rows):
        block_start = block_number * block_rows
        block_end = block_start + block_rows
        query_block = query_heads[block_start:block_end]
        ctx_block = ctx_heads[block_start:block_end]
        key_block = key_head[:block_end]
        value_block = value_head[:block_end]
        scores = (
            jnp.einsum("qhd,kd->hqk", query_block, key_block, preferred_element_type=jnp.float32)
            * scale
        )
        causal = jnp.arange(block_end)[None, :] <= (block_start + jnp.arange(block_rows))[:, None]
        scores = jnp.where(causal[None], scores, -1e30)
        highest = jnp.max(scores, axis=-1, keepdims=True)
        probs = jnp.exp(scores - highest)
        probs = probs / jnp.sum(probs, axis=-1, keepdims=True)
        probs_low = probs.astype(jnp.bfloat16)
        dprobs = jnp.einsum(
            "qhd,kd->hqk", ctx_block, value_block, preferred_element_type=jnp.float32
        )
        delta = jnp.sum(probs * dprobs, axis=-1, keepdims=True)
        dscores = (probs * (dprobs - delta)).astype(jnp.bfloat16)
        query_parts.append(
            (
                jnp.einsum("hqk,kd->qhd", dscores, key_block, preferred_element_type=jnp.float32)
                * scale
            ).astype(jnp.bfloat16)
        )
        key_acc = key_acc.at[:block_end].add(
            jnp.einsum("hqk,qhd->kd", dscores, query_block, preferred_element_type=jnp.float32)
            * scale
        )
        value_acc = value_acc.at[:block_end].add(
            jnp.einsum("hqk,qhd->kd", probs_low, ctx_block, preferred_element_type=jnp.float32)
        )
    query_all = jnp.concatenate(query_parts, axis=0).reshape(cp_count, local_tokens, 1, head_width)
    query_out = lax.all_to_all(query_all, "cp", split_axis=0, concat_axis=2, tiled=True).reshape(
        1, local_tokens, cp_count * head_width
    )
    zeroed_wide_rows = jnp.zeros((sequence_length, KEY_VALUE_HEADS * HEAD_SIZE), jnp.float32)
    key_wide = lax.dynamic_update_slice_in_dim(zeroed_wide_rows, key_acc, own_head * HEAD_SIZE, 1)
    value_wide = lax.dynamic_update_slice_in_dim(
        zeroed_wide_rows, value_acc, own_head * HEAD_SIZE, 1
    )
    key_gradient_sum, value_gradient_sum = (
        lax.psum_scatter(
            key_wide.astype(jnp.bfloat16), "cp", scatter_dimension=0, tiled=True
        ).astype(jnp.float32),
        lax.psum_scatter(
            value_wide.astype(jnp.bfloat16), "cp", scatter_dimension=0, tiled=True
        ).astype(jnp.float32),
    )
    key_gradient_out = key_gradient_sum.astype(jnp.bfloat16).reshape(
        1, local_tokens, KEY_VALUE_HEADS * HEAD_SIZE
    )
    value_gradient_out = value_gradient_sum.astype(jnp.bfloat16).reshape(
        1, local_tokens, KEY_VALUE_HEADS * HEAD_SIZE
    )
    return (resid.reshape(1, local_tokens, width), query_out, key_gradient_out, value_gradient_out)


def solution(mesh):
    placed = (
        P("dp", "cp", None),
        P("dp", "cp", None),
        P("dp", "cp", None),
        P("dp", "cp", None),
        P("dp", "cp", None),
        P("cp", "dp"),
        P("dp", "cp", None),
        P("dp", "cp", None),
        P(("cp", "dp"), None, None),
        P(("cp", "dp"), None, None),
        P(("cp", "dp"), None, None),
    )
    return jax.shard_map(
        body,
        mesh=mesh,
        in_specs=placed,
        out_specs=(
            P("dp", "cp", None),
            P("dp", "cp", None),
            P("dp", "cp", None),
            P("dp", "cp", None),
        ),
        check_vma=False,
    )
```

profile of v0, /device:TPU:0, one launch (start us, length us, event | category | flops | bytes accessed | tf_op | source)
XLA Modules:
  0.0 694.7 jit_solution(3695952736296254132)
XLA Ops:
  23.2 11.7 %all-to-all-start.1 = ((bf16[128,5,4096]{2,1,0:T(8,128)(2,1)}), bf16[128,5,4096]{2,1,0:T(8,128)(2,1)}, u32[]{:S(2)}, u32[]{:S(2)}) async-start(bf16[128,5,4096]{2,1,0:T(8,128)(2,1)} %bitcast.198), calls=%async_computation.1 | async-start | bytes 16777216 | tf_op jit(solution)/shard_map/all_to_all | solution.py:75
  41.9 97.4 %all-to-all-done.1 = bf16[128,5,4096]{2,1,0:T(8,128)(2,1)} async-done(((bf16[128,5,4096]{2,1,0:T(8,128)(2,1)}), bf16[128,5,4096]{2,1,0:T(8,128)(2,1)}, u32[]{:S(2)}, u32[]{:S(2)}) %all-to-all-start.1) | async-done | bytes 5242912 | tf_op jit(solution)/shard_map/all_to_all | solution.py:75
  145.9 9.2 %all-to-all-start = ((bf16[128,5,4096]{2,1,0:T(8,128)(2,1)}), bf16[128,5,4096]{2,1,0:T(8,128)(2,1)}, u32[]{:S(2)}, u32[]{:S(2)}) async-start(bf16[128,5,4096]{2,1,0:T(8,128)(2,1)} %bitcast.197), calls=%async_computation | async-start | bytes 16777216 | tf_op jit(solution)/shard_map/all_to_all | solution.py:76
  155.8 8.8 %reshape.271 = bf16[640,4096]{1,0:T(8,128)(2,1)} reshape(bf16[128,5,4096]{2,1,0:T(8,128)(2,1)} %all-to-all-done.1) | data formatting | bytes 10485760 | tf_op jit(solution)/shard_map/reshape | solution.py:79
  164.5 9.9 %fusion.8 = f32[640,768]{1,0:T(8,128)} fusion(bf16[640,4096]{1,0:T(8,128)(2,1)} %reshape.271, bf16[1,4096,768]{2,1,0:T(8,128)(2,1)} %param.31), kind=kOutput, calls=%fused_computation.15 | convolution fusion | flops 4026531840 | bytes 13500416 | tf_op jit(solution)/shard_map/dot_general | solution.py:12
  174.4 89.3 %all-to-all-done = bf16[128,5,4096]{2,1,0:T(8,128)(2,1)} async-done(((bf16[128,5,4096]{2,1,0:T(8,128)(2,1)}), bf16[128,5,4096]{2,1,0:T(8,128)(2,1)}, u32[]{:S(2)}, u32[]{:S(2)}) %all-to-all-start) | async-done | bytes 5242912 | tf_op jit(solution)/shard_map/all_to_all | solution.py:76
  263.7 8.9 %reshape.269 = bf16[640,4096]{1,0:T(8,128)(2,1)} reshape(bf16[128,5,4096]{2,1,0:T(8,128)(2,1)} %all-to-all-done) | data formatting | bytes 10485760 | tf_op jit(solution)/shard_map/reshape | solution.py:79
  272.7 8.2 %fusion.13 = f32[640,768]{1,0:T(8,128)S(1)} fusion(bf16[640,4096]{1,0:T(8,128)(2,1)} %reshape.269, bf16[1,768,4096]{2,1,0:T(8,128)(2,1)} %param.33), kind=kOutput, calls=%fused_computation.20 | convolution fusion | flops 4026531840 | bytes 13500416 | tf_op jit(solution)/shard_map/dot_general | solution.py:14
  281.0 8.2 %multiply_convert_fusion.1 = bf16[640,768]{1,0:T(8,128)(2,1)S(1)} fusion(f32[640,768]{1,0:T(8,128)S(1)} %copy-done.13, f32[640,768]{1,0:T(8,128)S(1)} %fusion.13, bf16[640,4096]{1,0:T(8,128)(2,1)S(1)} %bitcast.202, bf16[1,4096,768]{2,1,0:T(8,128)(2,1)} %param.32), kind=kOutput, calls=%fused_computation.50 | convolution fusion | flops 4031447040 | bytes 16449536 | tf_op jit(solution)/shard_map/dot_general | solution.py:13
  289.2 7.0 %fusion.6 = f32[640,4096]{1,0:T(8,128)} fusion(bf16[640,768]{1,0:T(8,128)(2,1)S(1)} %multiply_convert_fusion.1, bf16[1,4096,768]{2,1,0:T(8,128)(2,1)S(1)} %bitcast.215), kind=kOutput, calls=%fused_computation.13 | convolution fusion | flops 4026531840 | bytes 17760256 | tf_op jit(solution)/shard_map/dot_general | solution.py:22
  296.2 13.0 %add_convert_fusion = bf16[640,4096]{1,0:T(8,128)(2,1)} fusion(f32[640,4096]{1,0:T(8,128)} %fusion.6, bf16[1,4096,768]{2,1,0:T(8,128)(2,1)} %param.32, f32[640,768]{1,0:T(8,128)} %copy-done.15, f32[640,768]{1,0:T(8,128)S(1)} %copy-done.14), kind=kOutput, calls=%fused_computation.4 | convolution fusion | flops 4034723840 | bytes 25952256 | tf_op jit(solution)/shard_map/dot_general | solution.py:25
  309.2 8.4 %convert_element_type.90 = bf16[128,5,4096]{2,1,0:T(8,128)(2,1)} reshape(bf16[640,4096]{1,0:T(8,128)(2,1)} %add_convert_fusion) | data formatting | bytes 10485760 | tf_op jit(solution)/shard_map/convert_element_type | solution.py:83
  317.6 7.7 %all-to-all-start.2 = ((bf16[128,5,4096]{2,1,0:T(8,128)(2,1)}), bf16[128,5,4096]{2,1,0:T(8,128)(2,1)}, u32[]{:S(2)}, u32[]{:S(2)}) async-start(bf16[128,5,4096]{2,1,0:T(8,128)(2,1)} %convert_element_type.90), calls=%async_computation.2 | async-start | bytes 16777216 | tf_op jit(solution)/shard_map/all_to_all | solution.py:82
  325.6 104.1 %all-to-all-done.2 = bf16[128,5,4096]{2,1,0:T(8,128)(2,1)} async-done(((bf16[128,5,4096]{2,1,0:T(8,128)(2,1)}), bf16[128,5,4096]{2,1,0:T(8,128)(2,1)}, u32[]{:S(2)}, u32[]{:S(2)}) %all-to-all-start.2) | async-done | bytes 5242912 | tf_op jit(solution)/shard_map/all_to_all | solution.py:82
  429.7 9.6 %convert_reduce_fusion = f32[64,5,4096]{2,1,0:T(8,128)} fusion(bf16[128,5,4096]{2,1,0:T(8,128)(2,1)} %all-to-all-done.2), kind=kLoop, calls=%fused_computation.3 | loop fusion | flops 3932160 | bytes 10485760 | tf_op jit(solution)/shard_map/reduce_sum | solution.py:85
  439.3 6.8 reshape.274
  446.1 8.3 %gather_fusion = f32[256,4096]{1,0:T(8,128)} fusion(f32[320,4096]{1,0:T(8,128)} %reshape.274, s32[1024]{0:T(1024)S(1)} %pad_clamp_fusion), kind=kCustom, calls=%fused_computation | custom fusion | bytes 8389632 | tf_op jit(solution)/shard_map/gather | solution.py:88
  460.2 8.6 %multiply_reduce_fusion = f32[128,4096]{1,0:T(8,128)S(1)} fusion(f32[128,2,4096]{2,1,0:T(2,128)} %reshape.275, f32[128,2]{1,0:T(8,128)S(1)} %copy.90), kind=kLoop, calls=%fused_computation.36 | loop fusion | flops 1572864 | bytes 6292480 | tf_op jit(solution)/shard_map/reduce_sum | solution.py:89
  478.2 52.1 %all-gather = bf16[1,1024,256]{2,1,0:T(8,128)(2,1)} all-gather(bf16[1,128,256]{2,1,0:T(8,128)(2,1)S(1)} %copy-done.10), channel_id=2, replica_groups=mesh['cp'=8,'dp'=16] {'cp'}, dimensions={1}, use_global_device_ids=true | all-gather | bytes 589824 | tf_op jit(solution)/shard_map/all_gather | solution.py:107
  530.3 33.0 %all-gather.1 = bf16[1,1024,256]{2,1,0:T(8,128)(2,1)} all-gather(bf16[1,128,256]{2,1,0:T(8,128)(2,1)S(1)} %copy-done.11), channel_id=3, replica_groups=mesh['cp'=8,'dp'=16] {'cp'}, dimensions={1}, use_global_device_ids=true | all-gather | bytes 589824 | tf_op jit(solution)/shard_map/all_gather | solution.py:108
  574.4 7.6 %fusion.104 = (f32[4,512]{1,0:T(4,128)S(1)}, f32[4,512,1024]{1,2,0:T(8,128)}) fusion(pred[512,1024]{0,1:T(8,128)(4,1)} %iota_compare_fusion, bf16[512,4,128]{2,1,0:T(4,128)(2,1)} %slice.105, bf16[1,1024,256]{2,1,0:T(8,128)(2,1)S(1)} %copy-done.4, s32[]{:T(128)S(6)} %select_n.31), kind=kOutput, calls=%fused_computation.125 | convolution fusion | flops 545260544 | bytes 9707524 | tf_op jit(solution)/shard_map/sub | solution.py:133
  583.9 9.2 %convolution_convert_fusion.2 = bf16[1024,512]{0,1:T(8,128)(2,1)S(1)} fusion(bf16[1024,4096]{1,0:T(8,128)(2,1)} %all-gather.5.cloned.1.call-done, bf16[512,4096]{1,0:T(8,128)(2,1)} %all-gather.7.cloned.1.call-done), kind=kOutput, calls=%fused_computation.52 | convolution fusion | flops 4295491584 | bytes 13631488 | tf_op jit(solution)/shard_map/dot_general | solution.py:95
  623.0 15.5 %all-to-all-done.4 = bf16[8,128,1,512]{1,3,2,0:T(8,128)(2,1)} async-done(((bf16[8,128,1,512]{1,3,2,0:T(8,128)(2,1)}), bf16[8,128,1,512]{1,3,2,0:T(8,128)(2,1)}, u32[]{:S(2)}, u32[]{:S(2)}) %all-to-all-start.4) | async-done | bytes 1048608 | tf_op jit(solution)/shard_map/all_to_all | solution.py:155
  647.0 41.0 %reduce-scatter.5.cloned.1.call-done = bf16[128,256]{1,0:T(8,128)(2,1)} async-done(((bf16[1024,256]{1,0:T(8,128)(2,1)}), bf16[128,256]{1,0:T(8,128)(2,1)}) %reduce-scatter.5.cloned.1.call-update) | async-done | bytes 65552 | tf_op jit(solution)/shard_map/reduce_scatter | solution.py:167
  (117 shorter events, 96.9 us)
Async XLA Ops:
  23.2 11.7 %copy-start.2 = (bf16[1,128,4096]{2,1,0:T(8,128)(2,1)S(1)}, bf16[1,128,4096]{2,1,0:T(8,128)(2,1)}, u32[]{:S(2)}) copy-start(bf16[1,128,4096]{2,1,0:T(8,128)(2,1)} %param.24) | copy-start | bytes 3145732
  23.2 116.2 %all-to-all-start.1 = ((bf16[128,5,4096]{2,1,0:T(8,128)(2,1)}), bf16[128,5,4096]{2,1,0:T(8,128)(2,1)}, u32[]{:S(2)}, u32[]{:S(2)}) async-start(bf16[128,5,4096]{2,1,0:T(8,128)(2,1)} %bitcast.198), calls=%async_computation.1 | async-start | bytes 16777216 | tf_op jit(solution)/shard_map/all_to_all | solution.py:75
  145.9 117.8 %all-to-all-start = ((bf16[128,5,4096]{2,1,0:T(8,128)(2,1)}), bf16[128,5,4096]{2,1,0:T(8,128)(2,1)}, u32[]{:S(2)}, u32[]{:S(2)}) async-start(bf16[128,5,4096]{2,1,0:T(8,128)(2,1)} %bitcast.197), calls=%async_computation | async-start | bytes 16777216 | tf_op jit(solution)/shard_map/all_to_all | solution.py:76
  155.0 427.0 %all-gather.7.cloned.1.call-start = ((), (), s32[]{:S(2)}) async-start(), calls=%async_computation.8 | async-start | bytes 4456448 | tf_op jit(solution)/shard_map/all_gather | solution.py:97
  263.7 17.2 %slice-start.2 = ((s8[5242880]{0:T(1024)(128)(4,1)}), s8[1048576]{0:T(1024)(128)(4,1)S(1)}, s32[]{:S(2)}) async-start(s8[5242880]{0:T(1024)(128)(4,1)} %bitcast.201), calls=%async_computation.13 | async-start | bytes 2097152
  272.7 8.2 %slice-start.3 = ((s8[5242880]{0:T(1024)(128)(4,1)}), s8[4194304]{0:T(1024)(128)(4,1)S(1)}, s32[]{:S(2)}) async-start(s8[5242880]{0:T(1024)(128)(4,1)} %bitcast.201), calls=%async_computation.14 | async-start | bytes 8388608
  272.7 8.3 %copy-start.13 = (f32[640,768]{1,0:T(8,128)S(1)}, f32[640,768]{1,0:T(8,128)}, u32[]{:S(2)}) copy-start(f32[640,768]{1,0:T(8,128)} %fusion.8) | copy-start | bytes 5898244
  272.7 16.5 %slice-start.4 = ((s8[6291456]{0:T(1024)(128)(4,1)}), s8[4194304]{0:T(1024)(128)(4,1)S(1)}, s32[]{:S(2)}) async-start(s8[6291456]{0:T(1024)(128)(4,1)} %bitcast.214), calls=%async_computation.15 | async-start | bytes 8388608
  280.9 8.3 %copy-start.15 = (f32[640,768]{1,0:T(8,128)}, f32[640,768]{1,0:T(8,128)S(1)}, u32[]{:S(2)}) copy-start(f32[640,768]{1,0:T(8,128)S(1)} %fusion.13) | copy-start | bytes 5898244
  280.9 8.3 %slice-start.5 = ((s8[6291456]{0:T(1024)(128)(4,1)}), s8[2097152]{0:T(1024)(128)(4,1)S(1)}, s32[]{:S(2)}) async-start(s8[6291456]{0:T(1024)(128)(4,1)} %bitcast.214), calls=%async_computation.16 | async-start | bytes 4194304
  289.2 7.0 %copy-start.14 = (f32[640,768]{1,0:T(8,128)S(1)}, f32[640,768]{1,0:T(8,128)}, u32[]{:S(2)}) copy-start(f32[640,768]{1,0:T(8,128)} %fusion.8) | copy-start | bytes 5898244
  317.6 7.9 %copy-start.12 = (f32[1,128,2]{1,2,0:T(2,128)S(1)}, f32[1,128,2]{1,2,0:T(2,128)}, u32[]{:S(2)}) copy-start(f32[1,128,2]{1,2,0:T(2,128)} %param.30) | copy-start | bytes 3076
  317.6 112.2 %all-to-all-start.2 = ((bf16[128,5,4096]{2,1,0:T(8,128)(2,1)}), bf16[128,5,4096]{2,1,0:T(8,128)(2,1)}, u32[]{:S(2)}, u32[]{:S(2)}) async-start(bf16[128,5,4096]{2,1,0:T(8,128)(2,1)} %convert_element_type.90), calls=%async_computation.2 | async-start | bytes 16777216 | tf_op jit(solution)/shard_map/all_to_all | solution.py:82
  325.3 258.6 %all-gather.5.cloned.1.call-start = ((), (), s32[]{:S(2)}) async-start(), calls=%async_computation.7 | async-start | bytes 9437184 | tf_op jit(solution)/shard_map/all_gather | solution.py:94
  470.0 8.2 %copy-start.10 = (bf16[1,128,256]{2,1,0:T(8,128)(2,1)S(1)}, bf16[1,128,256]{2,1,0:T(8,128)(2,1)}, u32[]{:S(2)}) copy-start(bf16[1,128,256]{2,1,0:T(8,128)(2,1)} %param.26) | copy-start | bytes 196612
  470.0 60.4 %copy-start.11 = (bf16[1,128,256]{2,1,0:T(8,128)(2,1)S(1)}, bf16[1,128,256]{2,1,0:T(8,128)(2,1)}, u32[]{:S(2)}) copy-start(bf16[1,128,256]{2,1,0:T(8,128)(2,1)} %param.27) | copy-start | bytes 196612
  473.0 91.6 %all-to-all-start.3 = ((bf16[1,128,8,512]{3,1,0,2:T(8,128)(2,1)}), bf16[1,128,8,512]{3,1,0,2:T(8,128)(2,1)S(1)}, u32[]{:S(2)}, u32[]{:S(2)}) async-start(bf16[1,128,8,512]{3,1,0,2:T(8,128)(2,1)} %copy.92), calls=%async_computation.3 | async-start | bytes 2097152 | tf_op jit(solution)/shard_map/all_to_all | solution.py:103
  478.0 169.0 %reduce-scatter.3.cloned.1.call-start = ((), (), s32[]{:S(2)}) async-start(), calls=%async_computation.9 | async-start | bytes 589824 | tf_op jit(solution)/shard_map/reduce_scatter | solution.py:164
  583.9 9.3 %copy-start.3 = (f32[4,512,512]{1,2,0:T(8,128)S(1)}, f32[4,512,512]{1,2,0:T(8,128)}, u32[]{:S(2)}) copy-start(f32[4,512,512]{1,2,0:T(8,128)} %get-tuple-element.89) | copy-start | bytes 12582916
  583.9 9.4 %copy-start.7 = (bf16[1,1024,256]{2,1,0:T(8,128)(2,1)S(1)}, bf16[1,1024,256]{2,1,0:T(8,128)(2,1)}, u32[]{:S(2)}) copy-start(bf16[1,1024,256]{2,1,0:T(8,128)(2,1)} %all-gather.1) | copy-start | bytes 1572868
  593.2 5.6 copy-start.9
  607.8 80.1 %reduce-scatter.5.cloned.1.call-start = ((), (), s32[]{:S(2)}) async-start(), calls=%async_computation.10 | async-start | bytes 589824 | tf_op jit(solution)/shard_map/reduce_scatter | solution.py:167
  615.1 72.8 %copy-start.1 = (bf16[1,128,4096]{2,1,0:T(8,128)(2,1)S(1)}, bf16[1,128,4096]{2,1,0:T(8,128)(2,1)}, u32[]{:S(2)}) copy-start(bf16[1,128,4096]{2,1,0:T(8,128)(2,1)} %param.23) | copy-start | bytes 3145732
  616.3 22.2 %all-to-all-start.4 = ((bf16[8,128,1,512]{1,3,2,0:T(8,128)(2,1)}), bf16[8,128,1,512]{1,3,2,0:T(8,128)(2,1)}, u32[]{:S(2)}, u32[]{:S(2)}) async-start(bf16[8,128,1,512]{1,3,2,0:T(8,128)(2,1)} %copy.101), calls=%async_computation.4 | async-start | bytes 2097152 | tf_op jit(solution)/shard_map/all_to_all | solution.py:155
  (8 other events, 17.2 us)
Sparse Core Ops, SparseCore 0:
  158.1 137.2 all-gather.6
  470.1 113.7 all-gather.4
  607.9 38.9 reduce-scatter.2
  649.9 38.0 reduce-scatter.4
where the time goes:
time: 701 us; the launch traced here: 695 us
  waiting for transfers between devices  356 us (51%)
  local copies, waits for them, and re-layouts  85.4 us (12%)
  blocking collectives  85.2 us (12%)
  matrix products  82.6 us (12%)
  starting transfers between devices  38.1 us (5%)
  other arithmetic  33 us (5%)
  between operations  14.5 us (2%)
    all_to_all x1, waiting for transfers between devices, body(): lax.all_to_all(back.astype(jnp.bfloat16), ('cp', 'dp'), split_axis=0, con...  104 us
    all_to_all x1, waiting for transfers between devices, body(): lax.all_to_all(send_rows, ('cp', 'dp'), split_axis=0, concat_axis=0, tile...  97.4 us
    all_to_all x1, waiting for transfers between devices, body(): lax.all_to_all(send_grads, ('cp', 'dp'), split_axis=0, concat_axis=0, til...  89.3 us
    all_gather x1, blocking collectives, body(): lax.all_gather(keys[0], 'cp', axis=0, tiled=True)  52.1 us
    reduce_scatter x1, waiting for transfers between devices, body(): lax.psum_scatter(value_wide.astype(jnp.bfloat16), 'cp', scatter_dimension...  41 us
    all_gather x1, blocking collectives, body(): lax.all_gather(values[0], 'cp', axis=0, tiled=True)  33 us
    all_to_all x1, waiting for transfers between devices, body(): lax.all_to_all(query_all, 'cp', split_axis=0, concat_axis=2, tiled=True)  15.5 us
  transfers between devices with their start and end apart: 9, of which 7 were waited for; matrix products, arithmetic and copies ran while one was open for 22% of the time, Pallas kernels for 0%

commit v1 on v0

v1 whole, which is shorter than its diff:
```python
import jax
import jax.numpy as jnp
from jax import lax
from jax.experimental import pallas as pl
from jax.experimental.pallas import tpu as pltpu
from jax.sharding import Mesh
from jax.sharding import PartitionSpec as P

HEAD_SIZE = 128
GROUPS = 2
CHIPS = ("zlo", "y", "zhi", "x")
SEQ = ("zlo", "y")
HIDDEN_TILE = 256
NT = (((1,), (1,)), ((), ()))
TN = (((0,), (0,)), ((), ()))
F32 = jnp.float32
BF16 = jnp.bfloat16


def expert_kernel(rows, grads, g0, u0, d0, g1, u1, d1, out, total):
    step = pl.program_id(0)
    half_steps = pl.num_programs(0) // 2
    width = rows.shape[1]
    tile = 512

    @pl.when(step == 0)
    def _():
        total[...] = jnp.zeros_like(total)

    def part(gate, up, down):
        zero = jnp.zeros((rows.shape[0], HIDDEN_TILE), F32)

        def add(i, carry):
            pre_gate, pre_up, upstream = carry
            at = pl.ds(pl.multiple_of(i * tile, tile), tile)
            row_block = rows[:, at]
            pre_gate = pre_gate + jnp.dot(row_block, gate[0, at, :], preferred_element_type=F32)
            pre_up = pre_up + jnp.dot(row_block, up[0, at, :], preferred_element_type=F32)
            upstream = upstream + lax.dot_general(
                grads[:, at], down[0, :, at], NT, preferred_element_type=F32
            )
            return pre_gate, pre_up, upstream

        pre_gate, pre_up, upstream = lax.fori_loop(0, width // tile, add, (zero, zero, zero))
        sig = jax.nn.sigmoid(pre_gate)
        d_gate = (upstream * pre_up * sig * (1.0 + pre_gate * (1.0 - sig))).astype(BF16)
        d_up = (upstream * pre_gate * sig).astype(BF16)

        @pl.loop(0, width // tile)
        def _(i):
            at = pl.ds(pl.multiple_of(i * tile, tile), tile)
            total[:, at] += lax.dot_general(
                d_gate, gate[0, at, :], NT, preferred_element_type=F32
            ) + lax.dot_general(d_up, up[0, at, :], NT, preferred_element_type=F32)

    @pl.when(step < half_steps)
    def _():
        part(g0, u0, d0)

    @pl.when(step >= half_steps)
    def _():
        part(g1, u1, d1)

    @pl.when(step == 2 * half_steps - 1)
    def _():
        out[...] = total[...].astype(BF16)


def expert_back(rows, grads, own, other):
    count, width = rows.shape
    half = own[0].shape[2]
    steps = half // HIDDEN_TILE

    def own_at(i):
        return jnp.minimum(i, steps - 1)

    def other_at(i):
        return jnp.maximum(i - steps, 0)

    in_specs = [
        pl.BlockSpec((count, width), lambda i: (0, 0)),
        pl.BlockSpec((count, width), lambda i: (0, 0)),
    ]
    for at in (own_at, other_at):
        in_specs += [
            pl.BlockSpec((1, width, HIDDEN_TILE), lambda i, at=at: (0, 0, at(i))),
            pl.BlockSpec((1, width, HIDDEN_TILE), lambda i, at=at: (0, 0, at(i))),
            pl.BlockSpec((1, HIDDEN_TILE, width), lambda i, at=at: (0, at(i), 0)),
        ]
    return pl.pallas_call(
        expert_kernel,
        grid=(2 * steps,),
        in_specs=in_specs,
        out_specs=pl.BlockSpec((count, width), lambda i: (0, 0)),
        out_shape=jax.ShapeDtypeStruct((count, width), BF16),
        scratch_shapes=[pltpu.VMEM((count, width), F32)],
        compiler_params=pltpu.CompilerParams(vmem_limit_bytes=56 * 1024 * 1024),
        cost_estimate=pl.CostEstimate(
            flops=20 * count * width * half, bytes_accessed=12 * width * half, transcendentals=0
        ),
        name="expert_back",
    )(rows, grads, *own, *other)


def stack_heads(block):
    heads = block.shape[1] // HEAD_SIZE
    return jnp.concatenate(
        [block[:, h * HEAD_SIZE : (h + 1) * HEAD_SIZE] for h in range(heads)], axis=0
    )


def softmax_kernel(first_row, query, key, probs):
    scale = HEAD_SIZE ** (-0.5)
    tokens = query.shape[0]
    scores = (
        lax.dot_general(stack_heads(query[...]), key[...], NT, preferred_element_type=F32) * scale
    )
    row = lax.broadcasted_iota(jnp.int32, scores.shape, 0) % tokens + first_row[0]
    col = lax.broadcasted_iota(jnp.int32, scores.shape, 1)
    scores = jnp.where(col <= row, scores, -1e30)
    weights = jnp.exp(scores - jnp.max(scores, axis=1, keepdims=True))
    probs[...] = (weights / jnp.sum(weights, axis=1, keepdims=True)).astype(BF16)


def softmax_probs(first_row, queries, kv, block_heads):
    tokens, width = queries.shape
    length = kv.shape[0]
    rows = block_heads * tokens
    steps = width // (block_heads * HEAD_SIZE)
    return pl.pallas_call(
        softmax_kernel,
        grid=(steps,),
        in_specs=[
            pl.BlockSpec(memory_space=pltpu.SMEM),
            pl.BlockSpec((tokens, block_heads * HEAD_SIZE), lambda i: (0, i)),
            pl.BlockSpec((length, HEAD_SIZE), lambda i: (0, i * GROUPS // steps)),
        ],
        out_specs=pl.BlockSpec((rows, length), lambda i: (i, 0)),
        out_shape=jax.ShapeDtypeStruct((steps * rows, length), BF16),
        compiler_params=pltpu.CompilerParams(vmem_limit_bytes=48 * 1024 * 1024),
        cost_estimate=pl.CostEstimate(
            flops=20 * steps * rows * length * HEAD_SIZE,
            bytes_accessed=2 * steps * rows * length,
            transcendentals=steps * rows * length,
        ),
        name="softmax_probs",
    )(first_row, queries, kv)


def attention_kernel(core, resid, own, other, query, probs, key, value, dquery, dkv, dkey, dvalue):
    step = pl.program_id(0)
    scale = HEAD_SIZE ** (-0.5)
    tokens = resid.shape[0]
    pieces, block_cols, depth = own.shape[1:]

    @pl.when(step == 0)
    def _():
        dkey[...] = jnp.zeros_like(dkey)
        dvalue[...] = jnp.zeros_like(dvalue)

    ctx = jnp.zeros((tokens, block_cols), F32)
    for side, shard in ((core[0], own), (1 - core[0], other)):
        for piece in range(pieces):
            at = pl.ds(pl.multiple_of((2 * piece + side) * depth, depth), depth)
            ctx = ctx + lax.dot_general(
                resid[:, at], shard[0, piece], NT, preferred_element_type=F32
            )
    ctx = stack_heads(ctx.astype(BF16))
    query_rows = stack_heads(query[...])
    low = probs[...]
    weights = low.astype(F32)
    dprobs = lax.dot_general(ctx, value[...], NT, preferred_element_type=F32)
    delta = jnp.sum(weights * dprobs, axis=1, keepdims=True)
    dscores = (weights * (dprobs - delta)).astype(BF16)
    dq = jnp.dot(dscores, key[...], preferred_element_type=F32) * scale
    for h in range(block_cols // HEAD_SIZE):
        dquery[:, h * HEAD_SIZE : (h + 1) * HEAD_SIZE] = dq[h * tokens : (h + 1) * tokens].astype(
            BF16
        )
    dkey[...] += lax.dot_general(query_rows, dscores, TN, preferred_element_type=F32)
    dvalue[...] += lax.dot_general(ctx, low, TN, preferred_element_type=F32)

    @pl.when(step == pl.num_programs(0) - 1)
    def _():
        dkv[:, :HEAD_SIZE] = jnp.transpose(dkey[...] * scale).astype(BF16)
        dkv[:, HEAD_SIZE:] = jnp.transpose(dvalue[...]).astype(BF16)


def attention_back(group, core, resid, own, other, queries, probs, kv):
    tokens, width = resid.shape
    blocks, pieces, block_cols, depth = own.shape
    length = kv.shape[0]
    steps = blocks // GROUPS
    first = group * steps
    rows = tokens * block_cols // HEAD_SIZE
    return pl.pallas_call(
        attention_kernel,
        grid=(steps,),
        in_specs=[
            pl.BlockSpec(memory_space=pltpu.SMEM),
            pl.BlockSpec((tokens, width), lambda i: (0, 0)),
            pl.BlockSpec((1, pieces, block_cols, depth), lambda i: (first + i, 0, 0, 0)),
            pl.BlockSpec((1, pieces, block_cols, depth), lambda i: (first + i, 0, 0, 0)),
            pl.BlockSpec((tokens, block_cols), lambda i: (0, first + i)),
            pl.BlockSpec((rows, length), lambda i: (first + i, 0)),
            pl.BlockSpec((length, HEAD_SIZE), lambda i: (0, group)),
            pl.BlockSpec((length, HEAD_SIZE), lambda i: (0, GROUPS + group)),
        ],
        out_specs=[
            pl.BlockSpec((tokens, block_cols), lambda i: (0, i)),
            pl.BlockSpec((length, 2 * HEAD_SIZE), lambda i: (0, 0)),
        ],
        out_shape=[
            jax.ShapeDtypeStruct((tokens, steps * block_cols), BF16),
            jax.ShapeDtypeStruct((length, 2 * HEAD_SIZE), BF16),
        ],
        scratch_shapes=[pltpu.VMEM((HEAD_SIZE, length), F32)] * 2,
        compiler_params=pltpu.CompilerParams(vmem_limit_bytes=56 * 1024 * 1024),
        cost_estimate=pl.CostEstimate(
            flops=2 * steps * rows * (5 * length * HEAD_SIZE + width * HEAD_SIZE),
            bytes_accessed=steps * (2 * width * block_cols + 2 * rows * length),
            transcendentals=0,
        ),
        name="attention_back",
    )(core, resid, own, other, queries, probs, kv, kv)


def to_chips(rows, chips):
    width = rows.shape[1]
    sent = rows.reshape(chips, -1, width)
    return lax.all_to_all(sent, CHIPS, split_axis=0, concat_axis=0, tiled=True).reshape(-1, width)


def other_core(block):
    return lax.ppermute(block, "core", [(0, 1), (1, 0)])


def body(
    hidden_in,
    out_grad,
    queries,
    keys,
    values,
    out_proj,
    expert_ids,
    gate_probs,
    w_gate,
    w_up,
    w_down,
):
    tokens, width = hidden_in.shape[1:]
    top_count = expert_ids.shape[2]
    chips = lax.axis_size(CHIPS)
    experts = chips
    cp_count = lax.axis_size(SEQ)
    capacity = 5
    slots = experts * capacity
    core = lax.axis_index("core").astype(jnp.int32).reshape(1)
    first_row = (lax.axis_index(SEQ) * tokens).astype(jnp.int32).reshape(1)
    own = (w_gate, w_up, w_down)
    other = tuple(other_core(w) for w in own)
    kv = lax.all_gather(jnp.concatenate([keys[0], values[0]], axis=1), SEQ, axis=0, tiled=True)
    proj_own = lax.all_gather(out_proj, CHIPS, axis=0, tiled=False)
    proj_own = proj_own.reshape(cp_count, chips // cp_count, *out_proj.shape)
    proj_other = other_core(proj_own)

    flat_ids = expert_ids.reshape(tokens * top_count)
    hot = (flat_ids[:, None] == jnp.arange(experts, dtype=jnp.int32)[None, :]).astype(jnp.int32)
    earlier = jnp.cumsum(hot, axis=0) - hot
    slot_index = flat_ids * capacity + jnp.sum(earlier * hot, axis=1)
    slot_hot = slot_index.reshape(tokens, top_count, 1) == jnp.arange(slots, dtype=jnp.int32)
    picking = jnp.sum(slot_hot.astype(BF16), axis=1).T
    mixing = jnp.sum(jnp.where(slot_hot, gate_probs[0][:, :, None], 0.0), axis=1)
    mixing_high = mixing.astype(BF16)
    mixing_low = (mixing - mixing_high.astype(F32)).astype(BF16)
    mixing_both = jnp.concatenate([mixing_high, mixing_low], axis=0)

    rows = jnp.dot(picking, hidden_in[0], preferred_element_type=F32).astype(BF16)
    grads = jnp.dot(picking, out_grad[0], preferred_element_type=F32).astype(BF16)
    rows = to_chips(rows, chips)
    grads = to_chips(grads, chips)
    probs = softmax_probs(first_row, queries[0], kv, out_proj.shape[0] // HEAD_SIZE)
    back = expert_back(rows, grads, own, other)
    result = to_chips(back, chips)
    mixed = jnp.dot(mixing_both, result, preferred_element_type=F32)
    resid = (out_grad[0].astype(F32) + (mixed[:tokens] + mixed[tokens:])).astype(BF16)

    query_parts = []
    key_parts = []
    value_parts = []
    for group in range(GROUPS):
        dquery, dkv = attention_back(
            group, core, resid, proj_own, proj_other, queries[0], probs, kv
        )
        parts = lax.all_to_all(
            dkv.reshape(cp_count, tokens, 2 * HEAD_SIZE), SEQ, split_axis=0, concat_axis=0, tiled=True
        )
        dkv_sum = jnp.sum(parts.astype(F32), axis=0).astype(BF16)
        query_parts.append(dquery)
        key_parts.append(dkv_sum[:, :HEAD_SIZE])
        value_parts.append(dkv_sum[:, HEAD_SIZE:])
    return (
        resid[None],
        jnp.concatenate(query_parts, axis=1)[None],
        jnp.concatenate(key_parts, axis=1)[None],
        jnp.concatenate(value_parts, axis=1)[None],
    )


def solution(mesh):
    fine = Mesh(mesh.devices.reshape(2, 4, 2, 4, 2), ("zlo", "y", "zhi", "x", "core"))
    dp = ("zhi", "x", "core")
    token_spec = P(dp, SEQ, None)
    weight_spec = P((*SEQ, *dp), None, None)
    return jax.shard_map(
        body,
        mesh=fine,
        in_specs=(token_spec,) * 5
        + (P(SEQ, dp), token_spec, token_spec, weight_spec, weight_spec, weight_spec),
        out_specs=(token_spec,) * 4,
        check_vma=False,
    )
```

time: 701 us -> 710 us (1.013)
  waiting for transfers between devices: 356 us -> 514 us
  Pallas kernels: 0 us -> 94.7 us
  blocking collectives: 85.2 us -> 0 us
  matrix products: 82.6 us -> 7.72 us
  local copies, waits for them, and re-layouts: 85.4 us -> 31.3 us
  other arithmetic: 33 us -> 5.82 us
    all_gather x2, waiting for transfers between devices: 1.88 us -> 366 us  [the longest x1 366 us: body(): proj_own = lax.all_gather(out_proj, CHIPS, axis=0, tiled=False)]
    all_to_all x5, waiting for transfers between devices: 306 us -> 148 us  [the longest x3 141 us: to_chips(): lax.all_to_all(sent, CHIPS, split_axis=0, concat_axis=0, tiled=True)]
    pallas_call x0 -> x4, Pallas kernels: none -> 94.7 us  [the longest x1 54.6 us: expert_back(): pl.pallas_call(expert_kernel, grid=(2 * steps,), in_specs=in_specs, out_s...]
    all_gather x2 -> x0, blocking collectives: 85.2 us -> none  [the longest x1 52.1 us: body(): lax.all_gather(keys[0], 'cp', axis=0, tiled=True)]
    dot_general x17 -> x3, matrix products: 75 us -> 7.72 us  [the longest x1 3.02 us: body(): mixed = jnp.dot(mixing_both, result, preferred_element_type=F32)]
    reduce_scatter x2 -> x0, waiting for transfers between devices: 47.2 us -> none  [the longest x1 41 us: body(): lax.psum_scatter(value_wide.astype(jnp.bfloat16), 'cp', scatter_dimension...]
    broadcast_in_dim x6 -> x0, local copies, waits for them, and re-layouts: 22.5 us -> none  [the longest x2 11.2 us: body(): jnp.broadcast_to(send_grads.reshape(experts, 1, capacity, width), doubled)]
    reduce_sum x4 -> x5, other arithmetic: 18.3 us -> 0.36 us  [the longest x2 0.15 us: body(): dkv_sum = jnp.sum(parts.astype(F32), axis=0).astype(BF16)]
  transfers between devices with their start and end apart: 9 -> 11, of which waited for: 7 -> 5; matrix products, arithmetic and copies ran while one was open for 22% -> 6% of each run, Pallas kernels for 0% -> 11%
where the time goes in v1:
time: 710 us; the launch traced here: 708 us
  waiting for transfers between devices  514 us (72%)
  Pallas kernels  94.7 us (13%)
  starting transfers between devices  38.3 us (5%)
  local copies, waits for them, and re-layouts  31.3 us (4%)
  between operations  15.7 us (2%)
  matrix products  7.72 us (1%)
    all_gather x1, waiting for transfers between devices, body(): proj_own = lax.all_gather(out_proj, CHIPS, axis=0, tiled=False)  366 us
    all_to_all x3, waiting for transfers between devices, to_chips(): lax.all_to_all(sent, CHIPS, split_axis=0, concat_axis=0, tiled=True)  141 us
    pallas_call x1, Pallas kernels, expert_back(): pl.pallas_call(expert_kernel, grid=(2 * steps,), in_specs=in_specs, out_s...  54.6 us
    pallas_call x2, Pallas kernels, attention_back(): pl.pallas_call(attention_kernel, grid=(steps,), in_specs=[pl.BlockSpec(me...  30.9 us
    all_to_all x3, starting transfers between devices, to_chips(): lax.all_to_all(sent, CHIPS, split_axis=0, concat_axis=0, tiled=True)  26.7 us
    reshape x3, local copies, waits for them, and re-layouts, to_chips(): lax.all_to_all(sent, CHIPS, split_axis=0, concat_axis=0, tiled=True)  14.3 us
    reshape x3, local copies, waits for them, and re-layouts, to_chips(): sent = rows.reshape(chips, -1, width)  14.2 us
  transfers between devices with their start and end apart: 11, of which 5 were waited for; matrix products, arithmetic and copies ran while one was open for 6% of the time, Pallas kernels for 11%

profile of v1, /device:TPU:0, one launch (start us, length us, event | category | flops | bytes accessed | tf_op | source)
XLA Modules:
  0.0 707.9 jit_solution(15542538065167829853)
XLA Ops:
  8.7 365.8 %all-gather.6.cloned.1.call-done = bf16[32768,256]{1,0:T(8,128)(2,1)} async-done(((bf16[512,256]{1,0:T(8,128)(2,1)}), bf16[32768,256]{1,0:T(8,128)(2,1)}) %all-gather.6.cloned.1.call-update) | async-done | bytes 16777232 | tf_op jit(solution)/shard_map/all_gather | solution.py:263
  377.9 2.4 convolution_convert_fusion.1
  380.2 4.7 reshape.74
  385.0 8.6 %all-to-all-start = ((bf16[64,5,4096]{2,1,0:T(8,128)(2,1)}), bf16[64,5,4096]{2,1,0:T(8,128)(2,1)}, u32[]{:S(2)}, u32[]{:S(2)}) async-start(bf16[64,5,4096]{2,1,0:T(8,128)(2,1)} %reshape.74), calls=%async_computation | async-start | bytes 8388608 | tf_op jit(solution)/shard_map/all_to_all | solution.py:231
  393.6 2.3 convolution_convert_fusion
  395.9 4.8 reshape.76
  400.7 46.5 %all-to-all-done = bf16[64,5,4096]{2,1,0:T(8,128)(2,1)} async-done(((bf16[64,5,4096]{2,1,0:T(8,128)(2,1)}), bf16[64,5,4096]{2,1,0:T(8,128)(2,1)}, u32[]{:S(2)}, u32[]{:S(2)}) %all-to-all-start) | async-done | bytes 2621472 | tf_op jit(solution)/shard_map/all_to_all | solution.py:231
  447.2 9.5 %all-to-all-start.1 = ((bf16[64,5,4096]{2,1,0:T(8,128)(2,1)}), bf16[64,5,4096]{2,1,0:T(8,128)(2,1)}, u32[]{:S(2)}, u32[]{:S(2)}) async-start(bf16[64,5,4096]{2,1,0:T(8,128)(2,1)} %reshape.76), calls=%async_computation.1 | async-start | bytes 8388608 | tf_op jit(solution)/shard_map/all_to_all | solution.py:231
  457.4 4.8 reshape.75.rows
  462.2 53.4 %all-to-all-done.1 = bf16[64,5,4096]{2,1,0:T(8,128)(2,1)} async-done(((bf16[64,5,4096]{2,1,0:T(8,128)(2,1)}), bf16[64,5,4096]{2,1,0:T(8,128)(2,1)}, u32[]{:S(2)}, u32[]{:S(2)}) %all-to-all-start.1) | async-done | bytes 2621472 | tf_op jit(solution)/shard_map/all_to_all | solution.py:231
  515.6 4.8 reshape.77.grads
  520.4 54.6 %expert_back.1 = bf16[320,4096]{1,0:T(8,128)(2,1)} custom-call(bf16[320,4096]{1,0:T(8,128)(2,1)} %reshape.75.rows, bf16[320,4096]{1,0:T(8,128)(2,1)} %reshape.77.grads, bf16[1,4096,768]{2,1,0:T(8,128)(2,1)} %g0.1, bf16[1,4096,768]{2,1,0:T(8,128)(2,1)} %u0.1, bf16[1,768,4096]{2,1,0:T(8,128)(2,1)} %d0.1, bf16[1,4096,768]{2,1,0:T(8,128)(2,1)} %collective-permute-done.g1, ...), custom_call_target="tpu_custom_call" | custom-call | flops 20132659200 | bytes 37748736 | tf_op jit(solution)/shard_map/expert_back/pallas_call | solution.py:90
  575.0 4.7 reshape.78
  579.7 8.7 %all-to-all-start.2 = ((bf16[64,5,4096]{2,1,0:T(8,128)(2,1)}), bf16[64,5,4096]{2,1,0:T(8,128)(2,1)}, u32[]{:S(2)}, u32[]{:S(2)}) async-start(bf16[64,5,4096]{2,1,0:T(8,128)(2,1)} %reshape.78), calls=%async_computation.2 | async-start | bytes 8388608 | tf_op jit(solution)/shard_map/all_to_all | solution.py:231
  589.8 9.2 %softmax_probs.1.probs = bf16[4096,1024]{1,0:T(8,128)(2,1)} custom-call(s32[1]{0:T(128)} %bitcast.9.first_row, bf16[128,4096]{1,0:T(8,128)(2,1)S(1)} %bitcast.49, bf16[1024,512]{1,0:T(8,128)(2,1)S(1)} %copy-done.2), custom_call_target="tpu_custom_call" | custom-call | flops 10737418240 | bytes 8388608 | tf_op jit(solution)/shard_map/softmax_probs/pallas_call | solution.py:130
  599.0 41.6 %all-to-all-done.2 = bf16[64,5,4096]{2,1,0:T(8,128)(2,1)} async-done(((bf16[64,5,4096]{2,1,0:T(8,128)(2,1)}), bf16[64,5,4096]{2,1,0:T(8,128)(2,1)}, u32[]{:S(2)}, u32[]{:S(2)}) %all-to-all-start.2) | async-done | bytes 2621472 | tf_op jit(solution)/shard_map/all_to_all | solution.py:231
  640.5 4.8 reshape.79
  645.3 3.0 fusion.6
  649.7 15.4 %attention_back.2 = (bf16[128,2048]{1,0:T(8,128)(2,1)}, bf16[1024,256]{1,0:T(8,128)(2,1)}) custom-call(s32[1]{0:T(128)} %bitcast.6.core, bf16[128,4096]{1,0:T(8,128)(2,1)} %fusion.1.resid, bf16[8,8,512,256]{3,2,1,0:T(8,128)(2,1)} %bitcast.51, bf16[8,8,512,256]{3,2,1,0:T(8,128)(2,1)} %collective-permute-done.3.other, bf16[128,4096]{1,0:T(8,128)(2,1)} %bitcast.47, ...), custom_call_target="tpu_custom_call" | custom-call | flops 4831838208 | bytes 20971520 | tf_op jit(solution)/shard_map/attention_back/pallas_call | solution.py:196
  665.0 4.7 all-to-all-start.3
  669.8 15.5 %attention_back.3 = (bf16[128,2048]{1,0:T(8,128)(2,1)}, bf16[1024,256]{1,0:T(8,128)(2,1)}) custom-call(s32[1]{0:T(128)} %bitcast.6.core, bf16[128,4096]{1,0:T(8,128)(2,1)} %fusion.1.resid, bf16[8,8,512,256]{3,2,1,0:T(8,128)(2,1)} %bitcast.52, bf16[8,8,512,256]{3,2,1,0:T(8,128)(2,1)} %collective-permute-done.3.other, bf16[128,4096]{1,0:T(8,128)(2,1)} %bitcast.48, ...), custom_call_target="tpu_custom_call" | custom-call | flops 4831838208 | bytes 20971520 | tf_op jit(solution)/shard_map/attention_back/pallas_call | solution.py:196
  685.3 5.7 all-to-all-start.4
  691.0 2.1 maximum_bitcast_fusion
  693.2 6.5 all-to-all-done.4
  (54 shorter events, 8.3 us)
Async XLA Ops:
  8.0 369.9 %copy-start = (bf16[1,128,4096]{2,1,0:T(8,128)(2,1)S(1)}, bf16[1,128,4096]{2,1,0:T(8,128)(2,1)}, u32[]{:S(2)}) copy-start(bf16[1,128,4096]{2,1,0:T(8,128)(2,1)} %param.11) | copy-start | bytes 3145732
  8.0 366.5 %all-gather.6.cloned.1.call-start = ((), (), s32[]{:S(2)}) async-start(), calls=%async_computation.6 | async-start | bytes 17039360 | tf_op jit(solution)/shard_map/all_gather | solution.py:263
  374.5 275.2 %collective-permute-start.3 = (bf16[8,8,512,256]{3,2,1,0:T(8,128)(2,1)}, bf16[8,8,512,256]{3,2,1,0:T(8,128)(2,1)}, u32[]{:S(2)}, u32[]{:S(2)}) collective-permute-start(bf16[8,8,512,256]{3,2,1,0:T(8,128)(2,1)} %bitcast.50), channel_id=1, source_target_pairs={{0,1},{1,0},{2,3},{3,2},{4,5},{5,4},{6,7},{7,6},{8,9},{9,8},{10,11... | collective-permute-start | bytes 50331656 | tf_op jit(solution)/shard_map/ppermute | solution.py:235
  374.5 145.9 %collective-permute-start = (bf16[1,4096,768]{2,1,0:T(8,128)(2,1)}, bf16[1,4096,768]{2,1,0:T(8,128)(2,1)}, u32[]{:S(2)}, u32[]{:S(2)}) collective-permute-start(bf16[1,4096,768]{2,1,0:T(8,128)(2,1)} %g0.1), channel_id=1, source_target_pairs={{0,1},{1,0},{2,3},{3,2},{4,5},{5,4},{6,7},{7,6},{8,9},{9,8},{10,11... | collective-permute-start | bytes 18874376 | tf_op jit(solution)/shard_map/ppermute | solution.py:235
  375.0 145.3 %collective-permute-start.1 = (bf16[1,4096,768]{2,1,0:T(8,128)(2,1)}, bf16[1,4096,768]{2,1,0:T(8,128)(2,1)}, u32[]{:S(2)}, u32[]{:S(2)}) collective-permute-start(bf16[1,4096,768]{2,1,0:T(8,128)(2,1)} %u0.1), channel_id=1, source_target_pairs={{0,1},{1,0},{2,3},{3,2},{4,5},{5,4},{6,7},{7,6},{8,9},{9,8},{10,11... | collective-permute-start | bytes 18874376 | tf_op jit(solution)/shard_map/ppermute | solution.py:235
  375.0 145.3 %collective-permute-start.2 = (bf16[1,768,4096]{2,1,0:T(8,128)(2,1)}, bf16[1,768,4096]{2,1,0:T(8,128)(2,1)}, u32[]{:S(2)}, u32[]{:S(2)}) collective-permute-start(bf16[1,768,4096]{2,1,0:T(8,128)(2,1)} %d0.1), channel_id=1, source_target_pairs={{0,1},{1,0},{2,3},{3,2},{4,5},{5,4},{6,7},{7,6},{8,9},{9,8},{10,11... | collective-permute-start | bytes 18874376 | tf_op jit(solution)/shard_map/ppermute | solution.py:235
  385.0 8.6 %copy-start.4 = (bf16[1,128,4096]{2,1,0:T(8,128)(2,1)S(1)}, bf16[1,128,4096]{2,1,0:T(8,128)(2,1)}, u32[]{:S(2)}) copy-start(bf16[1,128,4096]{2,1,0:T(8,128)(2,1)} %param.12) | copy-start | bytes 3145732
  385.0 62.2 %all-to-all-start = ((bf16[64,5,4096]{2,1,0:T(8,128)(2,1)}), bf16[64,5,4096]{2,1,0:T(8,128)(2,1)}, u32[]{:S(2)}, u32[]{:S(2)}) async-start(bf16[64,5,4096]{2,1,0:T(8,128)(2,1)} %reshape.74), calls=%async_computation | async-start | bytes 8388608 | tf_op jit(solution)/shard_map/all_to_all | solution.py:231
  400.7 56.0 %copy-start.6 = (bf16[1,128,256]{2,1,0:T(8,128)(2,1)S(1)}, bf16[1,128,256]{2,1,0:T(8,128)(2,1)}, u32[]{:S(2)}) copy-start(bf16[1,128,256]{2,1,0:T(8,128)(2,1)} %param.15) | copy-start | bytes 196612
  400.7 56.0 %copy-start.7 = (bf16[1,128,256]{2,1,0:T(8,128)(2,1)S(1)}, bf16[1,128,256]{2,1,0:T(8,128)(2,1)}, u32[]{:S(2)}) copy-start(bf16[1,128,256]{2,1,0:T(8,128)(2,1)} %param.14) | copy-start | bytes 196612
  447.2 68.4 %all-to-all-start.1 = ((bf16[64,5,4096]{2,1,0:T(8,128)(2,1)}), bf16[64,5,4096]{2,1,0:T(8,128)(2,1)}, u32[]{:S(2)}, u32[]{:S(2)}) async-start(bf16[64,5,4096]{2,1,0:T(8,128)(2,1)} %reshape.76), calls=%async_computation.1 | async-start | bytes 8388608 | tf_op jit(solution)/shard_map/all_to_all | solution.py:231
  456.7 131.9 %all-gather.4.cloned.1.call-start = ((), (), s32[]{:S(2)}) async-start(), calls=%async_computation.5 | async-start | bytes 1179648 | tf_op jit(solution)/shard_map/all_gather | solution.py:262
  579.7 8.7 %copy-start.8 = (f32[1,128,2]{1,2,0:T(2,128)S(1)}, f32[1,128,2]{1,2,0:T(2,128)}, u32[]{:S(2)}) copy-start(f32[1,128,2]{1,2,0:T(2,128)} %param.18) | copy-start | bytes 3076
  579.7 8.8 %copy-start.3 = (bf16[1,128,4096]{2,1,0:T(8,128)(2,1)S(1)}, bf16[1,128,4096]{2,1,0:T(8,128)(2,1)}, u32[]{:S(2)}) copy-start(bf16[1,128,4096]{2,1,0:T(8,128)(2,1)} %param.13) | copy-start | bytes 3145732
  579.7 60.8 %all-to-all-start.2 = ((bf16[64,5,4096]{2,1,0:T(8,128)(2,1)}), bf16[64,5,4096]{2,1,0:T(8,128)(2,1)}, u32[]{:S(2)}, u32[]{:S(2)}) async-start(bf16[64,5,4096]{2,1,0:T(8,128)(2,1)} %reshape.78), calls=%async_computation.2 | async-start | bytes 8388608 | tf_op jit(solution)/shard_map/all_to_all | solution.py:231
  588.5 1.2 copy-start.2
  665.0 20.3 %all-to-all-start.3 = ((bf16[8,128,256]{2,1,0:T(8,128)(2,1)}), bf16[8,128,256]{2,1,0:T(8,128)(2,1)S(1)}, u32[]{:S(2)}, u32[]{:S(2)}) async-start(bf16[8,128,256]{2,1,0:T(8,128)(2,1)} %bitcast.55), calls=%async_computation.3 | async-start | bytes 1048576 | tf_op jit(solution)/shard_map/all_to_all | solution.py:295
  669.7 21.2 %copy-start.5 = (bf16[128,2048]{1,0:T(8,128)(2,1)S(1)}, bf16[128,2048]{1,0:T(8,128)(2,1)}, u32[]{:S(2)}) copy-start(bf16[128,2048]{1,0:T(8,128)(2,1)} %get-tuple-element.8) | copy-start | bytes 1572868
  669.8 30.7 %copy-start.1 = (bf16[1,128,4096]{2,1,0:T(8,128)(2,1)S(1)}, bf16[1,128,4096]{2,1,0:T(8,128)(2,1)}, u32[]{:S(2)}) copy-start(bf16[1,128,4096]{2,1,0:T(8,128)(2,1)} %param.11) | copy-start | bytes 3145732
  685.3 14.4 %all-to-all-start.4 = ((bf16[8,128,256]{2,1,0:T(8,128)(2,1)}), bf16[8,128,256]{2,1,0:T(8,128)(2,1)S(1)}, u32[]{:S(2)}, u32[]{:S(2)}) async-start(bf16[8,128,256]{2,1,0:T(8,128)(2,1)} %bitcast.54), calls=%async_computation.4 | async-start | bytes 1048576 | tf_op jit(solution)/shard_map/all_to_all | solution.py:295
Sparse Core Ops, SparseCore 0:
  10.5 363.9 all-gather.5
Sparse Core Ops, SparseCore 1:
  459.3 70.6 all-gather.3

commit v2 on v1

v2 whole, which is shorter than its diff:
```python
import functools

import jax
import jax.numpy as jnp
from jax import lax
from jax.experimental import pallas as pl
from jax.experimental.pallas import tpu as pltpu
from jax.sharding import Mesh
from jax.sharding import PartitionSpec as P

HEAD_SIZE = 128
GROUPS = 2
CHIPS = ("zlo", "y", "zhi", "x")
SEQ = ("zlo", "y")
HIDDEN_TILE = 256
NT = (((1,), (1,)), ((), ()))
TN = (((0,), (0,)), ((), ()))
F32 = jnp.float32
BF16 = jnp.bfloat16


def expert_kernel(rows, grads, g0, u0, d0, g1, u1, d1, out, gate, up, down, d_gate, d_up, sems):
    halves, width, half = gate.shape
    tile = 512
    loads = []
    for h, (g, u, d) in enumerate(((g0, u0, d0), (g1, u1, d1))):
        for at in range(0, half, HIDDEN_TILE):
            part = slice(at, at + HIDDEN_TILE)
            copies = [
                pltpu.make_async_copy(g.at[0, :, part], gate.at[h, :, part], sems.at[len(loads), 0]),
                pltpu.make_async_copy(u.at[0, :, part], up.at[h, :, part], sems.at[len(loads), 1]),
                pltpu.make_async_copy(d.at[0, part, :], down.at[h, part, :], sems.at[len(loads), 2]),
            ]
            for copy in copies:
                copy.start()
            loads.append((h, part, copies))
    for h, part, copies in loads:
        for copy in copies:
            copy.wait()
        pre_gate = jnp.dot(rows[...], gate[h, :, part], preferred_element_type=F32)
        pre_up = jnp.dot(rows[...], up[h, :, part], preferred_element_type=F32)
        upstream = lax.dot_general(grads[...], down[h, part, :], NT, preferred_element_type=F32)
        sig = jax.nn.sigmoid(pre_gate)
        d_gate[h, :, part] = (upstream * pre_up * sig * (1.0 + pre_gate * (1.0 - sig))).astype(BF16)
        d_up[h, :, part] = (upstream * pre_gate * sig).astype(BF16)

    @pl.loop(0, width // tile)
    def _(i):
        at = pl.ds(pl.multiple_of(i * tile, tile), tile)
        total = lax.dot_general(d_gate[0], gate[0, at, :], NT, preferred_element_type=F32)
        total += lax.dot_general(d_up[0], up[0, at, :], NT, preferred_element_type=F32)
        for h in range(1, halves):
            total += lax.dot_general(d_gate[h], gate[h, at, :], NT, preferred_element_type=F32)
            total += lax.dot_general(d_up[h], up[h, at, :], NT, preferred_element_type=F32)
        out[:, at] = total.astype(BF16)


def expert_back(rows, grads, own, other):
    count, width = rows.shape
    half = own[0].shape[2]
    held = pl.BlockSpec(memory_space=pltpu.VMEM)
    far = pl.BlockSpec(memory_space=pl.ANY)
    return pl.pallas_call(
        expert_kernel,
        in_specs=[held, held] + [far] * 6,
        out_specs=held,
        out_shape=jax.ShapeDtypeStruct((count, width), BF16),
        scratch_shapes=[
            pltpu.VMEM((2, width, half), BF16),
            pltpu.VMEM((2, width, half), BF16),
            pltpu.VMEM((2, half, width), BF16),
            pltpu.VMEM((2, count, half), BF16),
            pltpu.VMEM((2, count, half), BF16),
            pltpu.SemaphoreType.DMA((2 * half // HIDDEN_TILE, 3)),
        ],
        compiler_params=pltpu.CompilerParams(vmem_limit_bytes=60 * 1024 * 1024),
        cost_estimate=pl.CostEstimate(
            flops=20 * count * width * half, bytes_accessed=12 * width * half, transcendentals=0
        ),
        name="expert_back",
    )(rows, grads, *own, *other)


def stack_heads(block):
    heads = block.shape[1] // HEAD_SIZE
    return jnp.concatenate(
        [block[:, h * HEAD_SIZE : (h + 1) * HEAD_SIZE] for h in range(heads)], axis=0
    )


def softmax_kernel(first_row, query, key, probs):
    scale = HEAD_SIZE ** (-0.5)
    tokens = query.shape[0]
    scores = jnp.dot(stack_heads(query[...]), key[...], preferred_element_type=F32) * scale
    row = lax.broadcasted_iota(jnp.int32, scores.shape, 0) % tokens + first_row[0]
    col = lax.broadcasted_iota(jnp.int32, scores.shape, 1)
    scores = jnp.where(col <= row, scores, -1e30)
    weights = jnp.exp(scores - jnp.max(scores, axis=1, keepdims=True))
    probs[...] = (weights / jnp.sum(weights, axis=1, keepdims=True)).astype(BF16)


def softmax_probs(first_row, queries, key, block_heads):
    tokens, width = queries.shape
    length = key.shape[1]
    rows = block_heads * tokens
    steps = width // (block_heads * HEAD_SIZE)
    return pl.pallas_call(
        softmax_kernel,
        grid=(steps,),
        in_specs=[
            pl.BlockSpec(memory_space=pltpu.SMEM),
            pl.BlockSpec((tokens, block_heads * HEAD_SIZE), lambda i: (0, i)),
            pl.BlockSpec((HEAD_SIZE, length), lambda i: (0, 0)),
        ],
        out_specs=pl.BlockSpec((rows, length), lambda i: (i, 0)),
        out_shape=jax.ShapeDtypeStruct((steps * rows, length), BF16),
        compiler_params=pltpu.CompilerParams(vmem_limit_bytes=48 * 1024 * 1024),
        cost_estimate=pl.CostEstimate(
            flops=20 * steps * rows * length * HEAD_SIZE,
            bytes_accessed=2 * steps * rows * length,
            transcendentals=steps * rows * length,
        ),
        name="softmax_probs",
    )(first_row, queries, key)


def attention_kernel(last, place, resid, a_own, b_own, a_other, b_other, query, probs, key, value_t, *refs):
    if last:
        dkey_in, dvalue_in, dquery, dkv, dkey, dvalue = refs
    else:
        dquery, dkey, dvalue = refs
    core, x_at, zhi_at = place[0], place[1], place[2]
    step = pl.program_id(0)
    scale = HEAD_SIZE ** (-0.5)
    tokens = resid.shape[0]
    x_count, zhi_count, depth = b_own.shape[0], b_own.shape[2], b_own.shape[3]

    @pl.when(step == 0)
    def _():
        if last:
            dkey[...] = dkey_in[...]
            dvalue[...] = dvalue_in[...]
        else:
            dkey[...] = jnp.zeros_like(dkey)
            dvalue[...] = jnp.zeros_like(dvalue)

    first = jnp.zeros((tokens, a_own.shape[4]), F32)
    second = jnp.zeros((tokens, b_own.shape[4]), F32)
    for side, a_part, b_part in ((core, a_own, b_own), (1 - core, a_other, b_other)):
        for r_x in range(x_count):
            for r_z in range(zhi_count):
                x_from = lax.rem(x_at + x_count - r_x, x_count)
                z_from = lax.rem(zhi_at + zhi_count - r_z, zhi_count)
                piece = (z_from * x_count + x_from) * 2 + side
                columns = resid[:, pl.ds(pl.multiple_of(piece * depth, depth), depth)]
                first += jnp.dot(columns, a_part[0, r_x, r_z], preferred_element_type=F32)
                second += jnp.dot(columns, b_part[r_x, 0, r_z], preferred_element_type=F32)
    ctx = jnp.concatenate(
        [stack_heads(first.astype(BF16)), stack_heads(second.astype(BF16))], axis=0
    )
    query_rows = stack_heads(query[...])
    low = probs[...]
    weights = low.astype(F32)
    dprobs = jnp.dot(ctx, value_t[...], preferred_element_type=F32)
    delta = jnp.sum(weights * dprobs, axis=1, keepdims=True)
    dscores = (weights * (dprobs - delta)).astype(BF16)
    dq = jnp.dot(dscores, key[...], preferred_element_type=F32) * scale
    for h in range(query.shape[1] // HEAD_SIZE):
        dquery[:, h * HEAD_SIZE : (h + 1) * HEAD_SIZE] = dq[h * tokens : (h + 1) * tokens].astype(
            BF16
        )
    dkey[...] += lax.dot_general(query_rows, dscores, TN, preferred_element_type=F32)
    dvalue[...] += lax.dot_general(ctx, low, TN, preferred_element_type=F32)

    if last:

        @pl.when(step == pl.num_programs(0) - 1)
        def _():
            dkv[:, :HEAD_SIZE] = jnp.transpose(dkey[...] * scale).astype(BF16)
            dkv[:, HEAD_SIZE:] = jnp.transpose(dvalue[...]).astype(BF16)


def attention_back(place, resid, proj, queries, probs, key, value_t, carried):
    tokens, width = resid.shape
    y_count, x_count, zhi_count, depth, cols = proj[0].shape
    length = key.shape[0]
    block_cols = 2 * cols
    rows = tokens * block_cols // HEAD_SIZE
    last = carried is not None

    def y_of(i, place):
        return lax.rem(place[3] + y_count - i, y_count)

    def whole(*shape):
        return pl.BlockSpec(shape, lambda i, place: (0,) * len(shape))

    a_spec = pl.BlockSpec((1, x_count, zhi_count, depth, cols), lambda i, place: (i, 0, 0, 0, 0))
    b_spec = pl.BlockSpec((x_count, 1, zhi_count, depth, cols), lambda i, place: (0, i, 0, 0, 0))
    block = pl.BlockSpec((tokens, block_cols), lambda i, place: (0, y_of(i, place)))
    in_specs = [
        whole(tokens, width),
        a_spec,
        b_spec,
        a_spec,
        b_spec,
        block,
        pl.BlockSpec((rows, length), lambda i, place: (y_of(i, place), 0)),
        whole(length, HEAD_SIZE),
        whole(HEAD_SIZE, length),
    ]
    sums = jax.ShapeDtypeStruct((HEAD_SIZE, length), F32)
    dquery = jax.ShapeDtypeStruct((tokens, y_count * block_cols), BF16)
    if last:
        in_specs += [whole(HEAD_SIZE, length)] * 2
        out_specs = [block, whole(length, 2 * HEAD_SIZE)]
        out_shape = [dquery, jax.ShapeDtypeStruct((length, 2 * HEAD_SIZE), BF16)]
        scratch = [pltpu.VMEM((HEAD_SIZE, length), F32)] * 2
    else:
        out_specs = [block] + [whole(HEAD_SIZE, length)] * 2
        out_shape = [dquery, sums, sums]
        scratch = []
    return pl.pallas_call(
        functools.partial(attention_kernel, last),
        grid_spec=pltpu.PrefetchScalarGridSpec(
            num_scalar_prefetch=1,
            grid=(y_count,),
            in_specs=in_specs,
            out_specs=out_specs,
            scratch_shapes=scratch,
        ),
        out_shape=out_shape,
        compiler_params=pltpu.CompilerParams(vmem_limit_bytes=56 * 1024 * 1024),
        cost_estimate=pl.CostEstimate(
            flops=2 * y_count * rows * (5 * length * HEAD_SIZE + width * HEAD_SIZE),
            bytes_accessed=y_count * (2 * width * block_cols + 2 * rows * length),
            transcendentals=0,
        ),
        name="attention_back",
    )(place, resid, *proj, queries, probs, key, value_t, *(carried or ()))


def to_chips(rows, chips):
    width = rows.shape[1]
    sent = rows.reshape(chips, -1, width)
    return lax.all_to_all(sent, CHIPS, split_axis=0, concat_axis=0, tiled=True).reshape(-1, width)


def swapped(block, axis):
    return lax.ppermute(block, axis, [(0, 1), (1, 0)])


def shifted(block, axis, by):
    count = lax.axis_size(axis)
    return lax.ppermute(block, axis, [(i, (i + by) % count) for i in range(count)])


def gathered(block, axis):
    return jnp.stack([block] + [shifted(block, axis, k) for k in range(1, lax.axis_size(axis))])


def body(
    hidden_in,
    out_grad,
    queries,
    keys,
    values,
    out_proj,
    expert_ids,
    gate_probs,
    w_gate,
    w_up,
    w_down,
):
    tokens, width = hidden_in.shape[1:]
    top_count = expert_ids.shape[2]
    chips = lax.axis_size(CHIPS)
    experts = chips
    cp_count = lax.axis_size(SEQ)
    capacity = 5
    slots = experts * capacity
    zlo = lax.axis_index("zlo")
    y_at = lax.axis_index("y")
    y_count = lax.axis_size("y")
    place = jnp.stack([lax.axis_index(a) for a in ("core", "x", "zhi", "y")]).astype(jnp.int32)

    flat_ids = expert_ids.reshape(tokens * top_count)
    hot = (flat_ids[:, None] == jnp.arange(experts, dtype=jnp.int32)[None, :]).astype(jnp.int32)
    earlier = jnp.cumsum(hot, axis=0) - hot
    slot_index = flat_ids * capacity + jnp.sum(earlier * hot, axis=1)
    slot_hot = slot_index.reshape(tokens, top_count, 1) == jnp.arange(slots, dtype=jnp.int32)
    picking = jnp.sum(slot_hot.astype(BF16), axis=1).T
    mixing = jnp.sum(jnp.where(slot_hot, gate_probs[0][:, :, None], 0.0), axis=1)
    mixing_high = mixing.astype(BF16)
    mixing_low = (mixing - mixing_high.astype(F32)).astype(BF16)
    mixing_both = jnp.concatenate([mixing_high, mixing_low], axis=0)

    rows = jnp.dot(picking, hidden_in[0], preferred_element_type=F32).astype(BF16)
    grads = jnp.dot(picking, out_grad[0], preferred_element_type=F32).astype(BF16)
    rows = to_chips(rows, chips)
    grads = to_chips(grads, chips)

    own = (w_gate, w_up, w_down)
    other = tuple(swapped(w, "core") for w in own)

    kv = lax.all_gather(jnp.concatenate([keys[0], values[0]], axis=1), SEQ, axis=0, tiled=True)
    key = lax.dynamic_slice_in_dim(kv, zlo * HEAD_SIZE, HEAD_SIZE, 1)
    value = lax.dynamic_slice_in_dim(kv, (GROUPS + zlo) * HEAD_SIZE, HEAD_SIZE, 1)
    key_t, value_t = key.T, value.T
    group_width = width // GROUPS
    own_query = lax.dynamic_slice_in_dim(queries[0], zlo * group_width, group_width, 1)
    near_query = swapped(
        lax.dynamic_slice_in_dim(queries[0], (1 - zlo) * group_width, group_width, 1), "zlo"
    )
    block_heads = out_proj.shape[0] // HEAD_SIZE
    own_row = ((zlo * y_count + y_at) * tokens).astype(jnp.int32).reshape(1)
    near_row = (((1 - zlo) * y_count + y_at) * tokens).astype(jnp.int32).reshape(1)
    own_probs = softmax_probs(own_row, own_query, key_t, block_heads)
    near_probs = softmax_probs(near_row, near_query, key_t, block_heads)

    proj_t = out_proj.T
    cols = proj_t.shape[1] // 2
    proj_a = gathered(gathered(gathered(proj_t[:, :cols], "zhi"), "x"), "y")
    proj_b = gathered(gathered(gathered(proj_t[:, cols:], "zhi"), "y"), "x")
    proj = (proj_a, proj_b, swapped(proj_a, "core"), swapped(proj_b, "core"))

    back = expert_back(rows, grads, own, other)
    result = to_chips(back, chips)
    mixed = jnp.dot(mixing_both, result, preferred_element_type=F32)
    resid = (out_grad[0].astype(F32) + (mixed[:tokens] + mixed[tokens:])).astype(BF16)
    near_resid = swapped(resid, "zlo")

    dquery, dkey, dvalue = attention_back(
        place, resid, proj, own_query, own_probs, key, value_t, None
    )
    near_dquery, dkv = attention_back(
        place, near_resid, proj, near_query, near_probs, key, value_t, (dkey, dvalue)
    )
    far_dquery = swapped(near_dquery, "zlo")
    dquery = jnp.where(
        zlo == 0,
        jnp.concatenate([dquery, far_dquery], axis=1),
        jnp.concatenate([far_dquery, dquery], axis=1),
    )
    parts = lax.all_to_all(
        dkv.reshape(cp_count, tokens, 2 * HEAD_SIZE), SEQ, split_axis=0, concat_axis=0, tiled=True
    )
    parts = parts.reshape(GROUPS, y_count, tokens, 2 * HEAD_SIZE)
    sums = jnp.sum(parts.astype(F32), axis=1).astype(BF16)
    dkey = jnp.concatenate([sums[g, :, :HEAD_SIZE] for g in range(GROUPS)], axis=1)
    dvalue = jnp.concatenate([sums[g, :, HEAD_SIZE:] for g in range(GROUPS)], axis=1)
    return resid[None], dquery[None], dkey[None], dvalue[None]


def solution(mesh):
    fine = Mesh(mesh.devices.reshape(2, 4, 2, 4, 2), ("zlo", "y", "zhi", "x", "core"))
    dp = ("zhi", "x", "core")
    token_spec = P(dp, SEQ, None)
    weight_spec = P((*SEQ, *dp), None, None)
    return jax.shard_map(
        body,
        mesh=fine,
        in_specs=(token_spec,) * 5
        + (P(SEQ, dp), token_spec, token_spec, weight_spec, weight_spec, weight_spec),
        out_specs=(token_spec,) * 4,
        check_vma=False,
    )
```

time: 710 us -> 447 us (0.63)
  waiting for transfers between devices: 514 us -> 206 us
  starting transfers between devices: 38.3 us -> 84.4 us
  Pallas kernels: 94.7 us -> 78.1 us
  other arithmetic: 5.82 us -> 14.3 us
    all_gather x1 -> x0, waiting for transfers between devices: 366 us -> none  [body(): proj_own = lax.all_gather(out_proj, CHIPS, axis=0, tiled=False)]
    ppermute x4 -> x22, waiting for transfers between devices: 0.01 us -> 101 us  [the longest x14 96.8 us: shifted(): lax.ppermute(block, axis, [(i, (i + by) % count) for i in range(count)])]
    all_to_all x3, waiting for transfers between devices: 141 us -> 50.3 us  [to_chips(): lax.all_to_all(sent, CHIPS, split_axis=0, concat_axis=0, tiled=True)]
    all_gather x1, waiting for transfers between devices: 0.03 us -> 47.5 us  [body(): lax.all_gather(jnp.concatenate([keys[0], values[0]], axis=1), SEQ, axis=0...]
    ppermute x4 -> x22, starting transfers between devices: 1.02 us -> 38.8 us  [the longest x14 32.3 us: shifted(): lax.ppermute(block, axis, [(i, (i + by) % count) for i in range(count)])]
    pallas_call x3, Pallas kernels: 85.5 us -> 70.3 us  [the longest x1 43.4 us: expert_back(): pl.pallas_call(expert_kernel, in_specs=[held, held] + [far] * 6, out_spec...]
    all_to_all x3, starting transfers between devices: 26.7 us -> 40.6 us  [to_chips(): lax.all_to_all(sent, CHIPS, split_axis=0, concat_axis=0, tiled=True)]
    another operation x2 -> x9, other arithmetic: 0.65 us -> 11.1 us  [the longest x6 9.88 us: gathered(): jnp.stack([block] + [shifted(block, axis, k) for k in range(1, lax.axis_s...]
  transfers between devices with their start and end apart: 11 -> 27, of which waited for: 5 -> 10; matrix products, arithmetic and copies ran while one was open for 6% -> 12% of each run, Pallas kernels for 11% -> 15%
where the time goes in v2:
time: 447 us; the launch traced here: 442 us
  waiting for transfers between devices  206 us (46%)
  starting transfers between devices  84.4 us (19%)
  Pallas kernels  78.1 us (17%)
  local copies, waits for them, and re-layouts  37 us (8%)
  between operations  14.6 us (3%)
  other arithmetic  14.3 us (3%)
  matrix products  7.51 us (2%)
    ppermute x14, waiting for transfers between devices, shifted(): lax.ppermute(block, axis, [(i, (i + by) % count) for i in range(count)])  96.8 us
    all_to_all x3, waiting for transfers between devices, to_chips(): lax.all_to_all(sent, CHIPS, split_axis=0, concat_axis=0, tiled=True)  50.3 us
    all_gather x1, waiting for transfers between devices, body(): lax.all_gather(jnp.concatenate([keys[0], values[0]], axis=1), SEQ, axis=0...  47.5 us
    pallas_call x1, Pallas kernels, expert_back(): pl.pallas_call(expert_kernel, in_specs=[held, held] + [far] * 6, out_spec...  43.4 us
    all_to_all x3, starting transfers between devices, to_chips(): lax.all_to_all(sent, CHIPS, split_axis=0, concat_axis=0, tiled=True)  40.6 us
    ppermute x14, starting transfers between devices, shifted(): lax.ppermute(block, axis, [(i, (i + by) % count) for i in range(count)])  32.3 us
    pallas_call x2, Pallas kernels, attention_back(): pl.pallas_call(functools.partial(attention_kernel, last), grid_spec=pltpu...  26.9 us
    reshape x3, local copies, waits for them, and re-layouts, to_chips(): lax.all_to_all(sent, CHIPS, split_axis=0, concat_axis=0, tiled=True)  14.3 us
  transfers between devices with their start and end apart: 27, of which 10 were waited for; matrix products, arithmetic and copies ran while one was open for 12% of the time, Pallas kernels for 15%

profile of v2, /device:TPU:0, one launch (start us, length us, event | category | flops | bytes accessed | tf_op | source)
XLA Modules:
  0.0 441.9 jit_solution(4571100077931513285)
XLA Ops:
  12.6 4.7 %reshape.128 = bf16[64,5,4096]{2,1,0:T(8,128)(2,1)} reshape(bf16[320,4096]{1,0:T(8,128)(2,1)} %convolution_convert_fusion.1) | data formatting | bytes 5242880 | tf_op jit(solution)/shard_map/reshape | solution.py:244
  17.3 11.8 %all-to-all-start = ((bf16[64,5,4096]{2,1,0:T(8,128)(2,1)}), bf16[64,5,4096]{2,1,0:T(8,128)(2,1)}, u32[]{:S(2)}, u32[]{:S(2)}) async-start(bf16[64,5,4096]{2,1,0:T(8,128)(2,1)} %reshape.128), calls=%async_computation | async-start | bytes 8388608 | tf_op jit(solution)/shard_map/all_to_all | solution.py:245
  34.0 50.3 %all-to-all-done = bf16[64,5,4096]{2,1,0:T(8,128)(2,1)} async-done(((bf16[64,5,4096]{2,1,0:T(8,128)(2,1)}), bf16[64,5,4096]{2,1,0:T(8,128)(2,1)}, u32[]{:S(2)}, u32[]{:S(2)}) %all-to-all-start) | async-done | bytes 2621472 | tf_op jit(solution)/shard_map/all_to_all | solution.py:245
  84.3 8.6 %all-to-all-start.1 = ((bf16[64,5,4096]{2,1,0:T(8,128)(2,1)}), bf16[64,5,4096]{2,1,0:T(8,128)(2,1)}, u32[]{:S(2)}, u32[]{:S(2)}) async-start(bf16[64,5,4096]{2,1,0:T(8,128)(2,1)} %reshape.130), calls=%async_computation.1 | async-start | bytes 8388608 | tf_op jit(solution)/shard_map/all_to_all | solution.py:245
  96.2 49.3 %collective-permute-done.3 = bf16[256,256]{1,0:T(8,128)(2,1)S(1)} collective-permute-done((bf16[256,256]{1,0:T(8,128)(2,1)S(1)}, bf16[256,256]{1,0:T(8,128)(2,1)S(1)}, u32[]{:S(2)}, u32[]{:S(2)}) %collective-permute-start.3) | collective-permute-done | bytes 131104 | tf_op jit(solution)/shard_map/ppermute | solution.py:254
  145.5 3.9 collective-permute-start.6
  152.0 5.2 %collective-permute-done.6 = bf16[2,256,256]{2,1,0:T(8,128)(2,1)S(1)} collective-permute-done((bf16[2,256,256]{2,1,0:T(8,128)(2,1)S(1)}, bf16[2,256,256]{2,1,0:T(8,128)(2,1)S(1)}, u32[]{:S(2)}, u32[]{:S(2)}) %collective-permute-start.6) | collective-permute-done | bytes 262176 | tf_op jit(solution)/shard_map/ppermute | solution.py:254
  157.2 4.9 %collective-permute-start.4 = (bf16[2,256,256]{2,1,0:T(8,128)(2,1)S(1)}, bf16[2,256,256]{2,1,0:T(8,128)(2,1)S(1)}, u32[]{:S(2)}, u32[]{:S(2)}) collective-permute-start(bf16[2,256,256]{2,1,0:T(8,128)(2,1)S(1)} %get-tuple-element.31), channel_id=1, source_target_pairs={{0,2},{2,4},{4,6},{6,0},{1,3},{3,5},{5,7},{7,1},{8,10},{10,12},{12... | collective-permute-start | bytes 786440 | tf_op jit(solution)/shard_map/ppermute | solution.py:254
  166.1 7.3 %collective-permute-start.9 = (bf16[4,2,256,256]{3,2,1,0:T(8,128)(2,1)S(1)}, bf16[4,2,256,256]{3,2,1,0:T(8,128)(2,1)}, u32[]{:S(2)}, u32[]{:S(2)}) collective-permute-start(bf16[4,2,256,256]{3,2,1,0:T(8,128)(2,1)S(1)} %get-tuple-element.23), channel_id=1, source_target_pairs={{0,48},{16,0},{32,16},{48,32},{1,49},{17,1},{33,17},{49,33},{2,50}... | collective-permute-start | bytes 3145736 | tf_op jit(solution)/shard_map/ppermute | solution.py:254
  173.6 26.5 %collective-permute-done.13 = bf16[2,256,256]{2,1,0:T(8,128)(2,1)S(1)} collective-permute-done((bf16[2,256,256]{2,1,0:T(8,128)(2,1)S(1)}, bf16[2,256,256]{2,1,0:T(8,128)(2,1)S(1)}, u32[]{:S(2)}, u32[]{:S(2)}) %collective-permute-start.13) | collective-permute-done | bytes 262176 | tf_op jit(solution)/shard_map/ppermute | solution.py:254
  202.3 5.6 %collective-permute-done.12 = bf16[2,256,256]{2,1,0:T(8,128)(2,1)S(1)} collective-permute-done((bf16[2,256,256]{2,1,0:T(8,128)(2,1)S(1)}, bf16[2,256,256]{2,1,0:T(8,128)(2,1)S(1)}, u32[]{:S(2)}, u32[]{:S(2)}) %collective-permute-start.12) | collective-permute-done | bytes 262176 | tf_op jit(solution)/shard_map/ppermute | solution.py:254
  210.1 6.3 %collective-permute-done.11 = bf16[2,256,256]{2,1,0:T(8,128)(2,1)} collective-permute-done((bf16[2,256,256]{2,1,0:T(8,128)(2,1)S(1)}, bf16[2,256,256]{2,1,0:T(8,128)(2,1)}, u32[]{:S(2)}, u32[]{:S(2)}) %collective-permute-start.11) | collective-permute-done | bytes 262176 | tf_op jit(solution)/shard_map/ppermute | solution.py:254
  221.0 4.8 %reshape.129.rows = bf16[320,4096]{1,0:T(8,128)(2,1)} reshape(bf16[64,5,4096]{2,1,0:T(8,128)(2,1)} %all-to-all-done) | data formatting | bytes 5242880 | tf_op jit(solution)/shard_map/reshape | solution.py:245
  225.8 4.8 %reshape.131.grads = bf16[320,4096]{1,0:T(8,128)(2,1)} reshape(bf16[64,5,4096]{2,1,0:T(8,128)(2,1)} %all-to-all-done.1) | data formatting | bytes 5242880 | tf_op jit(solution)/shard_map/reshape | solution.py:245
  235.4 43.4 %expert_back.1 = bf16[320,4096]{1,0:T(8,128)(2,1)} custom-call(bf16[320,4096]{1,0:T(8,128)(2,1)} %reshape.129.rows, bf16[320,4096]{1,0:T(8,128)(2,1)} %reshape.131.grads, bf16[1,4096,768]{2,1,0:T(8,128)(2,1)} %g0.1, bf16[1,4096,768]{2,1,0:T(8,128)(2,1)} %u0.1, bf16[1,768,4096]{2,1,0:T(8,128)(2,1)} %d0.1, bf16[1,4096,768]{2,1,0:T(8,128)(2,1)} %collective-permute-done.g1, ...), custom_call_target="tpu_custom_call" | custom-call | flops 20132659200 | bytes 37748736 | tf_op jit(solution)/shard_map/expert_back/pallas_call | solution.py:63
  278.8 4.8 %reshape.132 = bf16[64,5,4096]{2,1,0:T(8,128)(2,1)} reshape(bf16[320,4096]{1,0:T(8,128)(2,1)} %expert_back.1) | data formatting | bytes 5242880 | tf_op jit(solution)/shard_map/reshape | solution.py:244
  283.7 20.2 %all-to-all-start.2 = ((bf16[64,5,4096]{2,1,0:T(8,128)(2,1)}), bf16[64,5,4096]{2,1,0:T(8,128)(2,1)}, u32[]{:S(2)}, u32[]{:S(2)}) async-start(bf16[64,5,4096]{2,1,0:T(8,128)(2,1)} %reshape.132), calls=%async_computation.2 | async-start | bytes 8388608 | tf_op jit(solution)/shard_map/all_to_all | solution.py:245
  315.7 47.5 %all-gather.2.cloned.1.call-done = bf16[1024,512]{0,1:T(8,128)(2,1)} async-done(((bf16[128,512]{0,1:T(8,128)(2,1)}), bf16[1024,512]{0,1:T(8,128)(2,1)}) %all-gather.2.cloned.1.call-update) | async-done | bytes 1048592 | tf_op jit(solution)/shard_map/all_gather | solution.py:305
  365.0 4.8 %reshape.133 = bf16[320,4096]{1,0:T(8,128)(2,1)} reshape(bf16[64,5,4096]{2,1,0:T(8,128)(2,1)} %all-to-all-done.2) | data formatting | bytes 5242880 | tf_op jit(solution)/shard_map/reshape | solution.py:245
  387.6 13.1 %attention_back.2 = (bf16[128,2048]{1,0:T(8,128)(2,1)}, f32[128,1024]{1,0:T(8,128)}, f32[128,1024]{1,0:T(8,128)}) custom-call(s32[4]{0:T(128)} %pad_add_fusion.place, bf16[128,4096]{1,0:T(8,128)(2,1)} %copy-done.6, bf16[4,4,2,256,256]{4,3,2,1,0:T(8,128)(2,1)} %pad_maximum_fusion.a_own, bf16[4,4,2,256,256]{4,3,2,1,0:T(8,128)(2,1)} %pad_maximum_fusion.1.b_own, ...), custom_call_target="tpu_custom_call" | custom-call | flops 4831838208 | bytes 20971520 | tf_op jit(solution)/shard_map/attention_back/pallas_call | solution.py:222
  400.8 13.8 %attention_back.3 = (bf16[128,2048]{1,0:T(8,128)(2,1)}, bf16[1024,256]{1,0:T(8,128)(2,1)}) custom-call(s32[4]{0:T(128)} %pad_add_fusion.place, bf16[128,4096]{1,0:T(8,128)(2,1)} %collective-permute-done.19.resid, bf16[4,4,2,256,256]{4,3,2,1,0:T(8,128)(2,1)} %pad_maximum_fusion.a_own, bf16[4,4,2,256,256]{4,3,2,1,0:T(8,128)(2,1)} %pad_maximum_fusion.1.b_own, ...), custom_call_target="tpu_custom_call" | custom-call | flops 4831838208 | bytes 20971520 | tf_op jit(solution)/shard_map/attention_back/pallas_call | solution.py:222
  414.5 4.9 %all-to-all-start.3 = ((bf16[8,128,256]{2,1,0:T(8,128)(2,1)}), bf16[8,128,256]{2,1,0:T(8,128)(2,1)S(1)}, u32[]{:S(2)}, u32[]{:S(2)}) async-start(bf16[8,128,256]{2,1,0:T(8,128)(2,1)} %bitcast.98), calls=%async_computation.3 | async-start | bytes 1048576 | tf_op jit(solution)/shard_map/all_to_all | solution.py:344
  421.5 6.7 %all-to-all-done.3 = bf16[8,128,256]{2,1,0:T(8,128)(2,1)S(1)} async-done(((bf16[8,128,256]{2,1,0:T(8,128)(2,1)}), bf16[8,128,256]{2,1,0:T(8,128)(2,1)S(1)}, u32[]{:S(2)}, u32[]{:S(2)}) %all-to-all-start.3) | async-done | bytes 524320 | tf_op jit(solution)/shard_map/all_to_all | solution.py:344
  429.0 4.6 %collective-permute-done.21 = bf16[128,2048]{1,0:T(8,128)(2,1)S(1)} collective-permute-done((bf16[128,2048]{1,0:T(8,128)(2,1)}, bf16[128,2048]{1,0:T(8,128)(2,1)S(1)}, u32[]{:S(2)}, u32[]{:S(2)}) %collective-permute-start.21) | collective-permute-done | bytes 524320 | tf_op jit(solution)/shard_map/ppermute | solution.py:249
  (110 shorter events, 69.4 us)
Async XLA Ops:
  7.2 225.4 %collective-permute-start = (bf16[1,4096,768]{2,1,0:T(8,128)(2,1)}, bf16[1,4096,768]{2,1,0:T(8,128)(2,1)}, u32[]{:S(2)}, u32[]{:S(2)}) collective-permute-start(bf16[1,4096,768]{2,1,0:T(8,128)(2,1)} %g0.1), channel_id=1, source_target_pairs={{0,1},{1,0},{2,3},{3,2},{4,5},{5,4},{6,7},{7,6},{8,9},{9,8},{10,11... | collective-permute-start | bytes 18874376 | tf_op jit(solution)/shard_map/ppermute | solution.py:249
  7.3 226.9 %collective-permute-start.1 = (bf16[1,4096,768]{2,1,0:T(8,128)(2,1)}, bf16[1,4096,768]{2,1,0:T(8,128)(2,1)}, u32[]{:S(2)}, u32[]{:S(2)}) collective-permute-start(bf16[1,4096,768]{2,1,0:T(8,128)(2,1)} %u0.1), channel_id=1, source_target_pairs={{0,1},{1,0},{2,3},{3,2},{4,5},{5,4},{6,7},{7,6},{8,9},{9,8},{10,11... | collective-permute-start | bytes 18874376 | tf_op jit(solution)/shard_map/ppermute | solution.py:249
  7.8 226.4 %collective-permute-start.2 = (bf16[1,768,4096]{2,1,0:T(8,128)(2,1)}, bf16[1,768,4096]{2,1,0:T(8,128)(2,1)}, u32[]{:S(2)}, u32[]{:S(2)}) collective-permute-start(bf16[1,768,4096]{2,1,0:T(8,128)(2,1)} %d0.1), channel_id=1, source_target_pairs={{0,1},{1,0},{2,3},{3,2},{4,5},{5,4},{6,7},{7,6},{8,9},{9,8},{10,11... | collective-permute-start | bytes 18874376 | tf_op jit(solution)/shard_map/ppermute | solution.py:249
  17.3 67.1 %all-to-all-start = ((bf16[64,5,4096]{2,1,0:T(8,128)(2,1)}), bf16[64,5,4096]{2,1,0:T(8,128)(2,1)}, u32[]{:S(2)}, u32[]{:S(2)}) async-start(bf16[64,5,4096]{2,1,0:T(8,128)(2,1)} %reshape.128), calls=%async_computation | async-start | bytes 8388608 | tf_op jit(solution)/shard_map/all_to_all | solution.py:245
  84.3 141.5 %all-to-all-start.1 = ((bf16[64,5,4096]{2,1,0:T(8,128)(2,1)}), bf16[64,5,4096]{2,1,0:T(8,128)(2,1)}, u32[]{:S(2)}, u32[]{:S(2)}) async-start(bf16[64,5,4096]{2,1,0:T(8,128)(2,1)} %reshape.130), calls=%async_computation.1 | async-start | bytes 8388608 | tf_op jit(solution)/shard_map/all_to_all | solution.py:245
  93.1 52.4 %collective-permute-start.3 = (bf16[256,256]{1,0:T(8,128)(2,1)S(1)}, bf16[256,256]{1,0:T(8,128)(2,1)S(1)}, u32[]{:S(2)}, u32[]{:S(2)}) collective-permute-start(bf16[256,256]{1,0:T(8,128)(2,1)S(1)} %get-tuple-element.29), channel_id=1, source_target_pairs={{0,8},{8,0},{1,9},{9,1},{2,10},{10,2},{3,11},{11,3},{4,12},{12,4},... | collective-permute-start | bytes 393224 | tf_op jit(solution)/shard_map/ppermute | solution.py:254
  145.5 11.6 %collective-permute-start.6 = (bf16[2,256,256]{2,1,0:T(8,128)(2,1)S(1)}, bf16[2,256,256]{2,1,0:T(8,128)(2,1)S(1)}, u32[]{:S(2)}, u32[]{:S(2)}) collective-permute-start(bf16[2,256,256]{2,1,0:T(8,128)(2,1)S(1)} %get-tuple-element.31), channel_id=1, source_target_pairs={{0,6},{2,0},{4,2},{6,4},{1,7},{3,1},{5,3},{7,5},{8,14},{10,8},{12,... | collective-permute-start | bytes 786440 | tf_op jit(solution)/shard_map/ppermute | solution.py:254
  149.5 12.6 %collective-permute-start.5 = (bf16[2,256,256]{2,1,0:T(8,128)(2,1)S(1)}, bf16[2,256,256]{2,1,0:T(8,128)(2,1)S(1)}, u32[]{:S(2)}, u32[]{:S(2)}) collective-permute-start(bf16[2,256,256]{2,1,0:T(8,128)(2,1)S(1)} %get-tuple-element.31), channel_id=1, source_target_pairs={{0,4},{2,6},{4,0},{6,2},{1,5},{3,7},{5,1},{7,3},{8,12},{10,14},{12... | collective-permute-start | bytes 786440 | tf_op jit(solution)/shard_map/ppermute | solution.py:254
  162.0 11.4 %collective-permute-start.10 = (bf16[256,256]{1,0:T(8,128)(2,1)S(1)}, bf16[256,256]{1,0:T(8,128)(2,1)S(1)}, u32[]{:S(2)}, u32[]{:S(2)}) collective-permute-start(bf16[256,256]{1,0:T(8,128)(2,1)S(1)} %get-tuple-element.28), channel_id=1, source_target_pairs={{0,8},{8,0},{1,9},{9,1},{2,10},{10,2},{3,11},{11,3},{4,12},{12,4},... | collective-permute-start | bytes 393224 | tf_op jit(solution)/shard_map/ppermute | solution.py:254
  166.1 64.4 %collective-permute-start.9 = (bf16[4,2,256,256]{3,2,1,0:T(8,128)(2,1)S(1)}, bf16[4,2,256,256]{3,2,1,0:T(8,128)(2,1)}, u32[]{:S(2)}, u32[]{:S(2)}) collective-permute-start(bf16[4,2,256,256]{3,2,1,0:T(8,128)(2,1)S(1)} %get-tuple-element.23), channel_id=1, source_target_pairs={{0,48},{16,0},{32,16},{48,32},{1,49},{17,1},{33,17},{49,33},{2,50}... | collective-permute-start | bytes 3145736 | tf_op jit(solution)/shard_map/ppermute | solution.py:254
  173.5 26.6 %collective-permute-start.13 = (bf16[2,256,256]{2,1,0:T(8,128)(2,1)S(1)}, bf16[2,256,256]{2,1,0:T(8,128)(2,1)S(1)}, u32[]{:S(2)}, u32[]{:S(2)}) collective-permute-start(bf16[2,256,256]{2,1,0:T(8,128)(2,1)S(1)} %get-tuple-element.25), channel_id=1, source_target_pairs={{0,48},{16,0},{32,16},{48,32},{1,49},{17,1},{33,17},{49,33},{2,50}... | collective-permute-start | bytes 786440 | tf_op jit(solution)/shard_map/ppermute | solution.py:254
  216.4 88.3 %collective-permute-start.8 = (bf16[4,2,256,256]{3,2,1,0:T(8,128)(2,1)S(1)}, bf16[4,2,256,256]{3,2,1,0:T(8,128)(2,1)}, u32[]{:S(2)}, u32[]{:S(2)}) collective-permute-start(bf16[4,2,256,256]{3,2,1,0:T(8,128)(2,1)S(1)} %get-tuple-element.23), channel_id=1, source_target_pairs={{0,32},{16,48},{32,0},{48,16},{1,33},{17,49},{33,1},{49,17},{2,34}... | collective-permute-start | bytes 3145736 | tf_op jit(solution)/shard_map/ppermute | solution.py:254
  230.6 74.1 %collective-permute-start.7 = (bf16[4,2,256,256]{3,2,1,0:T(8,128)(2,1)S(1)}, bf16[4,2,256,256]{3,2,1,0:T(8,128)(2,1)}, u32[]{:S(2)}, u32[]{:S(2)}) collective-permute-start(bf16[4,2,256,256]{3,2,1,0:T(8,128)(2,1)S(1)} %get-tuple-element.23), channel_id=1, source_target_pairs={{0,16},{16,32},{32,48},{48,0},{1,17},{17,33},{33,49},{49,1},{2,18}... | collective-permute-start | bytes 3145736 | tf_op jit(solution)/shard_map/ppermute | solution.py:254
  232.5 75.8 %collective-permute-start.16 = (bf16[4,2,256,256]{3,2,1,0:T(8,128)(2,1)}, bf16[4,2,256,256]{3,2,1,0:T(8,128)(2,1)}, u32[]{:S(2)}, u32[]{:S(2)}) collective-permute-start(bf16[4,2,256,256]{3,2,1,0:T(8,128)(2,1)} %get-tuple-element.21), channel_id=1, source_target_pairs={{0,6},{2,0},{4,2},{6,4},{1,7},{3,1},{5,3},{7,5},{8,14},{10,8},{12,... | collective-permute-start | bytes 3145736 | tf_op jit(solution)/shard_map/ppermute | solution.py:254
  234.2 74.1 %collective-permute-start.15 = (bf16[4,2,256,256]{3,2,1,0:T(8,128)(2,1)}, bf16[4,2,256,256]{3,2,1,0:T(8,128)(2,1)}, u32[]{:S(2)}, u32[]{:S(2)}) collective-permute-start(bf16[4,2,256,256]{3,2,1,0:T(8,128)(2,1)} %get-tuple-element.21), channel_id=1, source_target_pairs={{0,4},{2,6},{4,0},{6,2},{1,5},{3,7},{5,1},{7,3},{8,12},{10,14},{12... | collective-permute-start | bytes 3145736 | tf_op jit(solution)/shard_map/ppermute | solution.py:254
  234.2 74.1 %collective-permute-start.14 = (bf16[4,2,256,256]{3,2,1,0:T(8,128)(2,1)}, bf16[4,2,256,256]{3,2,1,0:T(8,128)(2,1)}, u32[]{:S(2)}, u32[]{:S(2)}) collective-permute-start(bf16[4,2,256,256]{3,2,1,0:T(8,128)(2,1)} %get-tuple-element.21), channel_id=1, source_target_pairs={{0,2},{2,4},{4,6},{6,0},{1,3},{3,5},{5,7},{7,1},{8,10},{10,12},{12... | collective-permute-start | bytes 3145736 | tf_op jit(solution)/shard_map/ppermute | solution.py:254
  283.7 81.3 %all-to-all-start.2 = ((bf16[64,5,4096]{2,1,0:T(8,128)(2,1)}), bf16[64,5,4096]{2,1,0:T(8,128)(2,1)}, u32[]{:S(2)}, u32[]{:S(2)}) async-start(bf16[64,5,4096]{2,1,0:T(8,128)(2,1)} %reshape.132), calls=%async_computation.2 | async-start | bytes 8388608 | tf_op jit(solution)/shard_map/all_to_all | solution.py:245
  303.9 59.3 %all-gather.2.cloned.1.call-start = ((), (), s32[]{:S(2)}) async-start(), calls=%async_computation.4 | async-start | bytes 1179648 | tf_op jit(solution)/shard_map/all_gather | solution.py:305
  308.3 79.3 %collective-permute-start.17 = (bf16[4,4,2,256,256]{4,3,2,1,0:T(8,128)(2,1)}, bf16[4,4,2,256,256]{4,3,2,1,0:T(8,128)(2,1)}, u32[]{:S(2)}, u32[]{:S(2)}) collective-permute-start(bf16[4,4,2,256,256]{4,3,2,1,0:T(8,128)(2,1)} %pad_maximum_fusion.a_own), channel_id=1, source_target_pairs={{0,1},{1,0},{2,3},{3,2},{4,5},{5,4},{6,7},{7,6},{8,9},{9,8},{10,11... | collective-permute-start | bytes 12582920 | tf_op jit(solution)/shard_map/ppermute | solution.py:249
  312.1 75.5 %collective-permute-start.18 = (bf16[4,4,2,256,256]{4,3,2,1,0:T(8,128)(2,1)}, bf16[4,4,2,256,256]{4,3,2,1,0:T(8,128)(2,1)}, u32[]{:S(2)}, u32[]{:S(2)}) collective-permute-start(bf16[4,4,2,256,256]{4,3,2,1,0:T(8,128)(2,1)} %pad_maximum_fusion.1.b_own), channel_id=1, source_target_pairs={{0,1},{1,0},{2,3},{3,2},{4,5},{5,4},{6,7},{7,6},{8,9},{9,8},{10,11... | collective-permute-start | bytes 12582920 | tf_op jit(solution)/shard_map/ppermute | solution.py:249
  313.5 68.2 %collective-permute-start.20 = (bf16[128,2048]{1,0:T(8,128)(2,1)}, bf16[128,2048]{1,0:T(8,128)(2,1)S(1)}, u32[]{:S(2)}, u32[]{:S(2)}) collective-permute-start(bf16[128,2048]{1,0:T(8,128)(2,1)} %get-tuple-element.17), channel_id=1, source_target_pairs={{0,64},{64,0},{1,65},{65,1},{2,66},{66,2},{3,67},{67,3},{4,68},{68... | collective-permute-start | bytes 1572872 | tf_op jit(solution)/shard_map/ppermute | solution.py:249
  373.2 27.5 %collective-permute-start.19 = (bf16[128,4096]{1,0:T(8,128)(2,1)S(1)}, bf16[128,4096]{1,0:T(8,128)(2,1)}, u32[]{:S(2)}, u32[]{:S(2)}) collective-permute-start(bf16[128,4096]{1,0:T(8,128)(2,1)S(1)} %fusion.1.resid), channel_id=1, source_target_pairs={{0,64},{64,0},{1,65},{65,1},{2,66},{66,2},{3,67},{67,3},{4,68},{68... | collective-permute-start | bytes 3145736 | tf_op jit(solution)/shard_map/ppermute | solution.py:249
  414.5 13.7 %all-to-all-start.3 = ((bf16[8,128,256]{2,1,0:T(8,128)(2,1)}), bf16[8,128,256]{2,1,0:T(8,128)(2,1)S(1)}, u32[]{:S(2)}, u32[]{:S(2)}) async-start(bf16[8,128,256]{2,1,0:T(8,128)(2,1)} %bitcast.98), calls=%async_computation.3 | async-start | bytes 1048576 | tf_op jit(solution)/shard_map/all_to_all | solution.py:344
  419.5 14.1 %collective-permute-start.21 = (bf16[128,2048]{1,0:T(8,128)(2,1)}, bf16[128,2048]{1,0:T(8,128)(2,1)S(1)}, u32[]{:S(2)}, u32[]{:S(2)}) collective-permute-start(bf16[128,2048]{1,0:T(8,128)(2,1)} %get-tuple-element.12), channel_id=1, source_target_pairs={{0,64},{64,0},{1,65},{65,1},{2,66},{66,2},{3,67},{67,3},{4,68},{68... | collective-permute-start | bytes 1572872 | tf_op jit(solution)/shard_map/ppermute | solution.py:249
  (18 other events, 389.1 us)
Sparse Core Ops, SparseCore 0:
  306.9 56.3 all-gather.1

commit v3 on v2

--- a/solution.py
+++ b/solution.py
@@ -2,6 +2,7 @@
 
 import jax
 import jax.numpy as jnp
+import numpy as np
 from jax import lax
 from jax.experimental import pallas as pl
 from jax.experimental.pallas import tpu as pltpu
@@ -10,8 +11,14 @@
 
 HEAD_SIZE = 128
 GROUPS = 2
-CHIPS = ("zlo", "y", "zhi", "x")
+CAPACITY = 5
 SEQ = ("zlo", "y")
+RINGS = {"x": ("x", (0, 1, 2, 3)), "y": ("y", (0, 1, 2, 3)), "z": (("zlo", "zhi"), (0, 2, 1, 3))}
+RING = 4
+ORDERS = (("x", "y", "z"), ("y", "z", "x"), ("z", "x", "y"))
+SLOTS = RING**3 * CAPACITY
+CHUNK = SLOTS // RING
+LANES = 128
 HIDDEN_TILE = 256
 NT = (((1,), (1,)), ((), ()))
 TN = (((0,), (0,)), ((), ()))
@@ -19,7 +26,143 @@
 BF16 = jnp.bfloat16
 
 
-def expert_kernel(rows, grads, g0, u0, d0, g1, u1, d1, out, gate, up, down, d_gate, d_up, sems):
+def bounds_of(width):
+    tiles = width // LANES
+    edges = [-(-tiles * p // len(ORDERS)) * LANES for p in range(len(ORDERS) + 1)]
+    return tuple(zip(edges[:-1], edges[1:]))
+
+
+def reorder(axes):
+    index = np.arange(SLOTS).reshape(RING, RING, RING, CAPACITY)
+    moved = index.transpose(*axes, 3).reshape(SLOTS)
+    return jnp.asarray(np.eye(SLOTS, dtype=np.float32)[moved], BF16)
+
+
+def ring(block, axis, by):
+    if by % RING == 0:
+        return block
+    name, number = RINGS[axis]
+    return lax.ppermute(block, name, [(number[i], number[(i + by) % RING]) for i in range(RING)])
+
+
+def route_rows(place, ids):
+    tokens, experts = ids.shape[0], RING**3
+    lane = lax.broadcasted_iota(jnp.int32, (tokens, experts), 1)
+    chosen = [ids[:, k : k + 1] for k in range(ids.shape[1])]
+    hots = [jnp.where(lane == e, 1.0, 0.0) for e in chosen]
+    before = jnp.where(
+        lax.broadcasted_iota(jnp.int32, (tokens, tokens), 1)
+        < lax.broadcasted_iota(jnp.int32, (tokens, tokens), 0),
+        1.0,
+        0.0,
+    ).astype(BF16)
+    earlier = jnp.dot(before, sum(hots).astype(BF16), preferred_element_type=F32)
+    rows = []
+    for e, hot in zip(chosen, hots):
+        slot = jnp.sum(earlier * hot, axis=1, keepdims=True).astype(jnp.int32)
+        z = ((e >> 2) & 1) * 2 + (e >> 5)
+        offset = {
+            "x": ((e & 3) - place[1]) & 3,
+            "y": (((e >> 3) & 3) - place[3]) & 3,
+            "z": (z - place[4]) & 3,
+        }
+        rows.append(
+            [
+                ((offset[a] * RING + offset[b]) * RING + offset[c]) * CAPACITY + slot
+                for a, b, c in ORDERS
+            ]
+        )
+    return rows
+
+
+def pick_kernel(bounds, place, ids, hidden, grads, *outs):
+    rows = route_rows(place, ids)
+    lane = lax.broadcasted_iota(jnp.int32, (ids.shape[0], SLOTS), 1)
+    for p, (low, high) in enumerate(bounds):
+        picking = sum(jnp.where(lane == route[p], 1.0, 0.0) for route in rows).astype(BF16)
+        for side, source in enumerate((hidden, grads)):
+            picked = lax.dot_general(
+                picking, source[:, low:high], TN, preferred_element_type=F32
+            ).astype(BF16)
+            at = slice(side * (high - low), (side + 1) * (high - low))
+            for k in range(RING):
+                outs[p * RING + k][:, at] = picked[k * CHUNK : (k + 1) * CHUNK]
+
+
+def pick(place, ids, hidden, grads):
+    bounds = bounds_of(hidden.shape[1])
+    held = pl.BlockSpec(memory_space=pltpu.VMEM)
+    outs = pl.pallas_call(
+        functools.partial(pick_kernel, bounds),
+        in_specs=[pl.BlockSpec(memory_space=pltpu.SMEM)] + [held] * 3,
+        out_specs=[held] * (RING * len(bounds)),
+        out_shape=[
+            jax.ShapeDtypeStruct((CHUNK, 2 * (high - low)), BF16)
+            for low, high in bounds
+            for _ in range(RING)
+        ],
+        compiler_params=pltpu.CompilerParams(vmem_limit_bytes=48 * 1024 * 1024),
+        name="pick",
+    )(place, ids, hidden, grads)
+    return [outs[p * RING : (p + 1) * RING] for p in range(len(bounds))]
+
+
+def mix_kernel(p, low, high, place, ids, probs, grads, *refs):
+    out = refs[-1]
+    lane = lax.broadcasted_iota(jnp.int32, (ids.shape[0], SLOTS), 1)
+    mixing = sum(
+        jnp.where(lane == route[p], probs[:, k : k + 1], 0.0)
+        for k, route in enumerate(route_rows(place, ids))
+    )
+    mixing_high = mixing.astype(BF16)
+    mixing_low = (mixing - mixing_high.astype(F32)).astype(BF16)
+    rows = jnp.concatenate([ref[...] for ref in refs[:-1]], axis=0)
+    mixed = jnp.dot(mixing_high, rows, preferred_element_type=F32)
+    mixed += jnp.dot(mixing_low, rows, preferred_element_type=F32)
+    out[...] = (grads[:, low:high].astype(F32) + mixed).astype(BF16)
+
+
+def mix(p, place, ids, probs, grads, parts):
+    low, high = bounds_of(grads.shape[1])[p]
+    held = pl.BlockSpec(memory_space=pltpu.VMEM)
+    return pl.pallas_call(
+        functools.partial(mix_kernel, p, low, high),
+        in_specs=[pl.BlockSpec(memory_space=pltpu.SMEM)] + [held] * 7,
+        out_specs=held,
+        out_shape=jax.ShapeDtypeStruct((grads.shape[0], high - low), BF16),
+        compiler_params=pltpu.CompilerParams(vmem_limit_bytes=48 * 1024 * 1024),
+        name="mix",
+    )(place, ids, probs, grads, *parts)
+
+
+def regroup_kernel(count, order, *refs):
+    parts, outs = refs[:RING], refs[len(refs) - count - RING : len(refs) - count]
+    rows = jnp.concatenate([part[...] for part in parts], axis=0)
+    moved = jnp.dot(order[...], rows, preferred_element_type=F32).astype(BF16)
+    for k, out in enumerate(outs):
+        out[...] = moved[k * CHUNK : (k + 1) * CHUNK]
+
+
+def regroup(order, parts, carried=()):
+    held = pl.BlockSpec(memory_space=pltpu.VMEM)
+    far = pl.BlockSpec(memory_space=pl.ANY)
+    count = len(carried)
+    outs = pl.pallas_call(
+        functools.partial(regroup_kernel, count),
+        in_specs=[held] * (1 + RING) + [far] * count,
+        out_specs=[held] * RING + [far] * count,
+        out_shape=[jax.ShapeDtypeStruct(a.shape, a.dtype) for a in (*parts, *carried)],
+        input_output_aliases={1 + RING + i: RING + i for i in range(count)},
+        compiler_params=pltpu.CompilerParams(vmem_limit_bytes=48 * 1024 * 1024),
+        name="regroup",
+    )(order, *parts, *carried)
+    return (outs[:RING], outs[RING:]) if count else outs
+
+
+def expert_kernel(bounds, turn, back_turn, g0, u0, d0, g1, u1, d1, *refs):
+    count = RING * len(bounds)
+    parts, outs = refs[:count], refs[count : 2 * count]
+    rows, grads, gate, up, down, d_gate, d_up, sems = refs[2 * count :]
     halves, width, half = gate.shape
     tile = 512
     loads = []
@@ -34,6 +177,13 @@
             for copy in copies:
                 copy.start()
             loads.append((h, part, copies))
+    for p, (low, high) in enumerate(bounds):
+        came = jnp.concatenate([ref[...] for ref in parts[p * RING : (p + 1) * RING]], axis=0)
+        if p > 0:
+            order = (turn if p == 1 else back_turn)[...]
+            came = jnp.dot(order, came, preferred_element_type=F32).astype(BF16)
+        rows[:, low:high] = came[:, : high - low]
+        grads[:, low:high] = came[:, high - low :]
     for h, part, copies in loads:
         for copy in copies:
             copy.wait()
@@ -52,33 +202,49 @@
         for h in range(1, halves):
             total += lax.dot_general(d_gate[h], gate[h, at, :], NT, preferred_element_type=F32)
             total += lax.dot_general(d_up[h], up[h, at, :], NT, preferred_element_type=F32)
-        out[:, at] = total.astype(BF16)
-
-
-def expert_back(rows, grads, own, other):
-    count, width = rows.shape
-    half = own[0].shape[2]
+        rows[:, at] = total.astype(BF16)
+
+    for p, (low, high) in enumerate(bounds):
+        back = rows[:, low:high]
+        if p > 0:
+            order = (back_turn if p == 1 else turn)[...]
+            back = jnp.dot(order, back, preferred_element_type=F32).astype(BF16)
+        for k in range(RING):
+            outs[p * RING + k][...] = back[k * CHUNK : (k + 1) * CHUNK]
+
+
+def expert_back(parts, own, other):
+    width, half = own[0].shape[1:]
+    bounds = bounds_of(width)
     held = pl.BlockSpec(memory_space=pltpu.VMEM)
     far = pl.BlockSpec(memory_space=pl.ANY)
-    return pl.pallas_call(
-        expert_kernel,
-        in_specs=[held, held] + [far] * 6,
-        out_specs=held,
-        out_shape=jax.ShapeDtypeStruct((count, width), BF16),
+    count = RING * len(bounds)
+    outs = pl.pallas_call(
+        functools.partial(expert_kernel, bounds),
+        in_specs=[held] * 2 + [far] * 6 + [held] * count,
+        out_specs=[held] * count,
+        out_shape=[
+            jax.ShapeDtypeStruct((CHUNK, high - low), BF16)
+            for low, high in bounds
+            for _ in range(RING)
+        ],
         scratch_shapes=[
+            pltpu.VMEM((SLOTS, width), BF16),
+            pltpu.VMEM((SLOTS, width), BF16),
             pltpu.VMEM((2, width, half), BF16),
             pltpu.VMEM((2, width, half), BF16),
             pltpu.VMEM((2, half, width), BF16),
-            pltpu.VMEM((2, count, half), BF16),
-            pltpu.VMEM((2, count, half), BF16),
+            pltpu.VMEM((2, SLOTS, half), BF16),
+            pltpu.VMEM((2, SLOTS, half), BF16),
             pltpu.SemaphoreType.DMA((2 * half // HIDDEN_TILE, 3)),
         ],
         compiler_params=pltpu.CompilerParams(vmem_limit_bytes=60 * 1024 * 1024),
         cost_estimate=pl.CostEstimate(
-            flops=20 * count * width * half, bytes_accessed=12 * width * half, transcendentals=0
+            flops=20 * SLOTS * width * half, bytes_accessed=12 * width * half, transcendentals=0
         ),
         name="expert_back",
-    )(rows, grads, *own, *other)
+    )(reorder((2, 0, 1)), reorder((1, 2, 0)), *own, *other, *[a for part in parts for a in part])
+    return [outs[p * RING : (p + 1) * RING] for p in range(len(bounds))]
 
 
 def stack_heads(block):
@@ -124,19 +290,24 @@
     )(first_row, queries, key)
 
 
-def attention_kernel(last, place, resid, a_own, b_own, a_other, b_other, query, probs, key, value_t, *refs):
+def attention_kernel(
+    last, bounds, place, a_own, b_own, a_other, b_other, query, probs, key, value_t, *refs
+):
+    pieces, refs = refs[: len(bounds)], refs[len(bounds) :]
     if last:
-        dkey_in, dvalue_in, dquery, dkv, dkey, dvalue = refs
+        dkey_in, dvalue_in, dquery, dkv, dkey, dvalue, resid = refs
     else:
-        dquery, dkey, dvalue = refs
+        dquery, dkey, dvalue, resid = refs
     core, x_at, zhi_at = place[0], place[1], place[2]
     step = pl.program_id(0)
     scale = HEAD_SIZE ** (-0.5)
-    tokens = resid.shape[0]
+    tokens = query.shape[0]
     x_count, zhi_count, depth = b_own.shape[0], b_own.shape[2], b_own.shape[3]
 
     @pl.when(step == 0)
     def _():
+        for (low, high), ref in zip(bounds, pieces):
+            resid[:, low:high] = ref[...]
         if last:
             dkey[...] = dkey_in[...]
             dvalue[...] = dvalue_in[...]
@@ -181,7 +352,8 @@
 
 
 def attention_back(place, resid, proj, queries, probs, key, value_t, carried):
-    tokens, width = resid.shape
+    tokens = queries.shape[0]
+    width = sum(piece.shape[1] for piece in resid)
     y_count, x_count, zhi_count, depth, cols = proj[0].shape
     length = key.shape[0]
     block_cols = 2 * cols
@@ -198,7 +370,6 @@
     b_spec = pl.BlockSpec((x_count, 1, zhi_count, depth, cols), lambda i, place: (0, i, 0, 0, 0))
     block = pl.BlockSpec((tokens, block_cols), lambda i, place: (0, y_of(i, place)))
     in_specs = [
-        whole(tokens, width),
         a_spec,
         b_spec,
         a_spec,
@@ -207,20 +378,20 @@
         pl.BlockSpec((rows, length), lambda i, place: (y_of(i, place), 0)),
         whole(length, HEAD_SIZE),
         whole(HEAD_SIZE, length),
-    ]
+    ] + [whole(*piece.shape) for piece in resid]
     sums = jax.ShapeDtypeStruct((HEAD_SIZE, length), F32)
     dquery = jax.ShapeDtypeStruct((tokens, y_count * block_cols), BF16)
     if last:
         in_specs += [whole(HEAD_SIZE, length)] * 2
         out_specs = [block, whole(length, 2 * HEAD_SIZE)]
         out_shape = [dquery, jax.ShapeDtypeStruct((length, 2 * HEAD_SIZE), BF16)]
-        scratch = [pltpu.VMEM((HEAD_SIZE, length), F32)] * 2
+        scratch = [pltpu.VMEM((HEAD_SIZE, length), F32)] * 2 + [pltpu.VMEM((tokens, width), BF16)]
     else:
-        out_specs = [block] + [whole(HEAD_SIZE, length)] * 2
-        out_shape = [dquery, sums, sums]
+        out_specs = [block] + [whole(HEAD_SIZE, length)] * 2 + [whole(tokens, width)]
+        out_shape = [dquery, sums, sums, jax.ShapeDtypeStruct((tokens, width), BF16)]
         scratch = []
     return pl.pallas_call(
-        functools.partial(attention_kernel, last),
+        functools.partial(attention_kernel, last, bounds_of(width)),
         grid_spec=pltpu.PrefetchScalarGridSpec(
             num_scalar_prefetch=1,
             grid=(y_count,),
@@ -236,13 +407,7 @@
             transcendentals=0,
         ),
         name="attention_back",
-    )(place, resid, *proj, queries, probs, key, value_t, *(carried or ()))
-
-
-def to_chips(rows, chips):
-    width = rows.shape[1]
-    sent = rows.reshape(chips, -1, width)
-    return lax.all_to_all(sent, CHIPS, split_axis=0, concat_axis=0, tiled=True).reshape(-1, width)
+    )(place, *proj, queries, probs, key, value_t, *resid, *(carried or ()))
 
 
 def swapped(block, axis):
@@ -272,39 +437,46 @@
     w_down,
 ):
     tokens, width = hidden_in.shape[1:]
-    top_count = expert_ids.shape[2]
-    chips = lax.axis_size(CHIPS)
-    experts = chips
-    cp_count = lax.axis_size(SEQ)
-    capacity = 5
-    slots = experts * capacity
     zlo = lax.axis_index("zlo")
     y_at = lax.axis_index("y")
+    zhi_at = lax.axis_index("zhi")
     y_count = lax.axis_size("y")
-    place = jnp.stack([lax.axis_index(a) for a in ("core", "x", "zhi", "y")]).astype(jnp.int32)
-
-    flat_ids = expert_ids.reshape(tokens * top_count)
-    hot = (flat_ids[:, None] == jnp.arange(experts, dtype=jnp.int32)[None, :]).astype(jnp.int32)
-    earlier = jnp.cumsum(hot, axis=0) - hot
-    slot_index = flat_ids * capacity + jnp.sum(earlier * hot, axis=1)
-    slot_hot = slot_index.reshape(tokens, top_count, 1) == jnp.arange(slots, dtype=jnp.int32)
-    picking = jnp.sum(slot_hot.astype(BF16), axis=1).T
-    mixing = jnp.sum(jnp.where(slot_hot, gate_probs[0][:, :, None], 0.0), axis=1)
-    mixing_high = mixing.astype(BF16)
-    mixing_low = (mixing - mixing_high.astype(F32)).astype(BF16)
-    mixing_both = jnp.concatenate([mixing_high, mixing_low], axis=0)
-
-    rows = jnp.dot(picking, hidden_in[0], preferred_element_type=F32).astype(BF16)
-    grads = jnp.dot(picking, out_grad[0], preferred_element_type=F32).astype(BF16)
-    rows = to_chips(rows, chips)
-    grads = to_chips(grads, chips)
+    place = jnp.stack(
+        [lax.axis_index("core"), lax.axis_index("x"), zhi_at, y_at, 2 * zhi_at + zlo]
+    ).astype(jnp.int32)
+    swap_two, swap_ends = reorder((1, 0, 2)), reorder((2, 1, 0))
+
+    proj_t = out_proj.T
+    cols = proj_t.shape[1] // 2
+    proj_pair = gathered(proj_t, "zhi")
+
+    parts = pick(place, expert_ids[0], hidden_in[0], out_grad[0])
+    for p, order in enumerate(ORDERS):
+        here = [ring(block, order[0], k) for k, block in enumerate(parts[p])]
+        here = regroup(swap_two, here)
+        parts[p] = [ring(block, order[1], k) for k, block in enumerate(here)]
+    for p, order in enumerate(ORDERS):
+        if p == 0:
+            here, (proj_pair,) = regroup(swap_ends, parts[p], (proj_pair,))
+        else:
+            here = regroup(swap_ends, parts[p])
+        parts[p] = [ring(block, order[2], k) for k, block in enumerate(here)]
 
     own = (w_gate, w_up, w_down)
     other = tuple(swapped(w, "core") for w in own)
-
-    kv = lax.all_gather(jnp.concatenate([keys[0], values[0]], axis=1), SEQ, axis=0, tiled=True)
-    key = lax.dynamic_slice_in_dim(kv, zlo * HEAD_SIZE, HEAD_SIZE, 1)
-    value = lax.dynamic_slice_in_dim(kv, (GROUPS + zlo) * HEAD_SIZE, HEAD_SIZE, 1)
+    proj_a = gathered(gathered(proj_pair[:, :, :cols], "x"), "y")
+    proj_b = gathered(gathered(proj_pair[:, :, cols:], "y"), "x")
+    proj = (proj_a, proj_b, swapped(proj_a, "core"), swapped(proj_b, "core"))
+
+    kv = jnp.stack([keys[0], values[0]]).reshape(2, tokens, GROUPS, HEAD_SIZE)
+    own_kv = lax.dynamic_index_in_dim(kv, zlo, 2, keepdims=False)
+    near_kv = swapped(lax.dynamic_index_in_dim(kv, 1 - zlo, 2, keepdims=False), "zlo")
+    all_kv = gathered(
+        jnp.where(zlo == 0, jnp.stack([own_kv, near_kv]), jnp.stack([near_kv, own_kv])), "y"
+    )
+    back_by = jnp.remainder(y_at - jnp.arange(y_count), y_count)
+    all_kv = jnp.take(all_kv, back_by, axis=0).transpose(2, 1, 0, 3, 4).reshape(2, -1, HEAD_SIZE)
+    key, value = all_kv[0], all_kv[1]
     key_t, value_t = key.T, value.T
     group_width = width // GROUPS
     own_query = lax.dynamic_slice_in_dim(queries[0], zlo * group_width, group_width, 1)
@@ -317,19 +489,20 @@
     own_probs = softmax_probs(own_row, own_query, key_t, block_heads)
     near_probs = softmax_probs(near_row, near_query, key_t, block_heads)
 
-    proj_t = out_proj.T
-    cols = proj_t.shape[1] // 2
-    proj_a = gathered(gathered(gathered(proj_t[:, :cols], "zhi"), "x"), "y")
-    proj_b = gathered(gathered(gathered(proj_t[:, cols:], "zhi"), "y"), "x")
-    proj = (proj_a, proj_b, swapped(proj_a, "core"), swapped(proj_b, "core"))
-
-    back = expert_back(rows, grads, own, other)
-    result = to_chips(back, chips)
-    mixed = jnp.dot(mixing_both, result, preferred_element_type=F32)
-    resid = (out_grad[0].astype(F32) + (mixed[:tokens] + mixed[tokens:])).astype(BF16)
-    near_resid = swapped(resid, "zlo")
-
-    dquery, dkey, dvalue = attention_back(
+    parts = expert_back(parts, own, other)
+    resid = []
+    near_resid = []
+    for p, order in enumerate(ORDERS):
+        here = [ring(block, order[2], -k) for k, block in enumerate(parts[p])]
+        here = regroup(swap_ends, here)
+        here = [ring(block, order[1], -k) for k, block in enumerate(here)]
+        here = regroup(swap_two, here)
+        here = [ring(block, order[0], -k) for k, block in enumerate(here)]
+        piece = mix(p, place, expert_ids[0], gate_probs[0], out_grad[0], here)
+        resid.append(piece)
+        near_resid.append(swapped(piece, "zlo"))
+
+    dquery, dkey, dvalue, whole_resid = attention_back(
         place, resid, proj, own_query, own_probs, key, value_t, None
     )
     near_dquery, dkv = attention_back(
@@ -341,14 +514,14 @@
         jnp.concatenate([dquery, far_dquery], axis=1),
         jnp.concatenate([far_dquery, dquery], axis=1),
     )
-    parts = lax.all_to_all(
-        dkv.reshape(cp_count, tokens, 2 * HEAD_SIZE), SEQ, split_axis=0, concat_axis=0, tiled=True
-    )
-    parts = parts.reshape(GROUPS, y_count, tokens, 2 * HEAD_SIZE)
-    sums = jnp.sum(parts.astype(F32), axis=1).astype(BF16)
+    sent = lax.all_to_all(
+        dkv.reshape(-1, tokens, 2 * HEAD_SIZE), SEQ, split_axis=0, concat_axis=0, tiled=True
+    )
+    sent = sent.reshape(GROUPS, y_count, tokens, 2 * HEAD_SIZE)
+    sums = jnp.sum(sent.astype(F32), axis=1).astype(BF16)
     dkey = jnp.concatenate([sums[g, :, :HEAD_SIZE] for g in range(GROUPS)], axis=1)
     dvalue = jnp.concatenate([sums[g, :, HEAD_SIZE:] for g in range(GROUPS)], axis=1)
-    return resid[None], dquery[None], dkey[None], dvalue[None]
+    return whole_resid[None], dquery[None], dkey[None], dvalue[None]
 
 
 def solution(mesh):

time: 447 us -> 508 us (1.14); the launches traced: 442 us -> 498 us
  starting transfers between devices: 84.4 us -> 114 us
  Pallas kernels: 78.1 us -> 97.8 us
  waiting for transfers between devices: 206 us -> 223 us
  between operations: 14.6 us -> 1.58 us
  local copies, waits for them, and re-layouts: 37 us -> 44.8 us
  matrix products: 7.51 us -> 0 us
    ppermute x0 -> x54, starting transfers between devices: none -> 79.3 us  [ring(): lax.ppermute(block, name, [(number[i], number[(i + by) % RING]) for i in...]
    ppermute x0 -> x54, waiting for transfers between devices: none -> 78.2 us  [ring(): lax.ppermute(block, name, [(number[i], number[(i + by) % RING]) for i in...]
    all_to_all x4 -> x1, waiting for transfers between devices: 57.1 us -> 6.72 us  [body(): lax.all_to_all(dkv.reshape(-1, tokens, 2 * HEAD_SIZE), SEQ, split_axis=0,...]
    all_gather x1 -> x0, waiting for transfers between devices: 47.5 us -> none  [body(): lax.all_gather(jnp.concatenate([keys[0], values[0]], axis=1), SEQ, axis=0...]
    all_to_all x4 -> x1, starting transfers between devices: 45.5 us -> 6.66 us  [body(): lax.all_to_all(dkv.reshape(-1, tokens, 2 * HEAD_SIZE), SEQ, split_axis=0,...]
    unnamed x34 -> x161, local copies, waits for them, and re-layouts: 6.06 us -> 34.6 us
    reshape x6 -> x0, local copies, waits for them, and re-layouts: 26.8 us -> none  [the longest x3 14.3 us: to_chips(): lax.all_to_all(sent, CHIPS, split_axis=0, concat_axis=0, tiled=True)]
    ppermute x14 -> x16, waiting for transfers between devices: 96.8 us -> 121 us  [shifted(): lax.ppermute(block, axis, [(i, (i + by) % count) for i in range(count)])]
  transfers between devices with their start and end apart: 27 -> 82, of which waited for: 10 -> 35; matrix products, arithmetic and copies ran while one was open for 12% -> 6% of each run, Pallas kernels for 15% -> 16%
where the time goes in v3:
time: 508 us; the launch traced here: 498 us
  waiting for transfers between devices  223 us (44%)
  starting transfers between devices  114 us (22%)
  Pallas kernels  97.8 us (19%)
  local copies, waits for them, and re-layouts  44.8 us (9%)
  other arithmetic  16 us (3%)
    ppermute x16, waiting for transfers between devices, shifted(): lax.ppermute(block, axis, [(i, (i + by) % count) for i in range(count)])  121 us
    ppermute x54, starting transfers between devices, ring(): lax.ppermute(block, name, [(number[i], number[(i + by) % RING]) for i in...  79.3 us
    ppermute x54, waiting for transfers between devices, ring(): lax.ppermute(block, name, [(number[i], number[(i + by) % RING]) for i in...  78.2 us
    pallas_call x1, Pallas kernels, expert_back(): pl.pallas_call(functools.partial(expert_kernel, bounds), in_specs=[held]...  35.3 us
    unnamed x161, local copies, waits for them, and re-layouts  34.6 us
    pallas_call x2, Pallas kernels, attention_back(): pl.pallas_call(functools.partial(attention_kernel, last, bounds_of(width)...  27.3 us
    ppermute x16, starting transfers between devices, shifted(): lax.ppermute(block, axis, [(i, (i + by) % count) for i in range(count)])  21.2 us
    ppermute x11, waiting for transfers between devices, swapped(): return lax.ppermute(block, axis, [(0, 1), (1, 0)])  17.5 us
  transfers between devices with their start and end apart: 82, of which 35 were waited for; matrix products, arithmetic and copies ran while one was open for 6% of the time, Pallas kernels for 16%

profile of v3, /device:TPU:0, one launch (start us, length us, event | category | flops | bytes accessed | tf_op | source)
XLA Modules:
  0.0 497.5 jit_solution(11689192440746121383)
XLA Ops:
  20.4 8.5 %collective-permute-done.21 = bf16[2,128,128]{2,1,0:T(8,128)(2,1)S(1)} collective-permute-done((bf16[2,128,128]{2,1,0:T(8,128)(2,1)S(1)}, bf16[2,128,128]{2,1,0:T(8,128)(2,1)S(1)}, u32[]{:S(2)}, u32[]{:S(2)}) %collective-permute-start.21) | collective-permute-done | bytes 65568 | tf_op jit(solution)/shard_map/ppermute | solution.py:414
  57.0 6.8 %collective-permute-done.22 = bf16[2,2,128,128]{3,2,1,0:T(8,128)(2,1)S(1)} collective-permute-done((bf16[2,2,128,128]{3,2,1,0:T(8,128)(2,1)S(1)}, bf16[2,2,128,128]{3,2,1,0:T(8,128)(2,1)S(1)}, u32[]{:S(2)}, u32[]{:S(2)}) %collective-permute-start.22) | collective-permute-done | bytes 131104 | tf_op jit(solution)/shard_map/ppermute | solution.py:419
  72.0 5.2 %collective-permute-done.6 = bf16[256,512]{1,0:T(8,128)(2,1)S(1)} collective-permute-done((bf16[256,512]{1,0:T(8,128)(2,1)}, bf16[256,512]{1,0:T(8,128)(2,1)S(1)}, u32[]{:S(2)}, u32[]{:S(2)}) %collective-permute-start.6) | collective-permute-done | bytes 262176 | tf_op jit(solution)/shard_map/ppermute | solution.py:419
  91.9 4.6 collective-permute-done.34.refs_1_
  100.9 11.2 %collective-permute-done.13 = bf16[2,256,256]{2,1,0:T(8,128)(2,1)S(1)} collective-permute-done((bf16[2,256,256]{2,1,0:T(8,128)(2,1)S(1)}, bf16[2,256,256]{2,1,0:T(8,128)(2,1)S(1)}, u32[]{:S(2)}, u32[]{:S(2)}) %collective-permute-start.13) | collective-permute-done | bytes 262176 | tf_op jit(solution)/shard_map/ppermute | solution.py:419
  112.6 7.4 %collective-permute-done.15 = bf16[2,256,256]{2,1,0:T(8,128)(2,1)S(1)} collective-permute-done((bf16[2,256,256]{2,1,0:T(8,128)(2,1)S(1)}, bf16[2,256,256]{2,1,0:T(8,128)(2,1)S(1)}, u32[]{:S(2)}, u32[]{:S(2)}) %collective-permute-start.15) | collective-permute-done | bytes 262176 | tf_op jit(solution)/shard_map/ppermute | solution.py:419
  123.5 5.1 %collective-permute-done.8 = bf16[2,256,256]{2,1,0:T(8,128)(2,1)S(1)} collective-permute-done((bf16[2,256,256]{2,1,0:T(8,128)(2,1)S(1)}, bf16[2,256,256]{2,1,0:T(8,128)(2,1)S(1)}, u32[]{:S(2)}, u32[]{:S(2)}) %collective-permute-start.8) | collective-permute-done | bytes 262176 | tf_op jit(solution)/shard_map/ppermute | solution.py:419
  140.3 5.0 %collective-permute-done.47.refs_10_ = bf16[80,2560]{1,0:T(8,128)(2,1)S(1)} collective-permute-done((bf16[80,2560]{1,0:T(8,128)(2,1)S(1)}, bf16[80,2560]{1,0:T(8,128)(2,1)S(1)}, u32[]{:S(2)}, u32[]{:S(2)}) %collective-permute-start.47) | collective-permute-done | bytes 409632 | tf_op jit(solution)/shard_map/ppermute | solution.py:45
  145.5 8.2 %collective-permute-done.48.refs_11_ = bf16[80,2560]{1,0:T(8,128)(2,1)S(1)} collective-permute-done((bf16[80,2560]{1,0:T(8,128)(2,1)S(1)}, bf16[80,2560]{1,0:T(8,128)(2,1)S(1)}, u32[]{:S(2)}, u32[]{:S(2)}) %collective-permute-start.48) | collective-permute-done | bytes 409632 | tf_op jit(solution)/shard_map/ppermute | solution.py:45
  157.4 8.9 %collective-permute-done.38.refs_6_ = bf16[80,2816]{1,0:T(8,128)(2,1)S(1)} collective-permute-done((bf16[80,2816]{1,0:T(8,128)(2,1)S(1)}, bf16[80,2816]{1,0:T(8,128)(2,1)S(1)}, u32[]{:S(2)}, u32[]{:S(2)}) %collective-permute-start.38) | collective-permute-done | bytes 450592 | tf_op jit(solution)/shard_map/ppermute | solution.py:45
  167.3 9.5 %collective-permute-done.39.refs_7_ = bf16[80,2816]{1,0:T(8,128)(2,1)} collective-permute-done((bf16[80,2816]{1,0:T(8,128)(2,1)S(1)}, bf16[80,2816]{1,0:T(8,128)(2,1)}, u32[]{:S(2)}, u32[]{:S(2)}) %collective-permute-start.39) | collective-permute-done | bytes 450592 | tf_op jit(solution)/shard_map/ppermute | solution.py:45
  182.1 20.2 %collective-permute-done.16 = bf16[4,2,256,256]{3,2,1,0:T(8,128)(2,1)S(1)} collective-permute-done((bf16[4,2,256,256]{3,2,1,0:T(8,128)(2,1)S(1)}, bf16[4,2,256,256]{3,2,1,0:T(8,128)(2,1)S(1)}, u32[]{:S(2)}, u32[]{:S(2)}) %collective-permute-start.16) | collective-permute-done | bytes 1048608 | tf_op jit(solution)/shard_map/ppermute | solution.py:419
  205.2 20.7 %collective-permute-done.17 = bf16[4,2,256,256]{3,2,1,0:T(8,128)(2,1)S(1)} collective-permute-done((bf16[4,2,256,256]{3,2,1,0:T(8,128)(2,1)S(1)}, bf16[4,2,256,256]{3,2,1,0:T(8,128)(2,1)S(1)}, u32[]{:S(2)}, u32[]{:S(2)}) %collective-permute-start.17) | collective-permute-done | bytes 1048608 | tf_op jit(solution)/shard_map/ppermute | solution.py:419
  231.2 21.8 %collective-permute-done.10 = bf16[4,2,256,256]{3,2,1,0:T(8,128)(2,1)S(1)} collective-permute-done((bf16[4,2,256,256]{3,2,1,0:T(8,128)(2,1)}, bf16[4,2,256,256]{3,2,1,0:T(8,128)(2,1)S(1)}, u32[]{:S(2)}, u32[]{:S(2)}) %collective-permute-start.10) | collective-permute-done | bytes 1048608 | tf_op jit(solution)/shard_map/ppermute | solution.py:419
  258.3 17.6 %collective-permute-done.11 = bf16[4,2,256,256]{3,2,1,0:T(8,128)(2,1)} collective-permute-done((bf16[4,2,256,256]{3,2,1,0:T(8,128)(2,1)}, bf16[4,2,256,256]{3,2,1,0:T(8,128)(2,1)}, u32[]{:S(2)}, u32[]{:S(2)}) %collective-permute-start.11) | collective-permute-done | bytes 1048608 | tf_op jit(solution)/shard_map/ppermute | solution.py:419
  289.0 6.4 %collective-permute-done.30.refs_3_ = bf16[80,2816]{1,0:T(8,128)(2,1)S(1)} collective-permute-done((bf16[80,2816]{1,0:T(8,128)(2,1)S(1)}, bf16[80,2816]{1,0:T(8,128)(2,1)S(1)}, u32[]{:S(2)}, u32[]{:S(2)}) %collective-permute-start.30) | collective-permute-done | bytes 450592 | tf_op jit(solution)/shard_map/ppermute | solution.py:45
  296.7 35.3 %expert_back.1 = (bf16[80,1408]{1,0:T(8,128)(2,1)}, bf16[80,1408]{1,0:T(8,128)(2,1)}, bf16[80,1408]{1,0:T(8,128)(2,1)}, bf16[80,1408]{1,0:T(8,128)(2,1)}, bf16[8...) custom-call(bf16[320,320]{1,0:T(8,128)(2,1)} %constant.82.clone.turn, ...), custom_call_target="tpu_custom_call" | custom-call | flops 20132659200 | bytes 37748736 | tf_op jit(solution)/shard_map/expert_back/pallas_call | solution.py:222
  337.0 7.9 %collective-permute-done.67.refs_1_ = bf16[80,1280]{1,0:T(8,128)(2,1)S(1)} collective-permute-done((bf16[80,1280]{1,0:T(8,128)(2,1)}, bf16[80,1280]{1,0:T(8,128)(2,1)S(1)}, u32[]{:S(2)}, u32[]{:S(2)}) %collective-permute-start.67) | collective-permute-done | bytes 204832 | tf_op jit(solution)/shard_map/ppermute | solution.py:45
  349.2 5.0 %collective-permute-done.58.refs_1_ = bf16[80,1408]{1,0:T(8,128)(2,1)S(1)} collective-permute-done((bf16[80,1408]{1,0:T(8,128)(2,1)}, bf16[80,1408]{1,0:T(8,128)(2,1)S(1)}, u32[]{:S(2)}, u32[]{:S(2)}) %collective-permute-start.58) | collective-permute-done | bytes 225312 | tf_op jit(solution)/shard_map/ppermute | solution.py:45
  442.8 13.5 %attention_back.2 = (bf16[128,2048]{1,0:T(8,128)(2,1)}, f32[128,1024]{1,0:T(8,128)}, f32[128,1024]{1,0:T(8,128)}, bf16[128,4096]{1,0:T(8,128)(2,1)}) custom-call(s32[5]{0:T(128)} %copy-done.36, bf16[4,4,2,256,256]{4,3,2,1,0:T(8,128)(2,1)} %pad_maximum_fusion.a_own, bf16[4,4,2,256,256]{4,3,2,1,0:T(8,128)(2,1)} %pad_maximum_fusion.1.b_own, ...), custom_call_target="tpu_custom_call" | custom-call | flops 4831838208 | bytes 20971520 | tf_op jit(solution)/shard_map/attention_back/pallas_call | solution.py:393
  459.2 13.8 %attention_back.3 = (bf16[128,2048]{1,0:T(8,128)(2,1)}, bf16[1024,256]{1,0:T(8,128)(2,1)}) custom-call(s32[5]{0:T(128)} %copy-done.36, bf16[4,4,2,256,256]{4,3,2,1,0:T(8,128)(2,1)} %pad_maximum_fusion.a_own, bf16[4,4,2,256,256]{4,3,2,1,0:T(8,128)(2,1)} %pad_maximum_fusion.1.b_own, bf16[4,4,2,256,256]{4,3,2,1,0:T(8,128)(2,1)} %collective-permute-done.19.a_other, ...), custom_call_target="tpu_custom_call" | custom-call | flops 4831838208 | bytes 20971520 | tf_op jit(solution)/shard_map/attention_back/pallas_call | solution.py:393
  473.0 6.7 %all-to-all-start = ((bf16[8,128,256]{2,1,0:T(8,128)(2,1)}), bf16[8,128,256]{2,1,0:T(8,128)(2,1)S(1)}, u32[]{:S(2)}, u32[]{:S(2)}) async-start(bf16[8,128,256]{2,1,0:T(8,128)(2,1)} %bitcast.103), calls=%async_computation | async-start | bytes 1048576 | tf_op jit(solution)/shard_map/all_to_all | solution.py:517
  481.7 6.7 %all-to-all-done = bf16[8,128,256]{2,1,0:T(8,128)(2,1)S(1)} async-done(((bf16[8,128,256]{2,1,0:T(8,128)(2,1)}), bf16[8,128,256]{2,1,0:T(8,128)(2,1)S(1)}, u32[]{:S(2)}, u32[]{:S(2)}) %all-to-all-start) | async-done | bytes 524320 | tf_op jit(solution)/shard_map/all_to_all | solution.py:517
  489.2 7.0 %collective-permute-done.80 = bf16[128,2048]{1,0:T(8,128)(2,1)S(1)} collective-permute-done((bf16[128,2048]{1,0:T(8,128)(2,1)}, bf16[128,2048]{1,0:T(8,128)(2,1)S(1)}, u32[]{:S(2)}, u32[]{:S(2)}) %collective-permute-start.80) | collective-permute-done | bytes 524320 | tf_op jit(solution)/shard_map/ppermute | solution.py:414
  (351 shorter events, 233.0 us)
Async XLA Ops:
  7.6 24.0 %collective-permute-start.40 = (bf16[80,2560]{1,0:T(8,128)(2,1)}, bf16[80,2560]{1,0:T(8,128)(2,1)S(1)}, u32[]{:S(2)}, u32[]{:S(2)}) collective-permute-start(bf16[80,2560]{1,0:T(8,128)(2,1)} %get-tuple-element.109), channel_id=1, source_target_pairs={{0,64},{64,8},{8,72},{72,0},{1,65},{65,9},{9,73},{73,1},{2,66},{66... | collective-permute-start | bytes 1228808 | tf_op jit(solution)/shard_map/ppermute | solution.py:45
  9.7 27.2 %collective-permute-start.41 = (bf16[80,2560]{1,0:T(8,128)(2,1)}, bf16[80,2560]{1,0:T(8,128)(2,1)}, u32[]{:S(2)}, u32[]{:S(2)}) collective-permute-start(bf16[80,2560]{1,0:T(8,128)(2,1)} %get-tuple-element.110), channel_id=1, source_target_pairs={{0,8},{64,72},{8,0},{72,64},{1,9},{65,73},{9,1},{73,65},{2,10},{66... | collective-permute-start | bytes 1228808 | tf_op jit(solution)/shard_map/ppermute | solution.py:45
  13.3 25.2 %collective-permute-start = (bf16[80,2816]{1,0:T(8,128)(2,1)}, bf16[80,2816]{1,0:T(8,128)(2,1)S(1)}, u32[]{:S(2)}, u32[]{:S(2)}) collective-permute-start(bf16[80,2816]{1,0:T(8,128)(2,1)} %get-tuple-element.84), channel_id=1, source_target_pairs={{0,2},{2,4},{4,6},{6,0},{1,3},{3,5},{5,7},{7,1},{8,10},{10,12},{12... | collective-permute-start | bytes 1351688 | tf_op jit(solution)/shard_map/ppermute | solution.py:45
  14.8 27.6 %collective-permute-start.1 = (bf16[80,2816]{1,0:T(8,128)(2,1)}, bf16[80,2816]{1,0:T(8,128)(2,1)S(1)}, u32[]{:S(2)}, u32[]{:S(2)}) collective-permute-start(bf16[80,2816]{1,0:T(8,128)(2,1)} %get-tuple-element.85), channel_id=1, source_target_pairs={{0,4},{2,6},{4,0},{6,2},{1,5},{3,7},{5,1},{7,3},{8,12},{10,14},{12... | collective-permute-start | bytes 1351688 | tf_op jit(solution)/shard_map/ppermute | solution.py:45
  36.9 29.3 %collective-permute-start.31 = (bf16[80,2816]{1,0:T(8,128)(2,1)}, bf16[80,2816]{1,0:T(8,128)(2,1)S(1)}, u32[]{:S(2)}, u32[]{:S(2)}) collective-permute-start(bf16[80,2816]{1,0:T(8,128)(2,1)} %copy-done.45), channel_id=1, source_target_pairs={{0,16},{16,32},{32,48},{48,0},{1,17},{17,33},{33,49},{49,1},{2,18}... | collective-permute-start | bytes 1351688 | tf_op jit(solution)/shard_map/ppermute | solution.py:45
  38.5 27.7 %collective-permute-start.32 = (bf16[80,2816]{1,0:T(8,128)(2,1)}, bf16[80,2816]{1,0:T(8,128)(2,1)}, u32[]{:S(2)}, u32[]{:S(2)}) collective-permute-start(bf16[80,2816]{1,0:T(8,128)(2,1)} %copy-done.44), channel_id=1, source_target_pairs={{0,32},{16,48},{32,0},{48,16},{1,33},{17,49},{33,1},{49,17},{2,34}... | collective-permute-start | bytes 1351688 | tf_op jit(solution)/shard_map/ppermute | solution.py:45
  42.4 26.2 %collective-permute-start.33 = (bf16[80,2816]{1,0:T(8,128)(2,1)}, bf16[80,2816]{1,0:T(8,128)(2,1)}, u32[]{:S(2)}, u32[]{:S(2)}) collective-permute-start(bf16[80,2816]{1,0:T(8,128)(2,1)} %copy-done.43), channel_id=1, source_target_pairs={{0,48},{16,0},{32,16},{48,32},{1,49},{17,1},{33,17},{49,33},{2,50}... | collective-permute-start | bytes 1351688 | tf_op jit(solution)/shard_map/ppermute | solution.py:45
  49.9 29.2 %collective-permute-start.3 = (bf16[80,2816]{1,0:T(8,128)(2,1)}, bf16[80,2816]{1,0:T(8,128)(2,1)S(1)}, u32[]{:S(2)}, u32[]{:S(2)}) collective-permute-start(bf16[80,2816]{1,0:T(8,128)(2,1)} %get-tuple-element.88), channel_id=1, source_target_pairs={{0,16},{16,32},{32,48},{48,0},{1,17},{17,33},{33,49},{49,1},{2,18}... | collective-permute-start | bytes 1351688 | tf_op jit(solution)/shard_map/ppermute | solution.py:45
  77.2 19.3 %collective-permute-start.34 = (bf16[80,2816]{1,0:T(8,128)(2,1)S(1)}, bf16[80,2816]{1,0:T(8,128)(2,1)S(1)}, u32[]{:S(2)}, u32[]{:S(2)}) collective-permute-start(bf16[80,2816]{1,0:T(8,128)(2,1)S(1)} %get-tuple-element.101), channel_id=1, source_target_pairs={{0,64},{64,8},{8,72},{72,0},{1,65},{65,9},{9,73},{73,1},{2,66},{66... | collective-permute-start | bytes 1351688 | tf_op jit(solution)/shard_map/ppermute | solution.py:45
  87.9 208.0 %collective-permute-start.25 = (bf16[1,4096,768]{2,1,0:T(8,128)(2,1)}, bf16[1,4096,768]{2,1,0:T(8,128)(2,1)}, u32[]{:S(2)}, u32[]{:S(2)}) collective-permute-start(bf16[1,4096,768]{2,1,0:T(8,128)(2,1)} %g0.1), channel_id=1, source_target_pairs={{0,1},{1,0},{2,3},{3,2},{4,5},{5,4},{6,7},{7,6},{8,9},{9,8},{10,11... | collective-permute-start | bytes 18874376 | tf_op jit(solution)/shard_map/ppermute | solution.py:414
  91.9 204.1 %collective-permute-start.26 = (bf16[1,4096,768]{2,1,0:T(8,128)(2,1)}, bf16[1,4096,768]{2,1,0:T(8,128)(2,1)}, u32[]{:S(2)}, u32[]{:S(2)}) collective-permute-start(bf16[1,4096,768]{2,1,0:T(8,128)(2,1)} %u0.1), channel_id=1, source_target_pairs={{0,1},{1,0},{2,3},{3,2},{4,5},{5,4},{6,7},{7,6},{8,9},{9,8},{10,11... | collective-permute-start | bytes 18874376 | tf_op jit(solution)/shard_map/ppermute | solution.py:414
  96.4 199.6 %collective-permute-start.27 = (bf16[1,768,4096]{2,1,0:T(8,128)(2,1)}, bf16[1,768,4096]{2,1,0:T(8,128)(2,1)}, u32[]{:S(2)}, u32[]{:S(2)}) collective-permute-start(bf16[1,768,4096]{2,1,0:T(8,128)(2,1)} %d0.1), channel_id=1, source_target_pairs={{0,1},{1,0},{2,3},{3,2},{4,5},{5,4},{6,7},{7,6},{8,9},{9,8},{10,11... | collective-permute-start | bytes 18874376 | tf_op jit(solution)/shard_map/ppermute | solution.py:414
  156.1 20.6 %collective-permute-start.39 = (bf16[80,2816]{1,0:T(8,128)(2,1)S(1)}, bf16[80,2816]{1,0:T(8,128)(2,1)}, u32[]{:S(2)}, u32[]{:S(2)}) collective-permute-start(bf16[80,2816]{1,0:T(8,128)(2,1)S(1)} %get-tuple-element.107), channel_id=1, source_target_pairs={{0,6},{2,0},{4,2},{6,4},{1,7},{3,1},{5,3},{7,5},{8,14},{10,8},{12,... | collective-permute-start | bytes 1351688 | tf_op jit(solution)/shard_map/ppermute | solution.py:45
  176.8 25.5 %collective-permute-start.16 = (bf16[4,2,256,256]{3,2,1,0:T(8,128)(2,1)S(1)}, bf16[4,2,256,256]{3,2,1,0:T(8,128)(2,1)S(1)}, u32[]{:S(2)}, u32[]{:S(2)}) collective-permute-start(bf16[4,2,256,256]{3,2,1,0:T(8,128)(2,1)S(1)} %get-tuple-element.165), channel_id=1, source_target_pairs={{0,2},{2,4},{4,6},{6,0},{1,3},{3,5},{5,7},{7,1},{8,10},{10,12},{12... | collective-permute-start | bytes 3145736 | tf_op jit(solution)/shard_map/ppermute | solution.py:419
  177.9 48.0 %collective-permute-start.17 = (bf16[4,2,256,256]{3,2,1,0:T(8,128)(2,1)S(1)}, bf16[4,2,256,256]{3,2,1,0:T(8,128)(2,1)S(1)}, u32[]{:S(2)}, u32[]{:S(2)}) collective-permute-start(bf16[4,2,256,256]{3,2,1,0:T(8,128)(2,1)S(1)} %get-tuple-element.165), channel_id=1, source_target_pairs={{0,4},{2,6},{4,0},{6,2},{1,5},{3,7},{5,1},{7,3},{8,12},{10,14},{12... | collective-permute-start | bytes 3145736 | tf_op jit(solution)/shard_map/ppermute | solution.py:419
  202.3 25.6 %collective-permute-start.18 = (bf16[4,2,256,256]{3,2,1,0:T(8,128)(2,1)S(1)}, bf16[4,2,256,256]{3,2,1,0:T(8,128)(2,1)S(1)}, u32[]{:S(2)}, u32[]{:S(2)}) collective-permute-start(bf16[4,2,256,256]{3,2,1,0:T(8,128)(2,1)S(1)} %get-tuple-element.165), channel_id=1, source_target_pairs={{0,6},{2,0},{4,2},{6,4},{1,7},{3,1},{5,3},{7,5},{8,14},{10,8},{12,... | collective-permute-start | bytes 3145736 | tf_op jit(solution)/shard_map/ppermute | solution.py:419
  225.9 27.1 %collective-permute-start.10 = (bf16[4,2,256,256]{3,2,1,0:T(8,128)(2,1)}, bf16[4,2,256,256]{3,2,1,0:T(8,128)(2,1)S(1)}, u32[]{:S(2)}, u32[]{:S(2)}) collective-permute-start(bf16[4,2,256,256]{3,2,1,0:T(8,128)(2,1)} %get-tuple-element.167), channel_id=1, source_target_pairs={{0,16},{16,32},{32,48},{48,0},{1,17},{17,33},{33,49},{49,1},{2,18}... | collective-permute-start | bytes 3145736 | tf_op jit(solution)/shard_map/ppermute | solution.py:419
  227.9 48.0 %collective-permute-start.11 = (bf16[4,2,256,256]{3,2,1,0:T(8,128)(2,1)}, bf16[4,2,256,256]{3,2,1,0:T(8,128)(2,1)}, u32[]{:S(2)}, u32[]{:S(2)}) collective-permute-start(bf16[4,2,256,256]{3,2,1,0:T(8,128)(2,1)} %get-tuple-element.167), channel_id=1, source_target_pairs={{0,32},{16,48},{32,0},{48,16},{1,33},{17,49},{33,1},{49,17},{2,34}... | collective-permute-start | bytes 3145736 | tf_op jit(solution)/shard_map/ppermute | solution.py:419
  254.1 22.7 %collective-permute-start.12 = (bf16[4,2,256,256]{3,2,1,0:T(8,128)(2,1)}, bf16[4,2,256,256]{3,2,1,0:T(8,128)(2,1)}, u32[]{:S(2)}, u32[]{:S(2)}) collective-permute-start(bf16[4,2,256,256]{3,2,1,0:T(8,128)(2,1)} %get-tuple-element.167), channel_id=1, source_target_pairs={{0,48},{16,0},{32,16},{48,32},{1,49},{17,1},{33,17},{49,33},{2,50}... | collective-permute-start | bytes 3145736 | tf_op jit(solution)/shard_map/ppermute | solution.py:419
  288.4 47.8 %collective-permute-start.76 = (bf16[128,2048]{1,0:T(8,128)(2,1)S(1)}, bf16[128,2048]{1,0:T(8,128)(2,1)S(1)}, u32[]{:S(2)}, u32[]{:S(2)}) collective-permute-start(bf16[128,2048]{1,0:T(8,128)(2,1)S(1)} %get-tuple-element.162), channel_id=1, source_target_pairs={{0,64},{64,0},{1,65},{65,1},{2,66},{66,2},{3,67},{67,3},{4,68},{68... | collective-permute-start | bytes 1572872 | tf_op jit(solution)/shard_map/ppermute | solution.py:414
  295.4 36.6 %collective-permute-start.23 = (bf16[2,2,128,128]{3,2,1,0:T(8,128)(2,1)S(1)}, bf16[2,2,128,128]{3,2,1,0:T(8,128)(2,1)S(1)}, u32[]{:S(2)}, u32[]{:S(2)}) collective-permute-start(bf16[2,2,128,128]{3,2,1,0:T(8,128)(2,1)S(1)} %copy-done.66), channel_id=1, source_target_pairs={{0,32},{16,48},{32,0},{48,16},{1,33},{17,49},{33,1},{49,17},{2,34}... | collective-permute-start | bytes 393224 | tf_op jit(solution)/shard_map/ppermute | solution.py:419
  295.9 39.7 %collective-permute-start.24 = (bf16[2,2,128,128]{3,2,1,0:T(8,128)(2,1)S(1)}, bf16[2,2,128,128]{3,2,1,0:T(8,128)(2,1)S(1)}, u32[]{:S(2)}, u32[]{:S(2)}) collective-permute-start(bf16[2,2,128,128]{3,2,1,0:T(8,128)(2,1)S(1)} %copy-done.66), channel_id=1, source_target_pairs={{0,48},{16,0},{32,16},{48,32},{1,49},{17,1},{33,17},{49,33},{2,50}... | collective-permute-start | bytes 393224 | tf_op jit(solution)/shard_map/ppermute | solution.py:419
  295.9 146.8 %collective-permute-start.20 = (bf16[4,4,2,256,256]{4,3,2,1,0:T(8,128)(2,1)}, bf16[4,4,2,256,256]{4,3,2,1,0:T(8,128)(2,1)}, u32[]{:S(2)}, u32[]{:S(2)}) collective-permute-start(bf16[4,4,2,256,256]{4,3,2,1,0:T(8,128)(2,1)} %pad_maximum_fusion.1.b_own), channel_id=1, source_target_pairs={{0,1},{1,0},{2,3},{3,2},{4,5},{5,4},{6,7},{7,6},{8,9},{9,8},{10,11... | collective-permute-start | bytes 12582920 | tf_op jit(solution)/shard_map/ppermute | solution.py:414
  296.0 146.7 %collective-permute-start.19 = (bf16[4,4,2,256,256]{4,3,2,1,0:T(8,128)(2,1)}, bf16[4,4,2,256,256]{4,3,2,1,0:T(8,128)(2,1)}, u32[]{:S(2)}, u32[]{:S(2)}) collective-permute-start(bf16[4,4,2,256,256]{4,3,2,1,0:T(8,128)(2,1)} %pad_maximum_fusion.a_own), channel_id=1, source_target_pairs={{0,1},{1,0},{2,3},{3,2},{4,5},{5,4},{6,7},{7,6},{8,9},{9,8},{10,11... | collective-permute-start | bytes 12582920 | tf_op jit(solution)/shard_map/ppermute | solution.py:414
  (136 other events, 2601.4 us)

commit v4 on v2

v4 whole, which is shorter than its diff:
```python
import functools

import jax
import jax.numpy as jnp
import numpy as np
from jax import lax
from jax.experimental import pallas as pl
from jax.experimental.pallas import tpu as pltpu
from jax.sharding import Mesh
from jax.sharding import PartitionSpec as P

HEAD_SIZE = 128
GROUPS = 2
CAPACITY = 5
EXPERTS = 64
SLOTS = EXPERTS * CAPACITY
SEQ = ("zlo", "y")
CHIPS = ("zlo", "y", "zhi", "x")
PLANE = ("y", "zhi", "x")
BLOCK = 512
PIECES = 8
BATCH = PIECES * CAPACITY
HIDDEN_TILE = 256
NT = (((1,), (1,)), ((), ()))
TN = (((0,), (0,)), ((), ()))
F32 = jnp.float32
BF16 = jnp.bfloat16


def chunk_order():
    index = np.arange(PIECES * BATCH).reshape(PIECES, PIECES, CAPACITY)
    moved = index.transpose(1, 0, 2).reshape(-1)
    return jnp.asarray(np.eye(PIECES * BATCH, dtype=np.float32)[moved], BF16)


def reordered(order, rows):
    return jnp.dot(order, rows, preferred_element_type=F32)


def slot_rows(ids):
    tokens = ids.shape[0]
    lane = lax.broadcasted_iota(jnp.int32, (tokens, EXPERTS), 1)
    chosen = [ids[:, k : k + 1] for k in range(ids.shape[1])]
    hots = [jnp.where(lane == e, 1.0, 0.0) for e in chosen]
    before = jnp.where(
        lax.broadcasted_iota(jnp.int32, (tokens, tokens), 1)
        < lax.broadcasted_iota(jnp.int32, (tokens, tokens), 0),
        1.0,
        0.0,
    ).astype(BF16)
    earlier = jnp.dot(before, sum(hots).astype(BF16), preferred_element_type=F32)
    return [
        e * CAPACITY + jnp.sum(earlier * hot, axis=1, keepdims=True).astype(jnp.int32)
        for e, hot in zip(chosen, hots)
    ]


def pick_kernel(order, ids, hidden, grads, out, rows, row_grads):
    lane = lax.broadcasted_iota(jnp.int32, (ids.shape[0], SLOTS), 1)
    picking = sum(jnp.where(lane == row, 1.0, 0.0) for row in slot_rows(ids)).astype(BF16)
    for piece in range(PIECES):
        at = slice(piece * BLOCK, (piece + 1) * BLOCK)
        rows[:, at] = lax.dot_general(picking, hidden[:, at], TN, preferred_element_type=F32)
        row_grads[:, at] = lax.dot_general(picking, grads[:, at], TN, preferred_element_type=F32)
    for g in range(SLOTS // BATCH):
        slots = slice(g * BATCH, (g + 1) * BATCH)
        for side, source in enumerate((rows, row_grads)):
            pieces = [source[slots, p * BLOCK : (p + 1) * BLOCK] for p in range(PIECES)]
            sent = reordered(order[...], jnp.concatenate(pieces, axis=0).astype(BF16))
            out[g * PIECES * BATCH : (g + 1) * PIECES * BATCH, side * BLOCK : (side + 1) * BLOCK] = (
                sent.astype(BF16)
            )


def pick(ids, hidden, grads):
    width = hidden.shape[1]
    held = pl.BlockSpec(memory_space=pltpu.VMEM)
    return pl.pallas_call(
        pick_kernel,
        in_specs=[held] * 4,
        out_specs=held,
        out_shape=jax.ShapeDtypeStruct((EXPERTS * BATCH, 2 * BLOCK), BF16),
        scratch_shapes=[pltpu.VMEM((SLOTS, width), F32)] * 2,
        compiler_params=pltpu.CompilerParams(vmem_limit_bytes=48 * 1024 * 1024),
        name="pick",
    )(chunk_order(), ids, hidden, grads)


def mix_kernel(order, ids, probs, grads, came, out, rows):
    for g in range(SLOTS // BATCH):
        batch = came[g * PIECES * BATCH : (g + 1) * PIECES * BATCH]
        batch = reordered(order[...], batch)
        for p in range(PIECES):
            rows[g * BATCH : (g + 1) * BATCH, p * BLOCK : (p + 1) * BLOCK] = batch[
                p * BATCH : (p + 1) * BATCH
            ]
    lane = lax.broadcasted_iota(jnp.int32, (ids.shape[0], SLOTS), 1)
    mixing = sum(
        jnp.where(lane == row, probs[:, k : k + 1], 0.0) for k, row in enumerate(slot_rows(ids))
    )
    mixing_high = mixing.astype(BF16)
    mixing_low = (mixing - mixing_high.astype(F32)).astype(BF16)
    for p in range(PIECES):
        at = slice(p * BLOCK, (p + 1) * BLOCK)
        block = rows[:, at].astype(BF16)
        mixed = jnp.dot(mixing_high, block, preferred_element_type=F32)
        mixed += jnp.dot(mixing_low, block, preferred_element_type=F32)
        out[:, at] = (grads[:, at].astype(F32) + mixed).astype(BF16)


def mix(ids, probs, grads, came):
    held = pl.BlockSpec(memory_space=pltpu.VMEM)
    return pl.pallas_call(
        mix_kernel,
        in_specs=[held] * 5,
        out_specs=held,
        out_shape=jax.ShapeDtypeStruct(grads.shape, BF16),
        scratch_shapes=[pltpu.VMEM((SLOTS, grads.shape[1]), F32)],
        compiler_params=pltpu.CompilerParams(vmem_limit_bytes=48 * 1024 * 1024),
        name="mix",
    )(chunk_order(), ids, probs, grads, came)


def after_kernel(*refs):
    pass


def after(arrays, event):
    far = pl.BlockSpec(memory_space=pl.ANY)
    count = len(arrays)
    return pl.pallas_call(
        after_kernel,
        in_specs=[far] * (count + 1),
        out_specs=[far] * count,
        out_shape=[jax.ShapeDtypeStruct(a.shape, a.dtype) for a in arrays],
        input_output_aliases={i: i for i in range(count)},
        name="after",
    )(*arrays, event)


def expert_kernel(order, g0, u0, d0, g1, u1, d1, came, *refs):
    carried = (len(refs) - 9) // 2
    out = refs[carried]
    rows, grads, gate, up, down, d_gate, d_up, sems = refs[2 * carried + 1 :]
    halves, width, half = gate.shape
    tile = 512
    loads = []
    for h, (g, u, d) in enumerate(((g0, u0, d0), (g1, u1, d1))):
        for at in range(0, half, HIDDEN_TILE):
            part = slice(at, at + HIDDEN_TILE)
            copies = [
                pltpu.make_async_copy(g.at[0, :, part], gate.at[h, :, part], sems.at[len(loads), 0]),
                pltpu.make_async_copy(u.at[0, :, part], up.at[h, :, part], sems.at[len(loads), 1]),
                pltpu.make_async_copy(d.at[0, part, :], down.at[h, part, :], sems.at[len(loads), 2]),
            ]
            for copy in copies:
                copy.start()
            loads.append((h, part, copies))
    size = PIECES * BATCH
    for g in range(0, SLOTS // BATCH, 2):
        batches = [reordered(order[...], came[(g + i) * size : (g + i + 1) * size]) for i in range(2)]
        slots = slice(g * BATCH, (g + 2) * BATCH)
        for p in range(PIECES):
            pair = [batch[p * BATCH : (p + 1) * BATCH] for batch in batches]
            pair = jnp.concatenate(pair, axis=0).astype(BF16)
            rows[slots, p * BLOCK : (p + 1) * BLOCK] = pair[:, :BLOCK]
            grads[slots, p * BLOCK : (p + 1) * BLOCK] = pair[:, BLOCK:]
    for h, part, copies in loads:
        for copy in copies:
            copy.wait()
        pre_gate = jnp.dot(rows[...], gate[h, :, part], preferred_element_type=F32)
        pre_up = jnp.dot(rows[...], up[h, :, part], preferred_element_type=F32)
        upstream = lax.dot_general(grads[...], down[h, part, :], NT, preferred_element_type=F32)
        sig = jax.nn.sigmoid(pre_gate)
        d_gate[h, :, part] = (upstream * pre_up * sig * (1.0 + pre_gate * (1.0 - sig))).astype(BF16)
        d_up[h, :, part] = (upstream * pre_gate * sig).astype(BF16)

    @pl.loop(0, width // tile)
    def _(i):
        at = pl.ds(pl.multiple_of(i * tile, tile), tile)
        total = lax.dot_general(d_gate[0], gate[0, at, :], NT, preferred_element_type=F32)
        total += lax.dot_general(d_up[0], up[0, at, :], NT, preferred_element_type=F32)
        for h in range(1, halves):
            total += lax.dot_general(d_gate[h], gate[h, at, :], NT, preferred_element_type=F32)
            total += lax.dot_general(d_up[h], up[h, at, :], NT, preferred_element_type=F32)
        rows[:, at] = total.astype(BF16)

    for g in range(0, SLOTS // BATCH, 2):
        slots = slice(g * BATCH, (g + 2) * BATCH)
        pieces = [rows[slots, p * BLOCK : (p + 1) * BLOCK].astype(F32) for p in range(PIECES)]
        for i in range(2):
            batch = [piece[i * BATCH : (i + 1) * BATCH] for piece in pieces]
            batch = jnp.concatenate(batch, axis=0).astype(BF16)
            out[(g + i) * size : (g + i + 1) * size] = reordered(order[...], batch).astype(BF16)


def expert_back(came, own, other, carried):
    width, half = own[0].shape[1:]
    held = pl.BlockSpec(memory_space=pltpu.VMEM)
    far = pl.BlockSpec(memory_space=pl.ANY)
    count = len(carried)
    return pl.pallas_call(
        expert_kernel,
        in_specs=[held] + [far] * 6 + [held] + [far] * count,
        out_specs=[held] + [far] * count,
        out_shape=[jax.ShapeDtypeStruct((EXPERTS * BATCH, BLOCK), BF16)]
        + [jax.ShapeDtypeStruct(a.shape, a.dtype) for a in carried],
        input_output_aliases={8 + i: 1 + i for i in range(count)},
        scratch_shapes=[
            pltpu.VMEM((SLOTS, width), BF16),
            pltpu.VMEM((SLOTS, width), BF16),
            pltpu.VMEM((2, width, half), BF16),
            pltpu.VMEM((2, width, half), BF16),
            pltpu.VMEM((2, half, width), BF16),
            pltpu.VMEM((2, SLOTS, half), BF16),
            pltpu.VMEM((2, SLOTS, half), BF16),
            pltpu.SemaphoreType.DMA((2 * half // HIDDEN_TILE, 3)),
        ],
        compiler_params=pltpu.CompilerParams(vmem_limit_bytes=60 * 1024 * 1024),
        cost_estimate=pl.CostEstimate(
            flops=20 * SLOTS * width * half, bytes_accessed=12 * width * half, transcendentals=0
        ),
        name="expert_back",
    )(chunk_order(), *own, *other, came, *carried)


def stack_heads(block):
    heads = block.shape[1] // HEAD_SIZE
    return jnp.concatenate(
        [block[:, h * HEAD_SIZE : (h + 1) * HEAD_SIZE] for h in range(heads)], axis=0
    )


def softmax_kernel(first_row, query, key, probs):
    scale = HEAD_SIZE ** (-0.5)
    tokens = query.shape[0]
    scores = jnp.dot(stack_heads(query[...]), key[...], preferred_element_type=F32) * scale
    row = lax.broadcasted_iota(jnp.int32, scores.shape, 0) % tokens + first_row[0]
    col = lax.broadcasted_iota(jnp.int32, scores.shape, 1)
    scores = jnp.where(col <= row, scores, -1e30)
    weights = jnp.exp(scores - jnp.max(scores, axis=1, keepdims=True))
    probs[...] = (weights / jnp.sum(weights, axis=1, keepdims=True)).astype(BF16)


def softmax_probs(first_row, queries, key, block_heads):
    tokens, width = queries.shape
    length = key.shape[1]
    rows = block_heads * tokens
    steps = width // (block_heads * HEAD_SIZE)
    return pl.pallas_call(
        softmax_kernel,
        grid=(steps,),
        in_specs=[
            pl.BlockSpec(memory_space=pltpu.SMEM),
            pl.BlockSpec((tokens, block_heads * HEAD_SIZE), lambda i: (0, i)),
            pl.BlockSpec((HEAD_SIZE, length), lambda i: (0, 0)),
        ],
        out_specs=pl.BlockSpec((rows, length), lambda i: (i, 0)),
        out_shape=jax.ShapeDtypeStruct((steps * rows, length), BF16),
        compiler_params=pltpu.CompilerParams(vmem_limit_bytes=48 * 1024 * 1024),
        cost_estimate=pl.CostEstimate(
            flops=20 * steps * rows * length * HEAD_SIZE,
            bytes_accessed=2 * steps * rows * length,
            transcendentals=steps * rows * length,
        ),
        name="softmax_probs",
    )(first_row, queries, key)


def attention_kernel(last, core, resid, own, other, query, probs, key, value_t, *refs):
    if last:
        dkey_in, dvalue_in, dquery, dkv, dkey, dvalue = refs
    else:
        dquery, dkey, dvalue = refs
    step = pl.program_id(0)
    scale = HEAD_SIZE ** (-0.5)
    tokens = query.shape[0]
    pieces, depth, block_cols = own.shape[1:]

    @pl.when(step == 0)
    def _():
        if last:
            dkey[...] = dkey_in[...]
            dvalue[...] = dvalue_in[...]
        else:
            dkey[...] = jnp.zeros_like(dkey)
            dvalue[...] = jnp.zeros_like(dvalue)

    ctx = jnp.zeros((tokens, block_cols), F32)
    for side, shard in ((core[0], own), (1 - core[0], other)):
        for piece in range(pieces):
            at = pl.ds(pl.multiple_of((2 * piece + side) * depth, depth), depth)
            ctx += jnp.dot(resid[:, at], shard[0, piece], preferred_element_type=F32)
    ctx = stack_heads(ctx.astype(BF16))
    query_rows = stack_heads(query[...])
    low = probs[...]
    weights = low.astype(F32)
    dprobs = jnp.dot(ctx, value_t[...], preferred_element_type=F32)
    delta = jnp.sum(weights * dprobs, axis=1, keepdims=True)
    dscores = (weights * (dprobs - delta)).astype(BF16)
    dq = jnp.dot(dscores, key[...], preferred_element_type=F32) * scale
    for h in range(query.shape[1] // HEAD_SIZE):
        dquery[:, h * HEAD_SIZE : (h + 1) * HEAD_SIZE] = dq[h * tokens : (h + 1) * tokens].astype(
            BF16
        )
    dkey[...] += lax.dot_general(query_rows, dscores, TN, preferred_element_type=F32)
    dvalue[...] += lax.dot_general(ctx, low, TN, preferred_element_type=F32)

    if last:

        @pl.when(step == pl.num_programs(0) - 1)
        def _():
            dkv[:, :HEAD_SIZE] = jnp.transpose(dkey[...] * scale).astype(BF16)
            dkv[:, HEAD_SIZE:] = jnp.transpose(dvalue[...]).astype(BF16)


def attention_back(core, resid, own, other, queries, probs, key, value_t, carried):
    tokens, width = resid.shape
    steps, pieces, depth, block_cols = own.shape
    length = key.shape[0]
    rows = tokens * block_cols // HEAD_SIZE
    last = carried is not None

    def whole(*shape):
        return pl.BlockSpec(shape, lambda i: (0,) * len(shape))

    shard = pl.BlockSpec((1, pieces, depth, block_cols), lambda i: (i, 0, 0, 0))
    block = pl.BlockSpec((tokens, block_cols), lambda i: (0, i))
    in_specs = [
        pl.BlockSpec(memory_space=pltpu.SMEM),
        whole(tokens, width),
        shard,
        shard,
        block,
        pl.BlockSpec((rows, length), lambda i: (i, 0)),
        whole(length, HEAD_SIZE),
        whole(HEAD_SIZE, length),
    ]
    sums = jax.ShapeDtypeStruct((HEAD_SIZE, length), F32)
    dquery = jax.ShapeDtypeStruct((tokens, steps * block_cols), BF16)
    if last:
        in_specs += [whole(HEAD_SIZE, length)] * 2
        out_specs = [block, whole(length, 2 * HEAD_SIZE)]
        out_shape = [dquery, jax.ShapeDtypeStruct((length, 2 * HEAD_SIZE), BF16)]
        scratch = [pltpu.VMEM((HEAD_SIZE, length), F32)] * 2
    else:
        out_specs = [block] + [whole(HEAD_SIZE, length)] * 2
        out_shape = [dquery, sums, sums]
        scratch = []
    return pl.pallas_call(
        functools.partial(attention_kernel, last),
        grid=(steps,),
        in_specs=in_specs,
        out_specs=out_specs,
        scratch_shapes=scratch,
        out_shape=out_shape,
        compiler_params=pltpu.CompilerParams(vmem_limit_bytes=56 * 1024 * 1024),
        cost_estimate=pl.CostEstimate(
            flops=2 * steps * rows * (5 * length * HEAD_SIZE + width * HEAD_SIZE),
            bytes_accessed=steps * (2 * width * block_cols + 2 * rows * length),
            transcendentals=0,
        ),
        name="attention_back",
    )(core, resid, own, other, queries, probs, key, value_t, *(carried or ()))


def swapped(block, axis):
    return lax.ppermute(block, axis, [(0, 1), (1, 0)])


def to_chips(chunks):
    sent = chunks.reshape(EXPERTS, BATCH, -1)
    return lax.all_to_all(sent, CHIPS, split_axis=0, concat_axis=0, tiled=True).reshape(
        chunks.shape
    )


def body(
    hidden_in,
    out_grad,
    queries,
    keys,
    values,
    out_proj,
    expert_ids,
    gate_probs,
    w_gate,
    w_up,
    w_down,
):
    tokens, width = hidden_in.shape[1:]
    zlo = lax.axis_index("zlo")
    y_at = lax.axis_index("y")
    y_count = lax.axis_size("y")
    core = lax.axis_index("core").astype(jnp.int32).reshape(1)
    own = (w_gate, w_up, w_down)
    other = tuple(swapped(w, "core") for w in own)

    came = to_chips(pick(expert_ids[0], hidden_in[0], out_grad[0]))

    kv = lax.all_gather(jnp.concatenate([keys[0], values[0]], axis=1), SEQ, axis=0, tiled=True)
    key = lax.dynamic_slice_in_dim(kv, zlo * HEAD_SIZE, HEAD_SIZE, 1)
    value = lax.dynamic_slice_in_dim(kv, (GROUPS + zlo) * HEAD_SIZE, HEAD_SIZE, 1)
    key_t, value_t = key.T, value.T
    group_width = width // GROUPS
    own_query = lax.dynamic_slice_in_dim(queries[0], zlo * group_width, group_width, 1)
    near_query = swapped(
        lax.dynamic_slice_in_dim(queries[0], (1 - zlo) * group_width, group_width, 1), "zlo"
    )
    block_heads = out_proj.shape[0] // HEAD_SIZE
    own_row = ((zlo * y_count + y_at) * tokens).astype(jnp.int32).reshape(1)
    near_row = (((1 - zlo) * y_count + y_at) * tokens).astype(jnp.int32).reshape(1)
    own_probs = softmax_probs(own_row, own_query, key_t, block_heads)
    near_probs = softmax_probs(near_row, near_query, key_t, block_heads)

    back, own_probs, near_probs = expert_back(came, own, other, (own_probs, near_probs))

    proj_own = lax.all_gather(out_proj.T, PLANE, axis=0, tiled=False)
    proj_own = proj_own.reshape(y_count, -1, *proj_own.shape[1:])
    (proj_own,) = after((proj_own,), back)
    proj_other = swapped(proj_own, "core")
    result = to_chips(back)
    resid = mix(expert_ids[0], gate_probs[0], out_grad[0], result)
    near_resid = swapped(resid, "zlo")

    dquery, dkey, dvalue = attention_back(
        core, resid, proj_own, proj_other, own_query, own_probs, key, value_t, None
    )
    near_dquery, dkv = attention_back(
        core,
        near_resid,
        proj_own,
        proj_other,
        near_query,
        near_probs,
        key,
        value_t,
        (dkey, dvalue),
    )
    far_dquery = swapped(near_dquery, "zlo")
    dquery = jnp.where(
        zlo == 0,
        jnp.concatenate([dquery, far_dquery], axis=1),
        jnp.concatenate([far_dquery, dquery], axis=1),
    )
    sent = lax.all_to_all(
        dkv.reshape(-1, tokens, 2 * HEAD_SIZE), SEQ, split_axis=0, concat_axis=0, tiled=True
    )
    sent = sent.reshape(GROUPS, y_count, tokens, 2 * HEAD_SIZE)
    sums = jnp.sum(sent.astype(F32), axis=1).astype(BF16)
    dkey = jnp.concatenate([sums[g, :, :HEAD_SIZE] for g in range(GROUPS)], axis=1)
    dvalue = jnp.concatenate([sums[g, :, HEAD_SIZE:] for g in range(GROUPS)], axis=1)
    return resid[None], dquery[None], dkey[None], dvalue[None]


def solution(mesh):
    fine = Mesh(mesh.devices.reshape(2, 4, 2, 4, 2), ("zlo", "y", "zhi", "x", "core"))
    dp = ("zhi", "x", "core")
    token_spec = P(dp, SEQ, None)
    weight_spec = P((*SEQ, *dp), None, None)
    return jax.shard_map(
        body,
        mesh=fine,
        in_specs=(token_spec,) * 5
        + (P(SEQ, dp), token_spec, token_spec, weight_spec, weight_spec, weight_spec),
        out_specs=(token_spec,) * 4,
        check_vma=False,
    )
```

time: 447 us -> 372 us (0.83)
  starting transfers between devices: 84.4 us -> 26.5 us
  waiting for transfers between devices: 206 us -> 218 us
  other arithmetic: 14.3 us -> 2.62 us
  local copies, waits for them, and re-layouts: 37 us -> 27 us
  matrix products: 7.51 us -> 0 us
    ppermute x14 -> x0, waiting for transfers between devices: 96.8 us -> none  [shifted(): lax.ppermute(block, axis, [(i, (i + by) % count) for i in range(count)])]
    all_gather x0 -> x1, waiting for transfers between devices: none -> 91.5 us  [body(): proj_own = lax.all_gather(out_proj.T, PLANE, axis=0, tiled=False)]
    ppermute x14 -> x0, starting transfers between devices: 32.3 us -> none  [shifted(): lax.ppermute(block, axis, [(i, (i + by) % count) for i in range(count)])]
    reshape x6 -> x0, local copies, waits for them, and re-layouts: 26.8 us -> none  [the longest x3 14.3 us: to_chips(): lax.all_to_all(sent, CHIPS, split_axis=0, concat_axis=0, tiled=True)]
    all_to_all x3 -> x2, starting transfers between devices: 40.6 us -> 17.8 us  [to_chips(): lax.all_to_all(sent, CHIPS, split_axis=0, concat_axis=0, tiled=True)]
    all_gather x1, waiting for transfers between devices: 47.5 us -> 64.1 us  [body(): lax.all_gather(jnp.concatenate([keys[0], values[0]], axis=1), SEQ, axis=0...]
    ppermute x8 -> x7, waiting for transfers between devices: 4.64 us -> 19.2 us  [swapped(): return lax.ppermute(block, axis, [(0, 1), (1, 0)])]
    all_to_all x3 -> x2, waiting for transfers between devices: 50.3 us -> 35.8 us  [to_chips(): lax.all_to_all(sent, CHIPS, split_axis=0, concat_axis=0, tiled=True)]
  transfers between devices with their start and end apart: 27 -> 12, of which waited for: 10 -> 7; matrix products, arithmetic and copies ran while one was open for 12% -> 1% of each run, Pallas kernels for 15% -> 18%
where the time goes in v4:
time: 372 us; the launch traced here: 370 us
  waiting for transfers between devices  218 us (59%)
  Pallas kernels  81.6 us (22%)
  local copies, waits for them, and re-layouts  27 us (7%)
  starting transfers between devices  26.5 us (7%)
  between operations  14.2 us (4%)
    all_gather x1, waiting for transfers between devices, body(): proj_own = lax.all_gather(out_proj.T, PLANE, axis=0, tiled=False)  91.5 us
    all_gather x1, waiting for transfers between devices, body(): lax.all_gather(jnp.concatenate([keys[0], values[0]], axis=1), SEQ, axis=0...  64.1 us
    pallas_call x1, Pallas kernels, expert_back(): pl.pallas_call(expert_kernel, in_specs=[held] + [far] * 6 + [held] + [far...  36.1 us
    all_to_all x2, waiting for transfers between devices, to_chips(): lax.all_to_all(sent, CHIPS, split_axis=0, concat_axis=0, tiled=True)  35.8 us
    pallas_call x2, Pallas kernels, attention_back(): pl.pallas_call(functools.partial(attention_kernel, last), grid=(steps,),...  26.5 us
    ppermute x7, waiting for transfers between devices, swapped(): return lax.ppermute(block, axis, [(0, 1), (1, 0)])  19.2 us
    all_to_all x2, starting transfers between devices, to_chips(): lax.all_to_all(sent, CHIPS, split_axis=0, concat_axis=0, tiled=True)  17.8 us
    unnamed x30, local copies, waits for them, and re-layouts  12.4 us
  transfers between devices with their start and end apart: 12, of which 7 were waited for; matrix products, arithmetic and copies ran while one was open for 1% of the time, Pallas kernels for 18%

profile of v4, /device:TPU:0, one launch (start us, length us, event | category | flops | bytes accessed | tf_op | source)
XLA Modules:
  0.0 369.8 jit_solution(12861293083696959066)
XLA Ops:
  13.3 1.2 copy-done.5
  15.4 7.1 %pick.1 = bf16[2560,1024]{1,0:T(8,128)(2,1)} custom-call(bf16[320,320]{1,0:T(8,128)(2,1)S(1)} %copy-done.6, s32[128,2]{1,0:T(8,128)S(1)} %bitcast.46, bf16[128,4096]{1,0:T(8,128)(2,1)S(1)} %bitcast.45, bf16[128,4096]{1,0:T(8,128)(2,1)S(1)} %bitcast.41), custom_call_target="tpu_custom_call" | custom-call | tf_op jit(solution)/shard_map/pick/pallas_call | solution.py:78
  22.5 11.9 %all-to-all-start = ((bf16[64,40,1024]{2,1,0:T(8,128)(2,1)}), bf16[64,40,1024]{2,1,0:T(8,128)(2,1)}, u32[]{:S(2)}, u32[]{:S(2)}) async-start(bf16[64,40,1024]{2,1,0:T(8,128)(2,1)} %bitcast.50), calls=%async_computation | async-start | bytes 10485760 | tf_op jit(solution)/shard_map/all_to_all | solution.py:373
  34.5 1.7 collective-permute-start.3
  36.2 64.1 %all-gather.4.cloned.1.call-done = bf16[1024,512]{0,1:T(8,128)(2,1)} async-done(((bf16[128,512]{0,1:T(8,128)(2,1)}), bf16[1024,512]{0,1:T(8,128)(2,1)}) %all-gather.4.cloned.1.call-update) | async-done | bytes 1048592 | tf_op jit(solution)/shard_map/all_gather | solution.py:401
  100.3 1.8 dynamic-slice_bitcast_fusion.2
  102.0 3.9 %softmax_probs.2.refs_0_ = bf16[2048,1024]{1,0:T(8,128)(2,1)S(1)} custom-call(s32[1]{0:T(128)} %bitcast.6.first_row, bf16[128,2048]{1,0:T(8,128)(2,1)S(1)} %get-tuple-element.23.query, bf16[128,1024]{1,0:T(8,128)(2,1)S(1)} %bitcast.43), custom_call_target="tpu_custom_call" | custom-call | flops 5368709120 | bytes 4194304 | tf_op jit(solution)/shard_map/softmax_probs/pallas_call | solution.py:250
  106.0 2.0 copy-done
  108.4 4.1 %softmax_probs.3.refs_1_ = bf16[2048,1024]{1,0:T(8,128)(2,1)S(1)} custom-call(s32[1]{0:T(128)} %bitcast.11.first_row, bf16[128,2048]{1,0:T(8,128)(2,1)S(1)} %collective-permute-done.3.query, bf16[128,1024]{1,0:T(8,128)(2,1)S(1)} %bitcast.44), custom_call_target="tpu_custom_call" | custom-call | flops 5368709120 | bytes 4194304 | tf_op jit(solution)/shard_map/softmax_probs/pallas_call | solution.py:250
  112.5 1.9 copy-done.1
  114.5 36.1 %expert_back.1 = (bf16[2560,512]{1,0:T(8,128)(2,1)}, bf16[2048,1024]{1,0:T(8,128)(2,1)}, bf16[2048,1024]{1,0:T(8,128)(2,1)}) custom-call(bf16[320,320]{1,0:T(8,128)(2,1)} %constant.37.clone.order, bf16[1,4096,768]{2,1,0:T(8,128)(2,1)} %g0.1, bf16[1,4096,768]{2,1,0:T(8,128)(2,1)} %u0.1, ...), custom_call_target="tpu_custom_call", output_to_operand_aliasing={{1}: (8, {}), {2}: (9, {})} | custom-call | flops 20132659200 | bytes 37748736 | tf_op jit(solution)/shard_map/expert_back/pallas_call | solution.py:202
  150.7 91.5 %all-gather.6.cloned.1.call-done = bf16[8192,512]{0,1:T(8,128)(2,1)} async-done(((bf16[256,512]{0,1:T(8,128)(2,1)}), bf16[8192,512]{0,1:T(8,128)(2,1)}) %all-gather.6.cloned.1.call-update) | async-done | bytes 8388624 | tf_op jit(solution)/shard_map/all_gather | solution.py:418
  242.1 11.9 %copy.25 = bf16[8192,512]{1,0:T(8,128)(2,1)} copy(bf16[8192,512]{0,1:T(8,128)(2,1)} %all-gather.6.cloned.1.call-done) | data formatting | bytes 16777216 | tf_op jit(solution)/shard_map/all_gather | solution.py:418
  254.1 6.0 %all-to-all-start.1 = ((bf16[64,40,512]{2,1,0:T(8,128)(2,1)}), bf16[64,40,512]{2,1,0:T(8,128)(2,1)S(1)}, u32[]{:S(2)}, u32[]{:S(2)}) async-start(bf16[64,40,512]{2,1,0:T(8,128)(2,1)} %bitcast.51), calls=%async_computation.1 | async-start | bytes 5242880 | tf_op jit(solution)/shard_map/all_to_all | solution.py:373
  260.2 35.8 %all-to-all-done.1 = bf16[64,40,512]{2,1,0:T(8,128)(2,1)S(1)} async-done(((bf16[64,40,512]{2,1,0:T(8,128)(2,1)}), bf16[64,40,512]{2,1,0:T(8,128)(2,1)S(1)}, u32[]{:S(2)}, u32[]{:S(2)}) %all-to-all-start.1) | async-done | bytes 2621472 | tf_op jit(solution)/shard_map/all_to_all | solution.py:373
  296.0 1.2 copy-done.3
  297.2 3.9 %mix.1.resid = bf16[128,4096]{1,0:T(8,128)(2,1)} custom-call(bf16[320,320]{1,0:T(8,128)(2,1)S(1)} %copy-done.7, s32[128,2]{1,0:T(8,128)S(1)} %bitcast.47, f32[128,2]{1,0:T(8,128)S(1)} %bitcast.48, bf16[128,4096]{1,0:T(8,128)(2,1)S(1)} %bitcast.42, bf16[2560,512]{1,0:T(8,128)(2,1)S(1)} %bitcast.40), custom_call_target="tpu_custom_call" | custom-call | tf_op jit(solution)/shard_map/mix/pallas_call | solution.py:113
  302.4 12.9 %attention_back.2 = (bf16[128,2048]{1,0:T(8,128)(2,1)}, f32[128,1024]{1,0:T(8,128)}, f32[128,1024]{1,0:T(8,128)}) custom-call(s32[1]{0:T(128)} %bitcast.16.core, bf16[128,4096]{1,0:T(8,128)(2,1)} %mix.1.resid, bf16[4,8,256,512]{3,2,1,0:T(8,128)(2,1)} %after.1.own, bf16[4,8,256,512]{3,2,1,0:T(8,128)(2,1)} %collective-permute-done.4.other, ...), custom_call_target="tpu_custom_call" | custom-call | flops 4831838208 | bytes 20971520 | tf_op jit(solution)/shard_map/attention_back/pallas_call | solution.py:350
  315.2 10.4 %collective-permute-done.5.resid = bf16[128,4096]{1,0:T(8,128)(2,1)S(1)} collective-permute-done((bf16[128,4096]{1,0:T(8,128)(2,1)}, bf16[128,4096]{1,0:T(8,128)(2,1)S(1)}, u32[]{:S(2)}, u32[]{:S(2)}) %collective-permute-start.5) | collective-permute-done | bytes 1048608 | tf_op jit(solution)/shard_map/ppermute | solution.py:368
  326.6 13.6 %attention_back.3 = (bf16[128,2048]{1,0:T(8,128)(2,1)}, bf16[1024,256]{1,0:T(8,128)(2,1)}) custom-call(s32[1]{0:T(128)} %bitcast.16.core, bf16[128,4096]{1,0:T(8,128)(2,1)} %copy-done.10, bf16[4,8,256,512]{3,2,1,0:T(8,128)(2,1)} %after.1.own, bf16[4,8,256,512]{3,2,1,0:T(8,128)(2,1)} %collective-permute-done.4.other, bf16[128,2048]{1,0:T(8,128)(2,1)} %copy-done.8, ...), custom_call_target="tpu_custom_call" | custom-call | flops 4831838208 | bytes 20971520 | tf_op jit(solution)/shard_map/attention_back/pallas_call | solution.py:350
  340.2 3.8 %all-to-all-start.2 = ((bf16[8,128,256]{2,1,0:T(8,128)(2,1)}), bf16[8,128,256]{2,1,0:T(8,128)(2,1)S(1)}, u32[]{:S(2)}, u32[]{:S(2)}) async-start(bf16[8,128,256]{2,1,0:T(8,128)(2,1)} %bitcast.55), calls=%async_computation.2 | async-start | bytes 1048576 | tf_op jit(solution)/shard_map/all_to_all | solution.py:446
  344.0 2.0 collective-permute-start.6
  346.0 6.7 %all-to-all-done.2 = bf16[8,128,256]{2,1,0:T(8,128)(2,1)S(1)} async-done(((bf16[8,128,256]{2,1,0:T(8,128)(2,1)}), bf16[8,128,256]{2,1,0:T(8,128)(2,1)S(1)}, u32[]{:S(2)}, u32[]{:S(2)}) %all-to-all-start.2) | async-done | bytes 524320 | tf_op jit(solution)/shard_map/all_to_all | solution.py:446
  353.5 8.3 %collective-permute-done.6 = bf16[128,2048]{1,0:T(8,128)(2,1)S(1)} collective-permute-done((bf16[128,2048]{1,0:T(8,128)(2,1)}, bf16[128,2048]{1,0:T(8,128)(2,1)S(1)}, u32[]{:S(2)}, u32[]{:S(2)}) %collective-permute-start.6) | collective-permute-done | bytes 524320 | tf_op jit(solution)/shard_map/ppermute | solution.py:368
  (49 shorter events, 11.9 us)
Async XLA Ops:
  7.2 93.1 %all-gather.4.cloned.1.call-start = ((), (), s32[]{:S(2)}) async-start(), calls=%async_computation.3 | async-start | bytes 1179648 | tf_op jit(solution)/shard_map/all_gather | solution.py:401
  9.8 232.3 %all-gather.6.cloned.1.call-start = ((), (), s32[]{:S(2)}) async-start(), calls=%async_computation.4 | async-start | bytes 8650752 | tf_op jit(solution)/shard_map/all_gather | solution.py:418
  10.6 103.9 %collective-permute-start = (bf16[1,4096,768]{2,1,0:T(8,128)(2,1)}, bf16[1,4096,768]{2,1,0:T(8,128)(2,1)}, u32[]{:S(2)}, u32[]{:S(2)}) collective-permute-start(bf16[1,4096,768]{2,1,0:T(8,128)(2,1)} %g0.1), channel_id=1, source_target_pairs={{0,1},{1,0},{2,3},{3,2},{4,5},{5,4},{6,7},{7,6},{8,9},{9,8},{10,11... | collective-permute-start | bytes 18874376 | tf_op jit(solution)/shard_map/ppermute | solution.py:368
  10.7 103.8 %collective-permute-start.1 = (bf16[1,4096,768]{2,1,0:T(8,128)(2,1)}, bf16[1,4096,768]{2,1,0:T(8,128)(2,1)}, u32[]{:S(2)}, u32[]{:S(2)}) collective-permute-start(bf16[1,4096,768]{2,1,0:T(8,128)(2,1)} %u0.1), channel_id=1, source_target_pairs={{0,1},{1,0},{2,3},{3,2},{4,5},{5,4},{6,7},{7,6},{8,9},{9,8},{10,11... | collective-permute-start | bytes 18874376 | tf_op jit(solution)/shard_map/ppermute | solution.py:368
  11.2 103.3 %collective-permute-start.2 = (bf16[1,768,4096]{2,1,0:T(8,128)(2,1)}, bf16[1,768,4096]{2,1,0:T(8,128)(2,1)}, u32[]{:S(2)}, u32[]{:S(2)}) collective-permute-start(bf16[1,768,4096]{2,1,0:T(8,128)(2,1)} %d0.1), channel_id=1, source_target_pairs={{0,1},{1,0},{2,3},{3,2},{4,5},{5,4},{6,7},{7,6},{8,9},{9,8},{10,11... | collective-permute-start | bytes 18874376 | tf_op jit(solution)/shard_map/ppermute | solution.py:368
  12.0 1.2 copy-start.2
  13.3 1.2 copy-start.5
  22.5 11.9 %copy-start.9 = (bf16[1,128,4096]{2,1,0:T(8,128)(2,1)S(1)}, bf16[1,128,4096]{2,1,0:T(8,128)(2,1)}, u32[]{:S(2)}) copy-start(bf16[1,128,4096]{2,1,0:T(8,128)(2,1)} %param.16) | copy-start | bytes 3145732
  22.5 92.0 %all-to-all-start = ((bf16[64,40,1024]{2,1,0:T(8,128)(2,1)}), bf16[64,40,1024]{2,1,0:T(8,128)(2,1)}, u32[]{:S(2)}, u32[]{:S(2)}) async-start(bf16[64,40,1024]{2,1,0:T(8,128)(2,1)} %bitcast.50), calls=%async_computation | async-start | bytes 10485760 | tf_op jit(solution)/shard_map/all_to_all | solution.py:373
  34.5 71.4 %copy-start.4 = (bf16[128,2048]{1,0:T(8,128)(2,1)}, bf16[128,2048]{1,0:T(8,128)(2,1)S(1)}, u32[]{:S(2)}) copy-start(bf16[128,2048]{1,0:T(8,128)(2,1)S(1)} %get-tuple-element.23.query) | copy-start | bytes 1572868
  34.5 73.9 %collective-permute-start.3 = (bf16[128,2048]{1,0:T(8,128)(2,1)S(1)}, bf16[128,2048]{1,0:T(8,128)(2,1)S(1)}, u32[]{:S(2)}, u32[]{:S(2)}) collective-permute-start(bf16[128,2048]{1,0:T(8,128)(2,1)S(1)} %get-tuple-element.22), channel_id=1, source_target_pairs={{0,64},{64,0},{1,65},{65,1},{2,66},{66,2},{3,67},{67,3},{4,68},{68... | collective-permute-start | bytes 1572872 | tf_op jit(solution)/shard_map/ppermute | solution.py:368
  105.9 2.0 copy-start
  108.4 4.1 %copy-start.8 = (bf16[128,2048]{1,0:T(8,128)(2,1)}, bf16[128,2048]{1,0:T(8,128)(2,1)S(1)}, u32[]{:S(2)}) copy-start(bf16[128,2048]{1,0:T(8,128)(2,1)S(1)} %collective-permute-done.3.query) | copy-start | bytes 1572868
  112.5 2.0 copy-start.1
  254.1 6.0 %copy-start.12 = (f32[1,128,2]{1,2,0:T(2,128)S(1)}, f32[1,128,2]{1,2,0:T(2,128)}, u32[]{:S(2)}) copy-start(f32[1,128,2]{1,2,0:T(2,128)} %param.21) | copy-start | bytes 3076
  254.1 42.0 %copy-start.7 = (bf16[320,320]{1,0:T(8,128)(2,1)S(1)}, bf16[320,320]{1,0:T(8,128)(2,1)}, u32[]{:S(2)}) copy-start(bf16[320,320]{1,0:T(8,128)(2,1)} %constant.37.clone.order) | copy-start | bytes 614404
  254.1 48.3 %collective-permute-start.4 = (bf16[4,8,256,512]{3,2,1,0:T(8,128)(2,1)}, bf16[4,8,256,512]{3,2,1,0:T(8,128)(2,1)}, u32[]{:S(2)}, u32[]{:S(2)}) collective-permute-start(bf16[4,8,256,512]{3,2,1,0:T(8,128)(2,1)} %after.1.own), channel_id=1, source_target_pairs={{0,1},{1,0},{2,3},{3,2},{4,5},{5,4},{6,7},{7,6},{8,9},{9,8},{10,11... | collective-permute-start | bytes 25165832 | tf_op jit(solution)/shard_map/ppermute | solution.py:368
  254.1 41.9 %all-to-all-start.1 = ((bf16[64,40,512]{2,1,0:T(8,128)(2,1)}), bf16[64,40,512]{2,1,0:T(8,128)(2,1)S(1)}, u32[]{:S(2)}, u32[]{:S(2)}) async-start(bf16[64,40,512]{2,1,0:T(8,128)(2,1)} %bitcast.51), calls=%async_computation.1 | async-start | bytes 5242880 | tf_op jit(solution)/shard_map/all_to_all | solution.py:373
  296.0 1.2 copy-start.3
  301.1 24.5 %collective-permute-start.5 = (bf16[128,4096]{1,0:T(8,128)(2,1)}, bf16[128,4096]{1,0:T(8,128)(2,1)S(1)}, u32[]{:S(2)}, u32[]{:S(2)}) collective-permute-start(bf16[128,4096]{1,0:T(8,128)(2,1)} %mix.1.resid), channel_id=1, source_target_pairs={{0,64},{64,0},{1,65},{65,1},{2,66},{66,2},{3,67},{67,3},{4,68},{68... | collective-permute-start | bytes 3145736 | tf_op jit(solution)/shard_map/ppermute | solution.py:368
  325.6 1.0 copy-start.10
  326.6 35.2 %copy-start.11 = (bf16[128,2048]{1,0:T(8,128)(2,1)S(1)}, bf16[128,2048]{1,0:T(8,128)(2,1)}, u32[]{:S(2)}) copy-start(bf16[128,2048]{1,0:T(8,128)(2,1)} %get-tuple-element.14) | copy-start | bytes 1572868
  340.2 12.5 %all-to-all-start.2 = ((bf16[8,128,256]{2,1,0:T(8,128)(2,1)}), bf16[8,128,256]{2,1,0:T(8,128)(2,1)S(1)}, u32[]{:S(2)}, u32[]{:S(2)}) async-start(bf16[8,128,256]{2,1,0:T(8,128)(2,1)} %bitcast.55), calls=%async_computation.2 | async-start | bytes 1048576 | tf_op jit(solution)/shard_map/all_to_all | solution.py:446
  344.0 17.8 %collective-permute-start.6 = (bf16[128,2048]{1,0:T(8,128)(2,1)}, bf16[128,2048]{1,0:T(8,128)(2,1)S(1)}, u32[]{:S(2)}, u32[]{:S(2)}) collective-permute-start(bf16[128,2048]{1,0:T(8,128)(2,1)} %get-tuple-element.18), channel_id=1, source_target_pairs={{0,64},{64,0},{1,65},{65,1},{2,66},{66,2},{3,67},{67,3},{4,68},{68... | collective-permute-start | bytes 1572872 | tf_op jit(solution)/shard_map/ppermute | solution.py:368
  (1 other events, 0.9 us)
Sparse Core Ops, SparseCore 0:
  10.1 90.0 all-gather.3
  103.0 139.0 all-gather.5
